TPU v7x, 32 devices: a whole 2x2x4 slice. The times are simulated.
32 devices in a mesh: row: 4 (over y, core), col: 4 (over z), win: 2 (over x).
Axes of the slice: x: 2, y: 2, z: 4, core: 2. Of those that a mesh axis runs over, the one named last changes fastest.
Arguments:
- spectra: bfloat16 [8, 32, 6144], P('win', 'row', 'col'), may hold values from -6 to 6
- usable: int32 [8, 32], replicated, may hold values 0 or 1
Outputs:
- stacked: float32 [32, 32, 9, 768], P(('row', 'win'), 'col')
All inputs are finite; a program needn't handle non-finite values.
Results may differ from a plain program's by a relative error of at most 0.0046.
Values may be sent and summed in bfloat16 or wider, within the bound.
No kernel may reach another device: no remote copies, remote signals or barrier semaphores. Data moves between devices by JAX's collectives and lax.ppermute only.
A program may use at most 64 MiB of HBM per device.

v0:
```python
import math

import jax
import jax.numpy as jnp
from jax import lax
from jax.sharding import PartitionSpec as P

F = 1024
LAG = 768
DEC = 2


def from_root(block, axis, owner):
    block = jnp.where(lax.axis_index(axis) == owner, block, jnp.zeros_like(block))
    return lax.psum(block, axis)


def build_table():
    frequency = jnp.arange(F, dtype=jnp.int32)
    lag_shift = DEC * (jnp.arange(LAG, dtype=jnp.int32) - LAG // 2)
    phase_index = frequency[:, None] * lag_shift[None, :] % (2 * F)
    phase_angle = phase_index.astype(jnp.float32) * (math.pi / F)
    scaling = 1.0 / math.sqrt(F)
    return jnp.concatenate(
        [jnp.cos(phase_angle) * scaling, -jnp.sin(phase_angle) * scaling], 0
    ).astype(jnp.bfloat16)


def lag_terms(row_part, col_part, dft_table):
    window_count, row_count = (row_part.shape[0], row_part.shape[1])
    col_count = col_part.shape[1]
    left_side = row_part.reshape(window_count, row_count, 3, 2, F)
    right_side = col_part.reshape(window_count, col_count, 3, 2, F)
    left_real = left_side[:, :, :, 0].reshape(window_count, row_count * 3, F)
    left_imag = left_side[:, :, :, 1].reshape(window_count, row_count * 3, F)
    right_real = right_side[:, :, :, 0].reshape(window_count, col_count * 3, F)
    right_imag = right_side[:, :, :, 1].reshape(window_count, col_count * 3, F)
    first_real = jnp.concatenate([left_real, left_imag], 0)
    second_real = jnp.concatenate([right_real, right_imag], 0)
    first_imag = jnp.concatenate([left_imag, left_real], 0)
    second_imag = jnp.concatenate([right_real, -right_imag], 0)
    real_part = jnp.einsum(
        "wpf,wqf->pqf", first_real, second_real, preferred_element_type=jnp.float32
    )
    imag_part = jnp.einsum(
        "wpf,wqf->pqf", first_imag, second_imag, preferred_element_type=jnp.float32
    )
    spectrum = jnp.stack([real_part, imag_part], 2).astype(jnp.bfloat16)
    flat_spectrum = spectrum.reshape(row_count * 3 * col_count * 3, 2 * F)
    lag_values = jnp.dot(flat_spectrum, dft_table, preferred_element_type=jnp.float32).astype(
        jnp.bfloat16
    )
    lag_values = lag_values.reshape(row_count, 3, col_count, 3, LAG).transpose(0, 2, 1, 3, 4)
    return lag_values.reshape(row_count, col_count, 9, LAG)


def body(spectra, usable):
    window_count, block_rows = (spectra.shape[0], spectra.shape[1])
    halves = lax.axis_size("win")
    win_index = lax.axis_index("win")
    row_index = lax.axis_index("row")
    col_index = lax.axis_index("col")
    half_rows = block_rows // halves
    first_row = win_index * half_rows
    dft_table = build_table()
    own_mask = lax.dynamic_slice(
        usable, (win_index * window_count, row_index * block_rows), (window_count, block_rows)
    )
    masked = spectra * own_mask[:, :, None].astype(jnp.bfloat16)
    pieces = masked[None]
    row_panels = lax.all_gather(pieces, "col", axis=3, tiled=True)
    col_panels = from_root(row_panels, "row", col_index)
    row_part = row_panels[0]
    lag_values = lag_terms(row_part, col_panels[0], dft_table)
    stacked_sum = lax.psum_scatter(
        lax.optimization_barrier(lag_values).astype(jnp.float32).astype(jnp.bfloat16),
        "win",
        scatter_dimension=0,
        tiled=True,
    ).astype(jnp.float32)
    weights = usable.astype(jnp.float32)
    row_weights = lax.dynamic_slice_in_dim(
        weights, row_index * block_rows + first_row, half_rows, 1
    )
    col_weights = lax.dynamic_slice_in_dim(weights, col_index * block_rows, block_rows, 1)
    pair_count = jnp.dot(row_weights.T, col_weights, precision=lax.Precision.HIGHEST)
    return stacked_sum / jnp.maximum(pair_count, 1.0)[:, :, None, None]


def solution(mesh):
    placed = (P("win", "row", "col"), P())
    return jax.shard_map(
        body,
        mesh=mesh,
        in_specs=placed,
        out_specs=P(("row", "win"), "col", None, None),
        check_vma=False,
    )
```

profile of v0, /device:TPU:0, one launch (start us, length us, event | category | flops | bytes accessed | tf_op | source)
XLA Modules:
  0.0 135.5 jit_solution(16546647663146585854)
XLA Ops:
  6.5 0.0 all-reduce.2.cloned.1.call-start
  6.5 0.8 dynamic-slice_convert_fusion
  7.3 1.0 broadcast_multiply_fusion
  8.3 16.2 %all-gather = bf16[4,8,6144]{2,1,0:T(8,128)(2,1)S(1)} all-gather(bf16[4,8,1536]{2,1,0:T(8,128)(2,1)S(1)} %broadcast_multiply_fusion), channel_id=2, replica_groups=mesh['row'=4,'col'=4,'win'=2] {'col'}, dimensions={2}, use_global_device_ids=true | all-gather | bytes 491520 | tf_op jit(solution)/shard_map/all_gather | solution.py:71
  24.5 1.1 copy.64
  25.6 0.0 all-reduce.2.cloned.1.call-update
  25.6 0.0 reduce-scatter.2.cloned.1.call-start
  25.7 13.8 %multiply_convert_fusion.1 = (bf16[1024,768]{1,0:T(8,128)(2,1)}, bf16[1024,768]{1,0:T(8,128)(2,1)}) fusion(s32[768]{0:T(1024)S(1)} %add_multiply_fusion), kind=kLoop, calls=%fused_computation.14 | loop fusion | flops 14942208 | bytes 3148800 | tf_op jit(solution)/shard_map/convert
  39.5 0.2 copy.78
  39.7 0.7 copy.69
  40.4 0.2 copy.79
  40.6 0.7 copy.70
  41.3 18.8 %all-reduce.2.cloned.1.call-done = bf16[4,8,3,2,1024]{4,0,2,1,3:T(4,128)(2,1)} async-done(((bf16[4,8,3,2,1024]{4,0,2,1,3:T(4,128)(2,1)}), bf16[4,8,3,2,1024]{4,0,2,1,3:T(4,128)(2,1)}) %all-reduce.2.cloned.1.call-update) | async-done | bytes 393232 | tf_op jit(solution)/shard_map/psum | solution.py:15
  60.1 1.2 fusion.29
  61.3 0.7 copy.65
  62.1 0.7 copy.72
  62.8 1.4 %copy.66 = bf16[4,24,1024]{1,0,2:T(4,128)(2,1)} copy(bf16[4,24,1024]{2,0,1:T(4,128)(2,1)S(1)} %bitcast.26) | data formatting | bytes 393216 | tf_op jit(solution)/shard_map/reshape;squeeze | solution.py:37
  64.2 0.1 copy_negate_fusion
  64.3 1.0 pad_maximum_fusion.1
  65.3 2.5 %copy.75 = bf16[8,24,1024]{1,0,2:T(8,128)(2,1)} copy(bf16[8,24,1024]{2,1,0:T(8,128)(2,1)S(1)} %pad_maximum_fusion.1) | data formatting | bytes 786432 | tf_op jit(solution)/shard_map/concatenate | solution.py:41
  67.8 0.0 copy-start
  67.8 5.0 %convert_bitcast_fusion = bf16[24,24,1,1024]{0,1,3,2:T(8,128)(2,1)S(1)} fusion(bf16[8,24,1024]{1,0,2:T(8,128)(2,1)} %copy.75, bf16[4,24,1024]{1,0,2:T(4,128)(2,1)S(1)} %copy.69, bf16[4,24,1024]{1,0,2:T(4,128)(2,1)S(1)} %copy.70), kind=kOutput, calls=%fused_computation.1 | convolution fusion | flops 10813440 | bytes 1966080 | tf_op jit(solution)/shard_map/wpf,wqf->pqf/dot_general | solution.py:45
  72.8 0.0 copy-done
  72.8 4.1 %convert_bitcast_fusion.1 = bf16[24,24,1,1024]{0,1,3,2:T(8,128)(2,1)S(1)} fusion(bf16[4,24,1024]{1,0,2:T(4,128)(2,1)S(1)} %copy-done, bf16[4,24,1024]{1,0,2:T(4,128)(2,1)S(1)} %copy.65, bf16[4,24,1024]{1,0,2:T(4,128)(2,1)S(1)} %copy.70, bf16[4,24,1024]{1,0,2:T(4,128)(2,1)S(1)} %copy.69), kind=kOutput, calls=%fused_computation.2 | convolution fusion | flops 11599872 | bytes 1966080 | tf_op jit(solution)/shard_map/wpf,wqf->pqf/dot_general | solution.py:42
  77.0 6.5 %pad_maximum_fusion = bf16[24,24,2,1024]{0,1,3,2:T(8,128)(2,1)} fusion(bf16[24,24,1,1024]{0,1,3,2:T(8,128)(2,1)S(1)} %convert_bitcast_fusion, bf16[24,24,1,1024]{0,1,3,2:T(8,128)(2,1)S(1)} %convert_bitcast_fusion.1), kind=kLoop, calls=%fused_computation | loop fusion | flops 1179648 | bytes 4718592 | tf_op jit(solution)/shard_map/stack | solution.py:48
  83.5 19.1 %copy.76 = bf16[24,24,2,1024]{3,2,1,0:T(2,128)(2,1)S(1)} copy(bf16[24,24,2,1024]{0,1,3,2:T(8,128)(2,1)} %pad_maximum_fusion) | data formatting | bytes 4718592 | tf_op jit(solution)/shard_map/stack | solution.py:48
  102.5 0.0 copy-start.1
  102.5 0.0 copy-start.2
  102.6 0.7 copy.80
  103.3 0.7 copy-done.1
  103.9 0.5 copy-done.2
  104.4 2.0 %fusion.19 = bf16[576,768]{1,0:T(8,128)(2,1)S(1)} fusion(bf16[576,2048]{1,0:T(8,128)(2,1)S(1)} %bitcast.25, bf16[1024,768]{1,0:T(8,128)(2,1)S(1)} %copy-done.2, bf16[1024,768]{1,0:T(8,128)(2,1)S(1)} %copy-done.1), kind=kOutput, calls=%fused_computation.27 | convolution fusion | flops 1818673152 | bytes 6389760 | tf_op jit(solution)/shard_map/dot_general | solution.py:50
  106.4 0.0 copy-start.3
  106.4 0.5 reshape.17
  106.9 1.0 copy.77
  107.9 0.0 reduce-scatter.2.cloned.1.call-update
  108.0 0.0 copy-done.3
  108.0 0.3 convolution_maximum_fusion
  108.3 18.4 %reduce-scatter.2.cloned.1.call-done = bf16[4,8,9,768]{3,1,2,0:T(8,128)(2,1)} async-done(((bf16[8,8,9,768]{3,1,2,0:T(8,128)(2,1)}), bf16[4,8,9,768]{3,1,2,0:T(8,128)(2,1)}) %reduce-scatter.2.cloned.1.call-update) | async-done | bytes 442384 | tf_op jit(solution)/shard_map/reduce_scatter | solution.py:75
  126.6 2.1 %convert_divide_fusion = f32[4,8,9,768]{3,1,2,0:T(8,128)} fusion(bf16[4,8,9,768]{3,1,2,0:T(8,128)(2,1)} %reduce-scatter.2.cloned.1.call-done, f32[4,8]{1,0:T(4,128)S(1)} %convolution_maximum_fusion), kind=kLoop, calls=%fused_computation.29 | loop fusion | flops 442368 | bytes 1327232 | tf_op jit(solution)/shard_map/div | solution.py:87
  (4 shorter events, 0.1 us)
Async XLA Ops:
  6.5 53.6 %all-reduce.2.cloned.1.call-start = ((), (), s32[]{:S(2)}) async-start(), calls=%async_computation.1 | async-start | bytes 786432 | tf_op jit(solution)/shard_map/psum | solution.py:15
  25.6 101.0 %reduce-scatter.2.cloned.1.call-start = ((), (), s32[]{:S(2)}) async-start(), calls=%async_computation.2 | async-start | bytes 1327104 | tf_op jit(solution)/shard_map/reduce_scatter | solution.py:75
  67.8 5.0 %copy-start = (bf16[4,24,1024]{1,0,2:T(4,128)(2,1)S(1)}, bf16[4,24,1024]{1,0,2:T(4,128)(2,1)}, u32[]{:S(2)}) copy-start(bf16[4,24,1024]{1,0,2:T(4,128)(2,1)} %copy.66) | copy-start | bytes 589828
  102.5 1.4 %copy-start.1 = (bf16[1024,768]{1,0:T(8,128)(2,1)S(1)}, bf16[1024,768]{1,0:T(8,128)(2,1)}, u32[]{:S(2)}) copy-start(bf16[1024,768]{1,0:T(8,128)(2,1)} %get-tuple-element.9) | copy-start | bytes 4718596
  102.5 1.9 %copy-start.2 = (bf16[1024,768]{1,0:T(8,128)(2,1)S(1)}, bf16[1024,768]{1,0:T(8,128)(2,1)}, u32[]{:S(2)}) copy-start(bf16[1024,768]{1,0:T(8,128)(2,1)} %get-tuple-element.10) | copy-start | bytes 4718596
  106.4 1.6 %copy-start.3 = (s32[8,32]{1,0:T(8,128)S(1)}, s32[8,32]{1,0:T(8,128)}, u32[]{:S(2)}) copy-start(s32[8,32]{1,0:T(8,128)} %param.3) | copy-start | bytes 3076
Sparse Core Ops, SparseCore 0:
  25.7 34.3 all-reduce.1
  108.1 18.5 reduce-scatter.1
where the time goes:
time: 136 us
  waiting for transfers between devices  37.2 us (27%)
  local copies, waits for them, and re-layouts  31.9 us (23%)
  other arithmetic  25.2 us (19%)
  blocking collectives  16.2 us (12%)
  between operations  13.6 us (10%)
  matrix products  11.4 us (8%)
    another operation x1, local copies, waits for them, and re-layouts, lag_terms(): spectrum = jnp.stack([real_part, imag_part], 2).astype(jnp.bfloat16)  19.1 us
    psum x1, waiting for transfers between devices, from_root(): return lax.psum(block, axis)  18.8 us
    reduce_scatter x1, waiting for transfers between devices, body(): lax.psum_scatter(lax.optimization_barrier(lag_values).astype(jnp.float32)...  18.4 us
    all_gather x1, blocking collectives, body(): row_panels = lax.all_gather(pieces, 'col', axis=3, tiled=True)  16.2 us
    another operation x1, other arithmetic  13.8 us
    another operation x1, other arithmetic, lag_terms(): spectrum = jnp.stack([real_part, imag_part], 2).astype(jnp.bfloat16)  6.5 us
    dot_general x1, matrix products, lag_terms(): jnp.einsum('wpf,wqf->pqf', first_imag, second_imag, preferred_element_typ...  5.03 us
    dot_general x1, matrix products, lag_terms(): jnp.einsum('wpf,wqf->pqf', first_real, second_real, preferred_element_typ...  4.13 us
  transfers between devices with their start and end apart: 2, of which 2 were waited for; matrix products, arithmetic and copies ran while one was open for 12% of the time, Pallas kernels for 0%

commit v1 on v0

v1 whole, which is shorter than its diff:
```python
import math

import jax
import jax.numpy as jnp
import numpy as np
from jax import lax
from jax.experimental import pallas as pl
from jax.experimental.pallas import tpu as pltpu
from jax.sharding import PartitionSpec as P

F = 1024
LAG = 768
DEC = 2
LANES = 128
CHUNKS = F // LANES


def build_table():
    shift = DEC * (np.arange(LAG, dtype=np.int64) - LAG // 2)
    phase = (np.arange(F, dtype=np.int64)[:, None] * shift[None, :]) % (2 * F)
    angle = phase.astype(np.float64) * (math.pi / F)
    scale = 1.0 / math.sqrt(F)
    both = np.stack([np.cos(angle) * scale, -np.sin(angle) * scale])
    both = both.reshape(2, CHUNKS, LANES, LAG).transpose(1, 0, 2, 3)
    return both.reshape(2 * F, LAG).astype(np.float32).astype(jnp.bfloat16)


def make_kernel(windows, half, block):
    def kernel(rows_ref, cols_ref, rmask_ref, cmask_ref, inv_ref, table_ref, out_ref, left, right, cross):
        per_shard = rows_ref.shape[2] // LANES

        def place(part, chunk):
            piece = part * CHUNKS + chunk
            return piece // per_shard, (piece % per_shard) * LANES

        rmask = rmask_ref[...]
        cmask = cmask_ref[...]
        for part in range(6):
            for chunk in range(CHUNKS):
                shard, at = place(part, chunk)
                left[chunk, part] = rows_ref[shard, :, at : at + LANES].astype(jnp.float32) * rmask
                right[chunk, part] = cols_ref[shard, :, at : at + LANES].astype(jnp.float32) * cmask

        def one_chunk(chunk, carry):
            for b in range(3):
                col_re = [right[chunk, 2 * b, w * block : (w + 1) * block] for w in range(windows)]
                col_im = [right[chunk, 2 * b + 1, w * block : (w + 1) * block] for w in range(windows)]
                for a in range(3):
                    for pair in range(half // 2):
                        reals, imags = [], []
                        for s in (2 * pair, 2 * pair + 1):
                            re = im = None
                            for w in range(windows):
                                at = w * half + s
                                row_re = jnp.broadcast_to(left[chunk, 2 * a, at : at + 1], (block, LANES))
                                row_im = jnp.broadcast_to(left[chunk, 2 * a + 1, at : at + 1], (block, LANES))
                                new_re = row_re * col_re[w] + row_im * col_im[w]
                                new_im = row_im * col_re[w] - row_re * col_im[w]
                                re = new_re if re is None else re + new_re
                                im = new_im if im is None else im + new_im
                            reals.append(re)
                            imags.append(im)
                        first = ((pair * 3 + a) * 3 + b) * 2 * block
                        cross[chunk, first : first + 2 * block, :LANES] = jnp.concatenate(reals, 0).astype(jnp.bfloat16)
                        cross[chunk, first : first + 2 * block, LANES:] = jnp.concatenate(imags, 0).astype(jnp.bfloat16)
            return carry

        lax.fori_loop(0, CHUNKS, one_chunk, 0)
        total = None
        for chunk in range(CHUNKS):
            new = jnp.dot(
                cross[chunk], table_ref[2 * LANES * chunk : 2 * LANES * (chunk + 1)], preferred_element_type=jnp.float32
            )
            total = new if total is None else total + new
        for s in range(half):
            inv = inv_ref[s * block : (s + 1) * block, :1]
            for c in range(9):
                group = ((s // 2) * 9 + c) * 2 + s % 2
                out_ref[s, c] = total[group * block : (group + 1) * block] * inv

    return kernel


def correlate(rows, cols, rmask, cmask, inv, table, half, block):
    windows = rows.shape[1] // half
    groups = half * 9 * block
    return pl.pallas_call(
        make_kernel(windows, half, block),
        out_shape=jax.ShapeDtypeStruct((half, 9, block, LAG), jnp.float32),
        in_specs=[pl.BlockSpec(memory_space=pltpu.VMEM)] * 6,
        out_specs=pl.BlockSpec(memory_space=pltpu.VMEM),
        scratch_shapes=[
            pltpu.VMEM((CHUNKS, 6, windows * half, LANES), jnp.float32),
            pltpu.VMEM((CHUNKS, 6, windows * block, LANES), jnp.float32),
            pltpu.VMEM((CHUNKS, groups, 2 * LANES), jnp.bfloat16),
        ],
        compiler_params=pltpu.CompilerParams(vmem_limit_bytes=40 * 1024 * 1024),
        cost_estimate=pl.CostEstimate(flops=2 * groups * 2 * F * LAG, bytes_accessed=8 * 1024 * 1024, transcendentals=0),
    )(rows, cols, rmask, cmask, inv, table)


def body(spectra, usable):
    block = spectra.shape[1]
    shard = spectra.shape[2]
    n_row, n_col, n_win = (lax.axis_size(a) for a in ("row", "col", "win"))
    assert n_row == n_col
    half = block // n_win
    windows = n_win * spectra.shape[0]
    row_index, col_index, win_index = (lax.axis_index(a) for a in ("row", "col", "win"))

    every = lax.all_gather(spectra, "win", axis=0, tiled=True)
    pairs = [
        ((r * n_col + c) * n_win + w, (c * n_col + r) * n_win + w)
        for r in range(n_row)
        for c in range(n_col)
        for w in range(n_win)
    ]
    turned = lax.ppermute(every.reshape(windows * block, shard), ("row", "col", "win"), pairs)
    own = lax.dynamic_slice_in_dim(every, win_index * half, half, 1).reshape(windows * half, shard)
    rows = lax.all_gather(own, "col", axis=0)
    cols = lax.all_gather(turned, "row", axis=0)

    weights = usable.astype(jnp.float32)
    row_weights = lax.dynamic_slice_in_dim(weights, row_index * block + win_index * half, half, 1)
    col_weights = lax.dynamic_slice_in_dim(weights, col_index * block, block, 1)
    count = jnp.sum(row_weights[:, :, None] * col_weights[:, None, :], 0)
    inv = jnp.broadcast_to((1.0 / jnp.maximum(count, 1.0)).reshape(half * block, 1), (half * block, LANES))
    rmask = jnp.broadcast_to(row_weights.reshape(windows * half, 1), (windows * half, LANES))
    cmask = jnp.broadcast_to(col_weights.reshape(windows * block, 1), (windows * block, LANES))
    out = correlate(rows, cols, rmask, cmask, inv, jnp.asarray(build_table()), half, block)
    return out.transpose(0, 2, 1, 3)


def solution(mesh):
    placed = (P("win", "row", "col"), P())
    return jax.shard_map(
        body,
        mesh=mesh,
        in_specs=placed,
        out_specs=P(("row", "win"), "col", None, None),
        check_vma=False,
    )
```

time: 136 us -> 45 us (0.33)
  waiting for transfers between devices: 37.2 us -> 0.01 us
  local copies, waits for them, and re-layouts: 31.9 us -> 2.66 us
  other arithmetic: 25.2 us -> 0.79 us
  blocking collectives: 16.2 us -> 36 us
  between operations: 13.6 us -> 0.04 us
  matrix products: 11.4 us -> 0 us
  Pallas kernels: 0 us -> 4.59 us
    another operation x7 -> x1, local copies, waits for them, and re-layouts: 24.5 us -> 0.03 us  [body(): rows = lax.all_gather(own, 'col', axis=0)]
    another operation x2 -> x0, other arithmetic: 20.3 us -> none
    all_gather x1 -> x3, blocking collectives: 16.2 us -> 36 us  [the longest x1 20.2 us: body(): rows = lax.all_gather(own, 'col', axis=0)]
    psum x1 -> x0, waiting for transfers between devices: 18.8 us -> none  [from_root(): return lax.psum(block, axis)]
    reduce_scatter x1 -> x0, waiting for transfers between devices: 18.4 us -> none  [body(): lax.psum_scatter(lax.optimization_barrier(lag_values).astype(jnp.float32)...]
    dot_general x4 -> x0, matrix products: 11.4 us -> none  [the longest x1 5.03 us: lag_terms(): jnp.einsum('wpf,wqf->pqf', first_imag, second_imag, preferred_element_typ...]
    pallas_call x0 -> x1, Pallas kernels: none -> 4.59 us  [correlate(): pl.pallas_call(make_kernel(windows, half, block), out_shape=jax.ShapeDtyp...]
    concatenate x1 -> x0, local copies, waits for them, and re-layouts: 2.5 us -> none  [lag_terms(): second_imag = jnp.concatenate([right_real, -right_imag], 0)]
  transfers between devices with their start and end apart: 2 -> 1, of which waited for: 2 -> 0; matrix products, arithmetic and copies ran while one was open for 12% -> 3% of each run, Pallas kernels for 0% -> 0%
where the time goes in v1:
time: 45 us; the launch traced here: 44.7 us
  blocking collectives  36 us (80%)
  Pallas kernels  4.59 us (10%)
  local copies, waits for them, and re-layouts  2.66 us (6%)
  other arithmetic  0.79 us (2%)
  starting transfers between devices  0.66 us (1%)
    all_gather x1, blocking collectives, body(): rows = lax.all_gather(own, 'col', axis=0)  20.2 us
    all_gather x1, blocking collectives, body(): cols = lax.all_gather(turned, 'row', axis=0)  9.11 us
    all_gather x1, blocking collectives, body(): every = lax.all_gather(spectra, 'win', axis=0, tiled=True)  6.65 us
    pallas_call x1, Pallas kernels, correlate(): pl.pallas_call(make_kernel(windows, half, block), out_shape=jax.ShapeDtyp...  4.59 us
    unnamed x2, local copies, waits for them, and re-layouts  1.9 us
  transfers between devices with their start and end apart: 1, of which 0 were waited for; matrix products, arithmetic and copies ran while one was open for 3% of the time, Pallas kernels for 0%

profile of v1, /device:TPU:0, one launch (start us, length us, event | category | flops | bytes accessed | tf_op | source)
XLA Modules:
  0.0 44.7 jit_solution(3432796684325539048)
XLA Ops:
  0.0 6.6 %all_gather.12 = bf16[8,8,1536]{2,1,0:T(8,128)(2,1)S(1)} all-gather(bf16[4,8,1536]{2,1,0:T(8,128)(2,1)} %param.3), channel_id=1, replica_groups=mesh['row'=4,'col'=4,'win'=2] {'win'}, dimensions={0}, use_global_device_ids=true | all-gather | bytes 294912 | tf_op jit(solution)/shard_map/all_gather | solution.py:111
  6.7 0.7 %collective-permute-start = (bf16[64,1536]{1,0:T(8,128)(2,1)S(1)}, bf16[64,1536]{1,0:T(8,128)(2,1)S(1)}, u32[]{:S(2)}, u32[]{:S(2)}) collective-permute-start(bf16[64,1536]{1,0:T(8,128)(2,1)S(1)} %bitcast.4), channel_id=1, source_target_pairs={{0,0},{1,1},{2,8},{3,9},{4,16},{5,17},{6,24},{7,25},{8,2},{9,3},{1... | collective-permute-start | bytes 589832 | tf_op jit(solution)/shard_map/ppermute | solution.py:118
  7.3 0.7 %convert_element_type.3 = f32[8,32]{1,0:T(8,128)S(1)} convert(s32[8,32]{1,0:T(8,128)} %param.4) | non-fusion elementwise | flops 256 | bytes 2048 | tf_op jit(solution)/shard_map/convert_element_type | solution.py:123
  8.0 0.1 constant_dynamic-slice_fusion
  8.1 0.1 constant_dynamic-slice_fusion.1
  8.2 0.1 copy.4
  8.3 0.1 constant_dynamic-slice_fusion.2
  8.3 0.1 multiply_reduce_fusion
  8.4 0.1 broadcast_in_dim.10
  8.5 0.1 broadcast_in_dim.23
  8.6 0.1 div.11
  8.7 20.2 %all_gather.13.rows_ref = bf16[4,32,1536]{2,1,0:T(8,128)(2,1)S(1)} all-gather(bf16[1,32,1536]{2,1,0:T(8,128)(2,1)S(1)} %all_gather_reshape.3), channel_id=1, replica_groups=mesh['row'=4,'col'=4,'win'=2] {'col'}, dimensions={0}, use_global_device_ids=true | all-gather | bytes 491520 | tf_op jit(solution)/shard_map/all_gather | solution.py:120
  28.9 0.0 collective-permute-done
  28.9 9.1 %all-gather = bf16[256,1536]{1,0:T(8,128)(2,1)S(1)} all-gather(bf16[64,1536]{1,0:T(8,128)(2,1)S(1)} %collective-permute-done), channel_id=2, replica_groups=mesh['row'=4,'col'=4,'win'=2] {'row'}, dimensions={0}, use_global_device_ids=true | all-gather | bytes 983040 | tf_op jit(solution)/shard_map/all_gather | solution.py:121
  38.0 0.1 broadcast_in_dim.25.inv_ref
  38.1 0.1 broadcast_in_dim.22.rmask_ref
  38.2 0.1 broadcast_in_dim.24.cmask_ref
  38.3 0.0 copy-start
  38.3 1.9 %copy-done = bf16[2048,768]{1,0:T(8,128)(2,1)S(1)} copy-done((bf16[2048,768]{1,0:T(8,128)(2,1)S(1)}, bf16[2048,768]{1,0:T(8,128)(2,1)}, u32[]{:S(2)}) %copy-start) | copy-done | bytes 3145752
  40.2 4.6 %shard_map.37 = f32[4,9,8,768]{3,2,1,0:T(8,128)} custom-call(bf16[4,32,1536]{2,1,0:T(8,128)(2,1)S(1)} %all_gather.13.rows_ref, bf16[4,64,1536]{2,1,0:T(8,128)(2,1)S(1)} %bitcast.3, f32[32,128]{1,0:T(8,128)S(1)} %broadcast_in_dim.22.rmask_ref, f32[64,128]{1,0:T(8,128)S(1)} %broadcast_in_dim.24.cmask_ref, f32[32,128]{1,0:T(8,128)S(1)} %broadcast_in_dim.25.inv_ref, ...), custom_call_target="tpu_custom_call" | custom-call | flops 905969664 | bytes 8388608 | tf_op jit(solution)/shard_map/pallas_call | solution.py:87
  (2 shorter events, 0.0 us)
Async XLA Ops:
  6.7 22.3 %collective-permute-start = (bf16[64,1536]{1,0:T(8,128)(2,1)S(1)}, bf16[64,1536]{1,0:T(8,128)(2,1)S(1)}, u32[]{:S(2)}, u32[]{:S(2)}) collective-permute-start(bf16[64,1536]{1,0:T(8,128)(2,1)S(1)} %bitcast.4), channel_id=1, source_target_pairs={{0,0},{1,1},{2,8},{3,9},{4,16},{5,17},{6,24},{7,25},{8,2},{9,3},{1... | collective-permute-start | bytes 589832 | tf_op jit(solution)/shard_map/ppermute | solution.py:118
  38.3 1.9 %copy-start = (bf16[2048,768]{1,0:T(8,128)(2,1)S(1)}, bf16[2048,768]{1,0:T(8,128)(2,1)}, u32[]{:S(2)}) copy-start(bf16[2048,768]{1,0:T(8,128)(2,1)} %constant.25.clone.table_ref) | copy-start | bytes 9437188

commit v2 on v1

v2 whole, which is shorter than its diff:
```python
import math

import jax
import jax.numpy as jnp
import numpy as np
from jax import lax
from jax.experimental import pallas as pl
from jax.experimental.pallas import tpu as pltpu
from jax.sharding import PartitionSpec as P

F = 1024
LAG = 768
DEC = 2
LANES = 128
CHUNKS = F // LANES
AXES = ("row", "col", "win")


def build_table():
    shift = DEC * (np.arange(LAG, dtype=np.int64) - LAG // 2)
    phase = (np.arange(F, dtype=np.int64)[:, None] * shift[None, :]) % (2 * F)
    angle = phase.astype(np.float64) * (math.pi / F)
    scale = 1.0 / math.sqrt(F)
    both = np.stack([np.cos(angle) * scale, -np.sin(angle) * scale])
    both = both.reshape(2, CHUNKS, LANES, LAG).transpose(1, 0, 2, 3)
    return both.reshape(2 * F, LAG).astype(np.float32).astype(jnp.bfloat16)


def make_kernel(row_places, col_places, half, block, span):
    n_rows, n_cols = len(row_places), len(col_places)

    def kernel(*refs):
        row_slots, col_slots = refs[:n_rows], refs[n_rows : n_rows + n_cols]
        usable_hbm, table_hbm, out_ref, left, right, cross, rmask, cmask, usable_ref, flag_sem, table_ref, sem = refs[
            n_rows + n_cols :
        ]
        flags = pltpu.make_async_copy(usable_hbm, usable_ref, flag_sem)
        flags.start()
        fetch = pltpu.make_async_copy(table_hbm, table_ref, sem)
        fetch.start()
        at = tuple(lax.axis_index(a) for a in AXES)
        row, col, win = at
        per_shard = row_slots[0].shape[1] // LANES

        flags.wait()
        usable = usable_ref[...].astype(jnp.float32)
        stations = usable.shape[1]

        def column(first, count, h):
            rows = jnp.concatenate(
                [jnp.broadcast_to(usable[w : w + 1], (count, stations)) for w in range(h * span, (h + 1) * span)], 0
            )
            shape = (span * count, stations)
            picked = lax.broadcasted_iota(jnp.int32, shape, 1) == first + lax.broadcasted_iota(jnp.int32, shape, 0) % count
            return jnp.sum(jnp.where(picked, rows, 0.0), 1, keepdims=True)

        counts = [jnp.zeros((block, LANES), jnp.float32) for _ in range(half)]
        for h in range(2):
            rm = jnp.broadcast_to(column(row * block + win * half, half, h), (span * half, LANES))
            cm = jnp.broadcast_to(column(col * block, block, h), (span * block, LANES))
            rmask[h] = rm
            cmask[h] = cm
            for w in range(span):
                for s in range(half):
                    counts[s] = counts[s] + rm[w * half + s : w * half + s + 1] * cm[w * block : (w + 1) * block]
        invs = [1.0 / jnp.maximum(c, 1.0) for c in counts]

        for ref, place in zip(row_slots, row_places):
            shard = place(*at)
            for h in range(2):
                own = win if h == 0 else 1 - win
                mask = rmask[own]
                for i in range(per_shard):
                    data = ref[h * span * half : (h + 1) * span * half, i * LANES : (i + 1) * LANES]
                    left[shard * per_shard + i, own] = data.astype(jnp.float32) * mask
        for ref, place in zip(col_slots, col_places):
            shard, own = place(*at)
            mask = cmask[own]
            for i in range(per_shard):
                data = ref[:, i * LANES : (i + 1) * LANES]
                right[shard * per_shard + i, own] = data.astype(jnp.float32) * mask

        windows = [(h, w) for h in range(2) for w in range(span)]

        def one_chunk(chunk, carry):
            for b in range(3):
                col_re = [right[2 * b * CHUNKS + chunk, h, w * block : (w + 1) * block] for h, w in windows]
                col_im = [right[(2 * b + 1) * CHUNKS + chunk, h, w * block : (w + 1) * block] for h, w in windows]
                for a in range(3):
                    for pair in range(half // 2):
                        reals, imags = [], []
                        for s in (2 * pair, 2 * pair + 1):
                            re = im = None
                            for (h, w), c_re, c_im in zip(windows, col_re, col_im):
                                r = w * half + s
                                r_re = jnp.broadcast_to(left[2 * a * CHUNKS + chunk, h, r : r + 1], (block, LANES))
                                r_im = jnp.broadcast_to(left[(2 * a + 1) * CHUNKS + chunk, h, r : r + 1], (block, LANES))
                                new_re = r_re * c_re + r_im * c_im
                                new_im = r_im * c_re - r_re * c_im
                                re = new_re if re is None else re + new_re
                                im = new_im if im is None else im + new_im
                            reals.append(re)
                            imags.append(im)
                        first = ((pair * 3 + a) * 3 + b) * 2 * block
                        cross[chunk, first : first + 2 * block, :LANES] = jnp.concatenate(reals, 0).astype(jnp.bfloat16)
                        cross[chunk, first : first + 2 * block, LANES:] = jnp.concatenate(imags, 0).astype(jnp.bfloat16)
            return carry

        lax.fori_loop(0, CHUNKS, one_chunk, 0)
        fetch.wait()
        total = None
        for chunk in range(CHUNKS):
            new = jnp.dot(
                cross[chunk], table_ref[2 * LANES * chunk : 2 * LANES * (chunk + 1)], preferred_element_type=jnp.float32
            )
            total = new if total is None else total + new
        for s in range(half):
            for c in range(9):
                group = ((s // 2) * 9 + c) * 2 + s % 2
                out_ref[s, c] = total[group * block : (group + 1) * block] * invs[s][:, :1]

    return kernel


def correlate(rows, cols, usable, table, row_places, col_places, half, block, span):
    groups = half * 9 * block
    pieces = 6 * CHUNKS
    in_vmem = pl.BlockSpec(memory_space=pltpu.VMEM)
    return pl.pallas_call(
        make_kernel(row_places, col_places, half, block, span),
        out_shape=jax.ShapeDtypeStruct((half, 9, block, LAG), jnp.float32),
        in_specs=[in_vmem] * (len(rows) + len(cols)) + [pl.BlockSpec(memory_space=pltpu.HBM)] * 2,
        out_specs=in_vmem,
        scratch_shapes=[
            pltpu.VMEM((pieces, 2, span * half, LANES), jnp.float32),
            pltpu.VMEM((pieces, 2, span * block, LANES), jnp.float32),
            pltpu.VMEM((CHUNKS, groups, 2 * LANES), jnp.bfloat16),
            pltpu.VMEM((2, span * half, LANES), jnp.float32),
            pltpu.VMEM((2, span * block, LANES), jnp.float32),
            pltpu.VMEM(usable.shape, jnp.int32),
            pltpu.SemaphoreType.DMA,
            pltpu.VMEM(table.shape, jnp.bfloat16),
            pltpu.SemaphoreType.DMA,
        ],
        compiler_params=pltpu.CompilerParams(vmem_limit_bytes=40 * 1024 * 1024),
    )(*rows, *cols, usable, table)


def split_stations(spectra, half):
    span, block, shard = spectra.shape

    def kernel(spectra_ref, theirs_ref, mine_ref):
        low = [spectra_ref[w, :half] for w in range(span)]
        high = [spectra_ref[w, half:] for w in range(span)]
        first = lax.axis_index("win") == 0
        low, high = jnp.concatenate(low, 0), jnp.concatenate(high, 0)
        theirs_ref[...] = jnp.where(first, high, low)
        mine_ref[: span * half] = jnp.where(first, low, high)
        mine_ref[span * half :] = jnp.zeros((span * half, shard), jnp.bfloat16)

    in_vmem = pl.BlockSpec(memory_space=pltpu.VMEM)
    return pl.pallas_call(
        kernel,
        out_shape=(
            jax.ShapeDtypeStruct((span * half, shard), jnp.bfloat16),
            jax.ShapeDtypeStruct((2 * span * half, shard), jnp.bfloat16),
        ),
        in_specs=[in_vmem],
        out_specs=(in_vmem, in_vmem),
    )(spectra)


def body(spectra, usable):
    span, block, shard = spectra.shape
    n_row, n_col, n_win = (lax.axis_size(a) for a in AXES)
    assert n_row == n_col and n_win == 2
    half = block // n_win

    def send(data, move):
        pairs = []
        for r in range(n_row):
            for c in range(n_col):
                for w in range(n_win):
                    r2, c2, w2 = move(r, c, w)
                    pairs.append(((r * n_col + c) * n_win + w, (r2 * n_col + c2) * n_win + w2))
        return lax.ppermute(data, AXES, pairs)

    def other_win(r, c, w):
        return r, c, 1 - w

    flat = spectra.reshape(span * block, shard)
    turned = send(flat, lambda r, c, w: (n_row - 1 - c, r, w))
    theirs, mine = split_stations(spectra, half)
    got = send(theirs, other_win)
    mine = lax.dynamic_update_slice(mine, got, (span * half, 0))

    if n_row == 4:
        shifted = [send(mine, lambda r, c, w, k=k: (r, (c + k) % n_col, w)) for k in (2, 1, 3)]
        rows = [mine] + shifted
        row_places = [lambda r, c, w, k=k: lax.rem(c + n_col - k, n_col) for k in (0, 2, 1, 3)]
        near = [
            turned,
            send(turned, lambda r, c, w: (r ^ 2, c, w)),
            send(turned, other_win),
            send(turned, lambda r, c, w: (r ^ 2, c, 1 - w)),
        ]
        last = lax.optimization_barrier((near[3], *shifted))[0]
        cols = near + [send(x, lambda r, c, w: (r ^ 1, c, w)) for x in near[:3] + [last]]
        col_places = [
            lambda r, c, w, e=e, d=d: (n_row - 1 - (r ^ e), w ^ d)
            for e, d in ((0, 0), (2, 0), (0, 1), (2, 1), (1, 0), (3, 0), (1, 1), (3, 1))
        ]
    else:
        gathered = lax.all_gather(mine, "col", axis=0)
        rows = [gathered[i] for i in range(n_col)]
        row_places = [lambda r, c, w, i=i: i for i in range(n_col)]
        near = lax.all_gather(turned, "row", axis=0)
        far = send(near, other_win)
        cols = [x[i] for x in (near, far) for i in range(n_row)]
        col_places = [lambda r, c, w, i=i, d=d: (n_row - 1 - i, w ^ d) for d in range(2) for i in range(n_row)]

    out = correlate(rows, cols, usable, jnp.asarray(build_table()), row_places, col_places, half, block, span)
    return out.transpose(0, 2, 1, 3)


def solution(mesh):
    placed = (P("win", "row", "col"), P())
    return jax.shard_map(
        body,
        mesh=mesh,
        in_specs=placed,
        out_specs=P(("row", "win"), "col", None, None),
        check_vma=False,
    )
```

time: 45 us -> 32.5 us (0.72)
  the two profiles are of different devices: /device:TPU:0 before, /device:TPU:25 now
where the time goes in v2:
time: 32.5 us; the launch traced here: 32.2 us
  starting transfers between devices  19.3 us (59%)
  Pallas kernels  6.51 us (20%)
  local copies, waits for them, and re-layouts  4.09 us (13%)
  waiting for transfers between devices  2.36 us (7%)
    ppermute x12, starting transfers between devices, send(): return lax.ppermute(data, AXES, pairs)  19.3 us
    pallas_call x1, Pallas kernels, correlate(): pl.pallas_call(make_kernel(row_places, col_places, half, block, span), ou...  4.93 us
    unnamed x6, local copies, waits for them, and re-layouts  3.47 us
    ppermute x12, waiting for transfers between devices, send(): return lax.ppermute(data, AXES, pairs)  2.36 us
    pallas_call x1, Pallas kernels, split_stations(): pl.pallas_call(kernel, out_shape=(jax.ShapeDtypeStruct((span * half, shar...  1.58 us
  transfers between devices with their start and end apart: 12, of which 3 were waited for; matrix products, arithmetic and copies ran while one was open for 2% of the time, Pallas kernels for 0%

profile of v2, /device:TPU:25, one launch (start us, length us, event | category | flops | bytes accessed | tf_op | source)
XLA Modules:
  0.0 32.2 jit_solution(15736905885839179031)
XLA Ops:
  0.0 1.6 %shard_map.37 = (bf16[16,1536]{1,0:T(8,128)(2,1)}, bf16[32,1536]{1,0:T(8,128)(2,1)}) custom-call(bf16[4,8,1536]{2,1,0:T(8,128)(2,1)} %spectra_ref.1), custom_call_target="tpu_custom_call" | custom-call | tf_op jit(solution)/shard_map/pallas_call | solution.py:162
  1.6 1.2 %collective-permute-start = (bf16[16,1536]{1,0:T(8,128)(2,1)}, bf16[16,1536]{1,0:T(8,128)(2,1)S(1)}, u32[]{:S(2)}, u32[]{:S(2)}) collective-permute-start(bf16[16,1536]{1,0:T(8,128)(2,1)} %get-tuple-element.9), channel_id=1, source_target_pairs={{0,1},{1,0},{2,3},{3,2},{4,5},{5,4},{6,7},{7,6},{8,9},{9,8},{10,11... | collective-permute-start | bytes 147464 | tf_op jit(solution)/shard_map/ppermute | solution.py:186
  2.8 0.9 %collective-permute-start.4 = (bf16[32,1536]{1,0:T(8,128)(2,1)}, bf16[32,1536]{1,0:T(8,128)(2,1)S(1)}, u32[]{:S(2)}, u32[]{:S(2)}) collective-permute-start(bf16[32,1536]{1,0:T(8,128)(2,1)} %bitcast.2), channel_id=1, source_target_pairs={{0,24},{1,25},{2,16},{3,17},{4,8},{5,9},{6,0},{7,1},{8,26},{9,27},... | collective-permute-start | bytes 294920 | tf_op jit(solution)/shard_map/ppermute | solution.py:186
  3.7 1.0 %collective-permute-done = bf16[16,1536]{1,0:T(8,128)(2,1)S(1)} collective-permute-done((bf16[16,1536]{1,0:T(8,128)(2,1)}, bf16[16,1536]{1,0:T(8,128)(2,1)S(1)}, u32[]{:S(2)}, u32[]{:S(2)}) %collective-permute-start) | collective-permute-done | bytes 49184 | tf_op jit(solution)/shard_map/ppermute | solution.py:186
  4.7 0.6 %constant_dynamic-update-slice_fusion.refs_0_ = bf16[32,1536]{1,0:T(8,128)(2,1)} fusion(bf16[32,1536]{1,0:T(8,128)(2,1)} %get-tuple-element.8, bf16[16,1536]{1,0:T(8,128)(2,1)S(1)} %collective-permute-done), kind=kLoop, calls=%fused_computation | loop fusion | bytes 98304 | tf_op jit(solution)/shard_map/dynamic_update_slice | solution.py:195
  5.4 0.2 collective-permute-start.3
  5.5 3.1 %collective-permute-start.2 = (bf16[32,1536]{1,0:T(8,128)(2,1)}, bf16[32,1536]{1,0:T(8,128)(2,1)S(1)}, u32[]{:S(2)}, u32[]{:S(2)}) collective-permute-start(bf16[32,1536]{1,0:T(8,128)(2,1)} %constant_dynamic-update-slice_fusion.refs_0_), channel_id=1, source_target_pairs={{0,2},{1,3},{2,4},{3,5},{4,6},{5,7},{6,0},{7,1},{8,10},{9,11},{10,... | collective-permute-start | bytes 294920 | tf_op jit(solution)/shard_map/ppermute | solution.py:186
  8.6 0.0 collective-permute-start.1
  8.6 0.0 collective-permute-done.4.refs_4_
  8.6 2.2 %collective-permute-start.7 = (bf16[32,1536]{1,0:T(8,128)(2,1)S(1)}, bf16[32,1536]{1,0:T(8,128)(2,1)S(1)}, u32[]{:S(2)}, u32[]{:S(2)}) collective-permute-start(bf16[32,1536]{1,0:T(8,128)(2,1)S(1)} %collective-permute-done.4.refs_4_), channel_id=1, source_target_pairs={{0,17},{1,16},{2,19},{3,18},{4,21},{5,20},{6,23},{7,22},{8,25},{9,... | collective-permute-start | bytes 294920 | tf_op jit(solution)/shard_map/ppermute | solution.py:186
  10.8 0.7 %collective-permute-start.6 = (bf16[32,1536]{1,0:T(8,128)(2,1)S(1)}, bf16[32,1536]{1,0:T(8,128)(2,1)S(1)}, u32[]{:S(2)}, u32[]{:S(2)}) collective-permute-start(bf16[32,1536]{1,0:T(8,128)(2,1)S(1)} %collective-permute-done.4.refs_4_), channel_id=1, source_target_pairs={{0,1},{1,0},{2,3},{3,2},{4,5},{5,4},{6,7},{7,6},{8,9},{9,8},{10,11... | collective-permute-start | bytes 294920 | tf_op jit(solution)/shard_map/ppermute | solution.py:186
  11.5 0.0 collective-permute-done.3.refs_3_
  11.5 0.7 %collective-permute-start.5 = (bf16[32,1536]{1,0:T(8,128)(2,1)S(1)}, bf16[32,1536]{1,0:T(8,128)(2,1)S(1)}, u32[]{:S(2)}, u32[]{:S(2)}) collective-permute-start(bf16[32,1536]{1,0:T(8,128)(2,1)S(1)} %collective-permute-done.4.refs_4_), channel_id=1, source_target_pairs={{0,16},{1,17},{2,18},{3,19},{4,20},{5,21},{6,22},{7,23},{8,24},{9,... | collective-permute-start | bytes 294920 | tf_op jit(solution)/shard_map/ppermute | solution.py:186
  12.2 0.0 collective-permute-done.2.refs_2_
  12.2 5.8 %collective-permute-start.8 = (bf16[32,1536]{1,0:T(8,128)(2,1)S(1)}, bf16[32,1536]{1,0:T(8,128)(2,1)S(1)}, u32[]{:S(2)}, u32[]{:S(2)}) collective-permute-start(bf16[32,1536]{1,0:T(8,128)(2,1)S(1)} %collective-permute-done.4.refs_4_), channel_id=1, source_target_pairs={{0,8},{1,9},{2,10},{3,11},{4,12},{5,13},{6,14},{7,15},{8,0},{9,1},... | collective-permute-start | bytes 294920 | tf_op jit(solution)/shard_map/ppermute | solution.py:186
  18.0 0.0 collective-permute-done.1.refs_1_
  18.0 0.0 collective-permute-done.7.refs_7_
  18.0 0.0 collective-permute-done.6.refs_6_
  18.0 3.6 %collective-permute-start.10 = (bf16[32,1536]{1,0:T(8,128)(2,1)S(1)}, bf16[32,1536]{1,0:T(8,128)(2,1)S(1)}, u32[]{:S(2)}, u32[]{:S(2)}) collective-permute-start(bf16[32,1536]{1,0:T(8,128)(2,1)S(1)} %collective-permute-done.6.refs_6_), channel_id=1, source_target_pairs={{0,8},{1,9},{2,10},{3,11},{4,12},{5,13},{6,14},{7,15},{8,0},{9,1},... | collective-permute-start | bytes 294920 | tf_op jit(solution)/shard_map/ppermute | solution.py:186
  21.6 0.0 collective-permute-done.5.refs_5_
  21.6 1.0 %collective-permute-start.9 = (bf16[32,1536]{1,0:T(8,128)(2,1)S(1)}, bf16[32,1536]{1,0:T(8,128)(2,1)S(1)}, u32[]{:S(2)}, u32[]{:S(2)}) collective-permute-start(bf16[32,1536]{1,0:T(8,128)(2,1)S(1)} %collective-permute-done.5.refs_5_), channel_id=1, source_target_pairs={{0,8},{1,9},{2,10},{3,11},{4,12},{5,13},{6,14},{7,15},{8,0},{9,1},... | collective-permute-start | bytes 294920 | tf_op jit(solution)/shard_map/ppermute | solution.py:186
  22.5 0.0 collective-permute-start.11
  22.5 0.0 collective-permute-done.8.refs_8_
  22.6 0.0 collective-permute-done.10.refs_10_
  22.6 0.9 %collective-permute-done.9.refs_9_ = bf16[32,1536]{1,0:T(8,128)(2,1)S(1)} collective-permute-done((bf16[32,1536]{1,0:T(8,128)(2,1)S(1)}, bf16[32,1536]{1,0:T(8,128)(2,1)S(1)}, u32[]{:S(2)}, u32[]{:S(2)}) %collective-permute-start.9) | collective-permute-done | bytes 98336 | tf_op jit(solution)/shard_map/ppermute | solution.py:186
  23.5 0.4 %collective-permute-done.11.refs_11_ = bf16[32,1536]{1,0:T(8,128)(2,1)S(1)} collective-permute-done((bf16[32,1536]{1,0:T(8,128)(2,1)S(1)}, bf16[32,1536]{1,0:T(8,128)(2,1)S(1)}, u32[]{:S(2)}, u32[]{:S(2)}) %collective-permute-start.11) | collective-permute-done | bytes 98336 | tf_op jit(solution)/shard_map/ppermute | solution.py:186
  23.8 0.0 copy-start
  23.8 1.9 %copy-done = bf16[2048,768]{1,0:T(8,128)(2,1)S(1)} copy-done((bf16[2048,768]{1,0:T(8,128)(2,1)S(1)}, bf16[2048,768]{1,0:T(8,128)(2,1)}, u32[]{:S(2)}) %copy-start) | copy-done | bytes 3145752
  25.7 0.0 copy-start.1
  25.7 0.9 %copy-done.1 = bf16[32,1536]{1,0:T(8,128)(2,1)S(1)} copy-done((bf16[32,1536]{1,0:T(8,128)(2,1)S(1)}, bf16[32,1536]{1,0:T(8,128)(2,1)}, u32[]{:S(2)}) %copy-start.1) | copy-done | bytes 98328
  26.6 0.0 copy-start.2
  26.6 0.7 %copy-done.2 = s32[8,32]{1,0:T(8,128)S(1)} copy-done((s32[8,32]{1,0:T(8,128)S(1)}, s32[8,32]{1,0:T(8,128)}, u32[]{:S(2)}) %copy-start.2) | copy-done | bytes 1048
  27.3 4.9 %shard_map.38 = f32[4,9,8,768]{3,2,1,0:T(8,128)} custom-call(bf16[32,1536]{1,0:T(8,128)(2,1)S(1)} %copy-done.1, bf16[32,1536]{1,0:T(8,128)(2,1)S(1)} %collective-permute-done.1.refs_1_, bf16[32,1536]{1,0:T(8,128)(2,1)S(1)} %collective-permute-done.2.refs_2_, bf16[32,1536]{1,0:T(8,128)(2,1)S(1)} %collective-permute-done.3.refs_3_, ...), custom_call_target="tpu_custom_call" | custom-call | tf_op jit(solution)/shard_map/pallas_call | solution.py:129
Async XLA Ops:
  1.6 3.2 %collective-permute-start = (bf16[16,1536]{1,0:T(8,128)(2,1)}, bf16[16,1536]{1,0:T(8,128)(2,1)S(1)}, u32[]{:S(2)}, u32[]{:S(2)}) collective-permute-start(bf16[16,1536]{1,0:T(8,128)(2,1)} %get-tuple-element.9), channel_id=1, source_target_pairs={{0,1},{1,0},{2,3},{3,2},{4,5},{5,4},{6,7},{7,6},{8,9},{9,8},{10,11... | collective-permute-start | bytes 147464 | tf_op jit(solution)/shard_map/ppermute | solution.py:186
  2.8 5.8 %collective-permute-start.4 = (bf16[32,1536]{1,0:T(8,128)(2,1)}, bf16[32,1536]{1,0:T(8,128)(2,1)S(1)}, u32[]{:S(2)}, u32[]{:S(2)}) collective-permute-start(bf16[32,1536]{1,0:T(8,128)(2,1)} %bitcast.2), channel_id=1, source_target_pairs={{0,24},{1,25},{2,16},{3,17},{4,8},{5,9},{6,0},{7,1},{8,26},{9,27},... | collective-permute-start | bytes 294920 | tf_op jit(solution)/shard_map/ppermute | solution.py:186
  5.4 6.2 %collective-permute-start.3 = (bf16[32,1536]{1,0:T(8,128)(2,1)}, bf16[32,1536]{1,0:T(8,128)(2,1)S(1)}, u32[]{:S(2)}, u32[]{:S(2)}) collective-permute-start(bf16[32,1536]{1,0:T(8,128)(2,1)} %constant_dynamic-update-slice_fusion.refs_0_), channel_id=1, source_target_pairs={{0,6},{1,7},{2,0},{3,1},{4,2},{5,3},{6,4},{7,5},{8,14},{9,15},{10,... | collective-permute-start | bytes 294920 | tf_op jit(solution)/shard_map/ppermute | solution.py:186
  5.5 6.7 %collective-permute-start.2 = (bf16[32,1536]{1,0:T(8,128)(2,1)}, bf16[32,1536]{1,0:T(8,128)(2,1)S(1)}, u32[]{:S(2)}, u32[]{:S(2)}) collective-permute-start(bf16[32,1536]{1,0:T(8,128)(2,1)} %constant_dynamic-update-slice_fusion.refs_0_), channel_id=1, source_target_pairs={{0,2},{1,3},{2,4},{3,5},{4,6},{5,7},{6,0},{7,1},{8,10},{9,11},{10,... | collective-permute-start | bytes 294920 | tf_op jit(solution)/shard_map/ppermute | solution.py:186
  8.6 9.4 %collective-permute-start.1 = (bf16[32,1536]{1,0:T(8,128)(2,1)}, bf16[32,1536]{1,0:T(8,128)(2,1)S(1)}, u32[]{:S(2)}, u32[]{:S(2)}) collective-permute-start(bf16[32,1536]{1,0:T(8,128)(2,1)} %constant_dynamic-update-slice_fusion.refs_0_), channel_id=1, source_target_pairs={{0,4},{1,5},{2,6},{3,7},{4,0},{5,1},{6,2},{7,3},{8,12},{9,13},{10,... | collective-permute-start | bytes 294920 | tf_op jit(solution)/shard_map/ppermute | solution.py:186
  8.6 9.4 %collective-permute-start.7 = (bf16[32,1536]{1,0:T(8,128)(2,1)S(1)}, bf16[32,1536]{1,0:T(8,128)(2,1)S(1)}, u32[]{:S(2)}, u32[]{:S(2)}) collective-permute-start(bf16[32,1536]{1,0:T(8,128)(2,1)S(1)} %collective-permute-done.4.refs_4_), channel_id=1, source_target_pairs={{0,17},{1,16},{2,19},{3,18},{4,21},{5,20},{6,23},{7,22},{8,25},{9,... | collective-permute-start | bytes 294920 | tf_op jit(solution)/shard_map/ppermute | solution.py:186
  10.8 7.2 %collective-permute-start.6 = (bf16[32,1536]{1,0:T(8,128)(2,1)S(1)}, bf16[32,1536]{1,0:T(8,128)(2,1)S(1)}, u32[]{:S(2)}, u32[]{:S(2)}) collective-permute-start(bf16[32,1536]{1,0:T(8,128)(2,1)S(1)} %collective-permute-done.4.refs_4_), channel_id=1, source_target_pairs={{0,1},{1,0},{2,3},{3,2},{4,5},{5,4},{6,7},{7,6},{8,9},{9,8},{10,11... | collective-permute-start | bytes 294920 | tf_op jit(solution)/shard_map/ppermute | solution.py:186
  11.5 10.1 %collective-permute-start.5 = (bf16[32,1536]{1,0:T(8,128)(2,1)S(1)}, bf16[32,1536]{1,0:T(8,128)(2,1)S(1)}, u32[]{:S(2)}, u32[]{:S(2)}) collective-permute-start(bf16[32,1536]{1,0:T(8,128)(2,1)S(1)} %collective-permute-done.4.refs_4_), channel_id=1, source_target_pairs={{0,16},{1,17},{2,18},{3,19},{4,20},{5,21},{6,22},{7,23},{8,24},{9,... | collective-permute-start | bytes 294920 | tf_op jit(solution)/shard_map/ppermute | solution.py:186
  12.2 10.3 %collective-permute-start.8 = (bf16[32,1536]{1,0:T(8,128)(2,1)S(1)}, bf16[32,1536]{1,0:T(8,128)(2,1)S(1)}, u32[]{:S(2)}, u32[]{:S(2)}) collective-permute-start(bf16[32,1536]{1,0:T(8,128)(2,1)S(1)} %collective-permute-done.4.refs_4_), channel_id=1, source_target_pairs={{0,8},{1,9},{2,10},{3,11},{4,12},{5,13},{6,14},{7,15},{8,0},{9,1},... | collective-permute-start | bytes 294920 | tf_op jit(solution)/shard_map/ppermute | solution.py:186
  18.0 4.5 %collective-permute-start.10 = (bf16[32,1536]{1,0:T(8,128)(2,1)S(1)}, bf16[32,1536]{1,0:T(8,128)(2,1)S(1)}, u32[]{:S(2)}, u32[]{:S(2)}) collective-permute-start(bf16[32,1536]{1,0:T(8,128)(2,1)S(1)} %collective-permute-done.6.refs_6_), channel_id=1, source_target_pairs={{0,8},{1,9},{2,10},{3,11},{4,12},{5,13},{6,14},{7,15},{8,0},{9,1},... | collective-permute-start | bytes 294920 | tf_op jit(solution)/shard_map/ppermute | solution.py:186
  21.6 1.9 %collective-permute-start.9 = (bf16[32,1536]{1,0:T(8,128)(2,1)S(1)}, bf16[32,1536]{1,0:T(8,128)(2,1)S(1)}, u32[]{:S(2)}, u32[]{:S(2)}) collective-permute-start(bf16[32,1536]{1,0:T(8,128)(2,1)S(1)} %collective-permute-done.5.refs_5_), channel_id=1, source_target_pairs={{0,8},{1,9},{2,10},{3,11},{4,12},{5,13},{6,14},{7,15},{8,0},{9,1},... | collective-permute-start | bytes 294920 | tf_op jit(solution)/shard_map/ppermute | solution.py:186
  22.5 1.3 %collective-permute-start.11 = (bf16[32,1536]{1,0:T(8,128)(2,1)S(1)}, bf16[32,1536]{1,0:T(8,128)(2,1)S(1)}, u32[]{:S(2)}, u32[]{:S(2)}) collective-permute-start(bf16[32,1536]{1,0:T(8,128)(2,1)S(1)} %collective-permute-done.7.refs_7_), channel_id=1, source_target_pairs={{0,8},{1,9},{2,10},{3,11},{4,12},{5,13},{6,14},{7,15},{8,0},{9,1},... | collective-permute-start | bytes 294920 | tf_op jit(solution)/shard_map/ppermute | solution.py:186
  23.8 1.9 %copy-start = (bf16[2048,768]{1,0:T(8,128)(2,1)S(1)}, bf16[2048,768]{1,0:T(8,128)(2,1)}, u32[]{:S(2)}) copy-start(bf16[2048,768]{1,0:T(8,128)(2,1)} %constant.6.clone.refs_13_) | copy-start | bytes 9437188
  25.7 0.9 %copy-start.1 = (bf16[32,1536]{1,0:T(8,128)(2,1)S(1)}, bf16[32,1536]{1,0:T(8,128)(2,1)}, u32[]{:S(2)}) copy-start(bf16[32,1536]{1,0:T(8,128)(2,1)} %constant_dynamic-update-slice_fusion.refs_0_) | copy-start | bytes 294916
  26.6 0.7 %copy-start.2 = (s32[8,32]{1,0:T(8,128)S(1)}, s32[8,32]{1,0:T(8,128)}, u32[]{:S(2)}) copy-start(s32[8,32]{1,0:T(8,128)} %refs_12_.1) | copy-start | bytes 3076

commit v3 on v2

v3 whole, which is shorter than its diff:
```python
import math

import jax
import jax.numpy as jnp
import numpy as np
from jax import lax
from jax.experimental import pallas as pl
from jax.experimental.pallas import tpu as pltpu
from jax.sharding import PartitionSpec as P

F = 1024
LAG = 768
DEC = 2
LANES = 128
CHUNKS = F // LANES
TILE = 256
AXES = ("row", "col", "win")


def build_table():
    shift = DEC * (np.arange(LAG, dtype=np.int64) - LAG // 2)
    phase = (np.arange(F, dtype=np.int64)[:, None] * shift[None, :]) % (2 * F)
    angle = phase.astype(np.float64) * (math.pi / F)
    scale = 1.0 / math.sqrt(F)
    both = np.stack([np.cos(angle) * scale, -np.sin(angle) * scale])
    both = both.reshape(2, CHUNKS, LANES, LAG).transpose(1, 0, 2, 3)
    return both.reshape(2 * F, LAG).astype(np.float32).astype(jnp.bfloat16)


def make_kernel(row_places, col_places, half, block, span):
    n_rows, n_cols = len(row_places), len(col_places)

    def kernel(*refs):
        row_slots, col_slots = refs[:n_rows], refs[n_rows : n_rows + n_cols]
        rmask, cmask, inv_ref, table_hbm, out_hbm, *scratch = refs[n_rows + n_cols :]
        left, right, cross, col_sum, col_diff, row_sum, staged, out_sem, table_ref, sem = scratch
        fetch = pltpu.make_async_copy(table_hbm, table_ref, sem)
        fetch.start()
        at = tuple(lax.axis_index(a) for a in AXES)
        win = at[2]
        per_shard = row_slots[0].shape[1] // LANES

        for ref, place in zip(row_slots, row_places):
            shard = place(*at)
            for h in range(2):
                own = win if h == 0 else 1 - win
                mask = rmask[own]
                for i in range(per_shard):
                    data = ref[h * span * half : (h + 1) * span * half, i * LANES : (i + 1) * LANES]
                    left[shard * per_shard + i, own] = data.astype(jnp.float32) * mask
        for ref, place in zip(col_slots, col_places):
            shard, own = place(*at)
            mask = cmask[own]
            for i in range(per_shard):
                data = ref[:, i * LANES : (i + 1) * LANES]
                right[shard * per_shard + i, own] = data.astype(jnp.float32) * mask

        windows = [(h, w) for h in range(2) for w in range(span)]

        def products(chunk, into):
            for b in range(3):
                for n, (h, w) in enumerate(windows):
                    c = right[2 * b * CHUNKS + chunk, h, w * block : (w + 1) * block]
                    e = right[(2 * b + 1) * CHUNKS + chunk, h, w * block : (w + 1) * block]
                    col_sum[b, n] = c + e
                    col_diff[b, n] = c - e
            for a in range(3):
                for h in range(2):
                    row_sum[a, h] = left[2 * a * CHUNKS + chunk, h] + left[(2 * a + 1) * CHUNKS + chunk, h]
            for a in range(3):
                one, two, three = {}, {}, {}
                for n, (h, w) in enumerate(windows):
                    c = [right[2 * b * CHUNKS + chunk, h, w * block : (w + 1) * block] for b in range(3)]
                    plus = [col_sum[b, n] for b in range(3)]
                    minus = [col_diff[b, n] for b in range(3)]
                    for s in range(half):
                        r = w * half + s
                        p = jnp.broadcast_to(left[2 * a * CHUNKS + chunk, h, r : r + 1], (block, LANES))
                        q = jnp.broadcast_to(left[(2 * a + 1) * CHUNKS + chunk, h, r : r + 1], (block, LANES))
                        pq = jnp.broadcast_to(row_sum[a, h, r : r + 1], (block, LANES))
                        for b in range(3):
                            x, y, z = pq * c[b], p * plus[b], q * minus[b]
                            one[s, b] = x if n == 0 else one[s, b] + x
                            two[s, b] = y if n == 0 else two[s, b] + y
                            three[s, b] = z if n == 0 else three[s, b] + z
                for pair in range(half // 2):
                    for b in range(3):
                        keys = [(2 * pair, b), (2 * pair + 1, b)]
                        re = jnp.concatenate([one[k] - three[k] for k in keys], 0).astype(jnp.bfloat16)
                        im = jnp.concatenate([one[k] - two[k] for k in keys], 0).astype(jnp.bfloat16)
                        first = ((pair * 3 + a) * 3 + b) * 2 * block
                        cross[into, first : first + 2 * block, :LANES] = re
                        cross[into, first : first + 2 * block, LANES:] = im

        def one_chunk(chunk, carry):
            products(chunk, chunk)
            return carry

        lax.fori_loop(0, CHUNKS, one_chunk, 0)
        fetch.wait()
        copies = []
        for n in range(LAG // TILE):
            acc = None
            for chunk in range(CHUNKS):
                new = jnp.dot(
                    cross[chunk],
                    table_ref[2 * LANES * chunk : 2 * LANES * (chunk + 1), n * TILE : (n + 1) * TILE],
                    preferred_element_type=jnp.float32,
                )
                acc = new if acc is None else acc + new
            for s in range(half):
                inv = inv_ref[s][:, :1]
                for c in range(9):
                    group = ((s // 2) * 9 + c) * 2 + s % 2
                    staged[n, s, c] = acc[group * block : (group + 1) * block] * inv
            copies.append(pltpu.make_async_copy(staged.at[n], out_hbm.at[:, :, :, pl.ds(n * TILE, TILE)], out_sem.at[n]))
            copies[-1].start()
        for copy in copies:
            copy.wait()

    return kernel


def masks(usable, half, block, span):
    def kernel(usable_ref, rmask, cmask, inv_ref):
        row, col, win = (lax.axis_index(a) for a in AXES)
        usable = usable_ref[...].astype(jnp.float32)
        stations = usable.shape[1]

        def column(first, count, h):
            rows = jnp.concatenate(
                [jnp.broadcast_to(usable[w : w + 1], (count, stations)) for w in range(h * span, (h + 1) * span)], 0
            )
            shape = (span * count, stations)
            picked = lax.broadcasted_iota(jnp.int32, shape, 1) == first + lax.broadcasted_iota(jnp.int32, shape, 0) % count
            return jnp.sum(jnp.where(picked, rows, 0.0), 1, keepdims=True)

        counts = [jnp.zeros((block, LANES), jnp.float32) for _ in range(half)]
        for h in range(2):
            rm = jnp.broadcast_to(column(row * block + win * half, half, h), (span * half, LANES))
            cm = jnp.broadcast_to(column(col * block, block, h), (span * block, LANES))
            rmask[h] = rm
            cmask[h] = cm
            for w in range(span):
                for s in range(half):
                    counts[s] = counts[s] + rm[w * half + s : w * half + s + 1] * cm[w * block : (w + 1) * block]
        for s in range(half):
            inv_ref[s] = 1.0 / jnp.maximum(counts[s], 1.0)

    in_vmem = pl.BlockSpec(memory_space=pltpu.VMEM)
    shapes = ((2, span * half, LANES), (2, span * block, LANES), (half, block, LANES))
    return pl.pallas_call(
        kernel,
        out_shape=tuple(jax.ShapeDtypeStruct(shape, jnp.float32) for shape in shapes),
        in_specs=[in_vmem],
        out_specs=(in_vmem,) * 3,
        compiler_params=pltpu.CompilerParams(vmem_limit_bytes=4 * 1024 * 1024),
    )(usable)


def correlate(rows, cols, flags, table, row_places, col_places, half, block, span):
    groups = half * 9 * block
    pieces = 6 * CHUNKS
    slots = len(rows) + len(cols) + 3
    hbm = pl.BlockSpec(memory_space=pltpu.HBM)
    return pl.pallas_call(
        make_kernel(row_places, col_places, half, block, span),
        out_shape=jax.ShapeDtypeStruct((half, 9, block, LAG), jnp.float32),
        in_specs=[pl.BlockSpec(memory_space=pltpu.VMEM)] * slots + [hbm],
        out_specs=hbm,
        scratch_shapes=[
            pltpu.VMEM((pieces, 2, span * half, LANES), jnp.float32),
            pltpu.VMEM((pieces, 2, span * block, LANES), jnp.float32),
            pltpu.VMEM((CHUNKS, groups, 2 * LANES), jnp.bfloat16),
            pltpu.VMEM((3, 2 * span, block, LANES), jnp.float32),
            pltpu.VMEM((3, 2 * span, block, LANES), jnp.float32),
            pltpu.VMEM((3, 2, span * half, LANES), jnp.float32),
            pltpu.VMEM((LAG // TILE, half, 9, block, TILE), jnp.float32),
            pltpu.SemaphoreType.DMA((LAG // TILE,)),
            pltpu.VMEM(table.shape, jnp.bfloat16),
            pltpu.SemaphoreType.DMA,
        ],
        compiler_params=pltpu.CompilerParams(vmem_limit_bytes=52 * 1024 * 1024),
    )(*rows, *cols, *flags, table)


def split_stations(spectra, half):
    span, block, shard = spectra.shape

    def kernel(spectra_ref, theirs_ref, mine_ref):
        low = [spectra_ref[w, :half] for w in range(span)]
        high = [spectra_ref[w, half:] for w in range(span)]
        first = lax.axis_index("win") == 0
        low, high = jnp.concatenate(low, 0), jnp.concatenate(high, 0)
        theirs_ref[...] = jnp.where(first, high, low)
        mine_ref[: span * half] = jnp.where(first, low, high)
        mine_ref[span * half :] = jnp.zeros((span * half, shard), jnp.bfloat16)

    in_vmem = pl.BlockSpec(memory_space=pltpu.VMEM)
    return pl.pallas_call(
        kernel,
        out_shape=(
            jax.ShapeDtypeStruct((span * half, shard), jnp.bfloat16),
            jax.ShapeDtypeStruct((2 * span * half, shard), jnp.bfloat16),
        ),
        in_specs=[in_vmem],
        out_specs=(in_vmem, in_vmem),
        compiler_params=pltpu.CompilerParams(vmem_limit_bytes=4 * 1024 * 1024),
    )(spectra)


def body(spectra, usable):
    span, block, shard = spectra.shape
    n_row, n_col, n_win = (lax.axis_size(a) for a in AXES)
    assert n_row == n_col and n_win == 2
    half = block // n_win

    def send(data, move):
        pairs = []
        for r in range(n_row):
            for c in range(n_col):
                for w in range(n_win):
                    r2, c2, w2 = move(r, c, w)
                    pairs.append(((r * n_col + c) * n_win + w, (r2 * n_col + c2) * n_win + w2))
        return lax.ppermute(data, AXES, pairs)

    def other_win(r, c, w):
        return r, c, 1 - w

    flat = spectra.reshape(span * block, shard)
    turned = send(flat, lambda r, c, w: (n_row - 1 - c, r, w))
    theirs, mine = split_stations(spectra, half)
    got = send(theirs, other_win)
    flags = masks(usable, half, block, span)
    mine, *flags = lax.optimization_barrier((mine, *flags))
    mine = lax.dynamic_update_slice(mine, got, (span * half, 0))

    if n_row == 4:
        across = send(mine, lambda r, c, w: (r, c ^ 2, w))
        beside = send(mine, lambda r, c, w: (r, c ^ 1, w))
        shifted = [across, beside, send(across, lambda r, c, w: (r, c ^ 1, w))]
        rows = [mine] + shifted
        row_places = [lambda r, c, w, k=k: c ^ k for k in (0, 2, 1, 3)]
        near = [
            turned,
            send(turned, lambda r, c, w: (r ^ 2, c, w)),
            send(turned, other_win),
            send(turned, lambda r, c, w: (r ^ 2, c, 1 - w)),
        ]
        last = lax.optimization_barrier((near[3], *shifted))[0]
        cols = near + [send(x, lambda r, c, w: (r ^ 1, c, w)) for x in near[:3] + [last]]
        col_places = [
            lambda r, c, w, e=e, d=d: (n_row - 1 - (r ^ e), w ^ d)
            for e, d in ((0, 0), (2, 0), (0, 1), (2, 1), (1, 0), (3, 0), (1, 1), (3, 1))
        ]
    else:
        gathered = lax.all_gather(mine, "col", axis=0)
        rows = [gathered[i] for i in range(n_col)]
        row_places = [lambda r, c, w, i=i: i for i in range(n_col)]
        near = lax.all_gather(turned, "row", axis=0)
        far = send(near, other_win)
        cols = [x[i] for x in (near, far) for i in range(n_row)]
        col_places = [lambda r, c, w, i=i, d=d: (n_row - 1 - i, w ^ d) for d in range(2) for i in range(n_row)]

    out = correlate(rows, cols, flags, jnp.asarray(build_table()), row_places, col_places, half, block, span)
    return out.transpose(0, 2, 1, 3)


def solution(mesh):
    placed = (P("win", "row", "col"), P())
    return jax.shard_map(
        body,
        mesh=mesh,
        in_specs=placed,
        out_specs=P(("row", "win"), "col", None, None),
        check_vma=False,
    )
```

time: 32.5 us -> 26.8 us (0.82)
  the two profiles are of different devices: /device:TPU:25 before, /device:TPU:29 now
where the time goes in v3:
time: 26.8 us; the launch traced here: 26.6 us
  starting transfers between devices  14.2 us (53%)
  waiting for transfers between devices  6.36 us (24%)
  Pallas kernels  5.28 us (20%)
  local copies, waits for them, and re-layouts  0.69 us (3%)
    ppermute x12, starting transfers between devices, send(): return lax.ppermute(data, AXES, pairs)  14.2 us
    ppermute x12, waiting for transfers between devices, send(): return lax.ppermute(data, AXES, pairs)  6.36 us
    pallas_call x1, Pallas kernels, correlate(): pl.pallas_call(make_kernel(row_places, col_places, half, block, span), ou...  4.25 us
    pallas_call x1, Pallas kernels, split_stations(): pl.pallas_call(kernel, out_shape=(jax.ShapeDtypeStruct((span * half, shar...  0.93 us
    unnamed x2, local copies, waits for them, and re-layouts  0.69 us
  transfers between devices with their start and end apart: 12, of which 3 were waited for; matrix products, arithmetic and copies ran while one was open for 0% of the time, Pallas kernels for 0%

profile of v3, /device:TPU:29, one launch (start us, length us, event | category | flops | bytes accessed | tf_op | source)
XLA Modules:
  0.0 26.6 jit_solution(1948294572631709089)
XLA Ops:
  0.0 0.9 %shard_map.37 = (bf16[16,1536]{1,0:T(8,128)(2,1)S(1)}, bf16[32,1536]{1,0:T(8,128)(2,1)S(1)}) custom-call(bf16[4,8,1536]{2,1,0:T(8,128)(2,1)} %spectra_ref.1), custom_call_target="tpu_custom_call" | custom-call | tf_op jit(solution)/shard_map/pallas_call | solution.py:200
  0.9 1.3 %collective-permute-start = (bf16[16,1536]{1,0:T(8,128)(2,1)S(1)}, bf16[16,1536]{1,0:T(8,128)(2,1)S(1)}, u32[]{:S(2)}, u32[]{:S(2)}) collective-permute-start(bf16[16,1536]{1,0:T(8,128)(2,1)S(1)} %get-tuple-element.20), channel_id=1, source_target_pairs={{0,1},{1,0},{2,3},{3,2},{4,5},{5,4},{6,7},{7,6},{8,9},{9,8},{10,11... | collective-permute-start | bytes 147464 | tf_op jit(solution)/shard_map/ppermute | solution.py:225
  2.2 1.1 %collective-permute-start.4 = (bf16[32,1536]{1,0:T(8,128)(2,1)}, bf16[32,1536]{1,0:T(8,128)(2,1)S(1)}, u32[]{:S(2)}, u32[]{:S(2)}) collective-permute-start(bf16[32,1536]{1,0:T(8,128)(2,1)} %bitcast), channel_id=1, source_target_pairs={{0,24},{1,25},{2,16},{3,17},{4,8},{5,9},{6,0},{7,1},{8,26},{9,27},... | collective-permute-start | bytes 294920 | tf_op jit(solution)/shard_map/ppermute | solution.py:225
  3.3 0.0 copy-start
  3.3 0.7 %copy-done = s32[8,32]{1,0:T(8,128)S(1)} copy-done((s32[8,32]{1,0:T(8,128)S(1)}, s32[8,32]{1,0:T(8,128)}, u32[]{:S(2)}) %copy-start) | copy-done | bytes 1048
  4.0 0.1 shard_map.38
  4.1 0.0 collective-permute-done
  4.1 2.2 %collective-permute-start.1 = (bf16[32,1536]{1,0:T(8,128)(2,1)S(1)}, bf16[32,1536]{1,0:T(8,128)(2,1)S(1)}, u32[]{:S(2)}, u32[]{:S(2)}) collective-permute-start(bf16[32,1536]{1,0:T(8,128)(2,1)S(1)} %constant_dynamic-update-slice_fusion.refs_0_), channel_id=1, source_target_pairs={{0,4},{1,5},{2,6},{3,7},{4,0},{5,1},{6,2},{7,3},{8,12},{9,13},{10,... | collective-permute-start | bytes 294920 | tf_op jit(solution)/shard_map/ppermute | solution.py:225
  6.3 0.3 %collective-permute-start.2 = (bf16[32,1536]{1,0:T(8,128)(2,1)S(1)}, bf16[32,1536]{1,0:T(8,128)(2,1)S(1)}, u32[]{:S(2)}, u32[]{:S(2)}) collective-permute-start(bf16[32,1536]{1,0:T(8,128)(2,1)S(1)} %constant_dynamic-update-slice_fusion.refs_0_), channel_id=1, source_target_pairs={{0,2},{1,3},{2,0},{3,1},{4,6},{5,7},{6,4},{7,5},{8,10},{9,11},{10,... | collective-permute-start | bytes 294920 | tf_op jit(solution)/shard_map/ppermute | solution.py:225
  6.6 1.8 %collective-permute-done.4.refs_4_ = bf16[32,1536]{1,0:T(8,128)(2,1)S(1)} collective-permute-done((bf16[32,1536]{1,0:T(8,128)(2,1)}, bf16[32,1536]{1,0:T(8,128)(2,1)S(1)}, u32[]{:S(2)}, u32[]{:S(2)}) %collective-permute-start.4) | collective-permute-done | bytes 98336 | tf_op jit(solution)/shard_map/ppermute | solution.py:225
  8.4 0.3 collective-permute-start.6
  8.7 0.0 collective-permute-start.5
  8.7 2.4 %collective-permute-start.7 = (bf16[32,1536]{1,0:T(8,128)(2,1)S(1)}, bf16[32,1536]{1,0:T(8,128)(2,1)S(1)}, u32[]{:S(2)}, u32[]{:S(2)}) collective-permute-start(bf16[32,1536]{1,0:T(8,128)(2,1)S(1)} %collective-permute-done.4.refs_4_), channel_id=1, source_target_pairs={{0,17},{1,16},{2,19},{3,18},{4,21},{5,20},{6,23},{7,22},{8,25},{9,... | collective-permute-start | bytes 294920 | tf_op jit(solution)/shard_map/ppermute | solution.py:225
  11.1 3.6 %collective-permute-done.1.refs_1_ = bf16[32,1536]{1,0:T(8,128)(2,1)S(1)} collective-permute-done((bf16[32,1536]{1,0:T(8,128)(2,1)S(1)}, bf16[32,1536]{1,0:T(8,128)(2,1)S(1)}, u32[]{:S(2)}, u32[]{:S(2)}) %collective-permute-start.1) | collective-permute-done | bytes 98336 | tf_op jit(solution)/shard_map/ppermute | solution.py:225
  14.7 0.0 collective-permute-start.3
  14.7 0.0 collective-permute-done.2.refs_2_
  14.7 2.3 %collective-permute-start.8 = (bf16[32,1536]{1,0:T(8,128)(2,1)S(1)}, bf16[32,1536]{1,0:T(8,128)(2,1)S(1)}, u32[]{:S(2)}, u32[]{:S(2)}) collective-permute-start(bf16[32,1536]{1,0:T(8,128)(2,1)S(1)} %collective-permute-done.4.refs_4_), channel_id=1, source_target_pairs={{0,8},{1,9},{2,10},{3,11},{4,12},{5,13},{6,14},{7,15},{8,0},{9,1},... | collective-permute-start | bytes 294920 | tf_op jit(solution)/shard_map/ppermute | solution.py:225
  17.0 0.0 collective-permute-done.6.refs_6_
  17.1 0.9 %collective-permute-start.10 = (bf16[32,1536]{1,0:T(8,128)(2,1)S(1)}, bf16[32,1536]{1,0:T(8,128)(2,1)S(1)}, u32[]{:S(2)}, u32[]{:S(2)}) collective-permute-start(bf16[32,1536]{1,0:T(8,128)(2,1)S(1)} %collective-permute-done.6.refs_6_), channel_id=1, source_target_pairs={{0,8},{1,9},{2,10},{3,11},{4,12},{5,13},{6,14},{7,15},{8,0},{9,1},... | collective-permute-start | bytes 294920 | tf_op jit(solution)/shard_map/ppermute | solution.py:225
  17.9 0.0 collective-permute-done.5.refs_5_
  17.9 1.6 %collective-permute-start.9 = (bf16[32,1536]{1,0:T(8,128)(2,1)S(1)}, bf16[32,1536]{1,0:T(8,128)(2,1)S(1)}, u32[]{:S(2)}, u32[]{:S(2)}) collective-permute-start(bf16[32,1536]{1,0:T(8,128)(2,1)S(1)} %collective-permute-done.5.refs_5_), channel_id=1, source_target_pairs={{0,8},{1,9},{2,10},{3,11},{4,12},{5,13},{6,14},{7,15},{8,0},{9,1},... | collective-permute-start | bytes 294920 | tf_op jit(solution)/shard_map/ppermute | solution.py:225
  19.5 0.0 collective-permute-done.7.refs_7_
  19.5 0.0 collective-permute-done.3.refs_3_
  19.5 1.9 %collective-permute-start.11 = (bf16[32,1536]{1,0:T(8,128)(2,1)S(1)}, bf16[32,1536]{1,0:T(8,128)(2,1)S(1)}, u32[]{:S(2)}, u32[]{:S(2)}) collective-permute-start(bf16[32,1536]{1,0:T(8,128)(2,1)S(1)} %collective-permute-done.7.refs_7_), channel_id=1, source_target_pairs={{0,8},{1,9},{2,10},{3,11},{4,12},{5,13},{6,14},{7,15},{8,0},{9,1},... | collective-permute-start | bytes 294920 | tf_op jit(solution)/shard_map/ppermute | solution.py:225
  21.4 0.0 collective-permute-done.8.refs_8_
  21.4 0.0 collective-permute-done.10.refs_10_
  21.4 0.0 collective-permute-done.9.refs_9_
  21.4 0.9 %collective-permute-done.11.refs_11_ = bf16[32,1536]{1,0:T(8,128)(2,1)S(1)} collective-permute-done((bf16[32,1536]{1,0:T(8,128)(2,1)S(1)}, bf16[32,1536]{1,0:T(8,128)(2,1)S(1)}, u32[]{:S(2)}, u32[]{:S(2)}) %collective-permute-start.11) | collective-permute-done | bytes 98336 | tf_op jit(solution)/shard_map/ppermute | solution.py:225
  22.4 4.2 %shard_map.39 = f32[4,9,8,768]{3,2,1,0:T(8,128)} custom-call(bf16[32,1536]{1,0:T(8,128)(2,1)S(1)} %constant_dynamic-update-slice_fusion.refs_0_, bf16[32,1536]{1,0:T(8,128)(2,1)S(1)} %collective-permute-done.1.refs_1_, bf16[32,1536]{1,0:T(8,128)(2,1)S(1)} %collective-permute-done.2.refs_2_, bf16[32,1536]{1,0:T(8,128)(2,1)S(1)} %collective-permute-done.3.refs_3_, ...), custom_call_target="tpu_custom_call" | custom-call | tf_op jit(solution)/shard_map/pallas_call | solution.py:166
  (1 shorter events, 0.0 us)
Async XLA Ops:
  0.9 3.1 %collective-permute-start = (bf16[16,1536]{1,0:T(8,128)(2,1)S(1)}, bf16[16,1536]{1,0:T(8,128)(2,1)S(1)}, u32[]{:S(2)}, u32[]{:S(2)}) collective-permute-start(bf16[16,1536]{1,0:T(8,128)(2,1)S(1)} %get-tuple-element.20), channel_id=1, source_target_pairs={{0,1},{1,0},{2,3},{3,2},{4,5},{5,4},{6,7},{7,6},{8,9},{9,8},{10,11... | collective-permute-start | bytes 147464 | tf_op jit(solution)/shard_map/ppermute | solution.py:225
  2.2 6.2 %collective-permute-start.4 = (bf16[32,1536]{1,0:T(8,128)(2,1)}, bf16[32,1536]{1,0:T(8,128)(2,1)S(1)}, u32[]{:S(2)}, u32[]{:S(2)}) collective-permute-start(bf16[32,1536]{1,0:T(8,128)(2,1)} %bitcast), channel_id=1, source_target_pairs={{0,24},{1,25},{2,16},{3,17},{4,8},{5,9},{6,0},{7,1},{8,26},{9,27},... | collective-permute-start | bytes 294920 | tf_op jit(solution)/shard_map/ppermute | solution.py:225
  3.3 0.7 %copy-start = (s32[8,32]{1,0:T(8,128)S(1)}, s32[8,32]{1,0:T(8,128)}, u32[]{:S(2)}) copy-start(s32[8,32]{1,0:T(8,128)} %usable_ref.1) | copy-start | bytes 3076
  4.1 10.6 %collective-permute-start.1 = (bf16[32,1536]{1,0:T(8,128)(2,1)S(1)}, bf16[32,1536]{1,0:T(8,128)(2,1)S(1)}, u32[]{:S(2)}, u32[]{:S(2)}) collective-permute-start(bf16[32,1536]{1,0:T(8,128)(2,1)S(1)} %constant_dynamic-update-slice_fusion.refs_0_), channel_id=1, source_target_pairs={{0,4},{1,5},{2,6},{3,7},{4,0},{5,1},{6,2},{7,3},{8,12},{9,13},{10,... | collective-permute-start | bytes 294920 | tf_op jit(solution)/shard_map/ppermute | solution.py:225
  6.3 8.4 %collective-permute-start.2 = (bf16[32,1536]{1,0:T(8,128)(2,1)S(1)}, bf16[32,1536]{1,0:T(8,128)(2,1)S(1)}, u32[]{:S(2)}, u32[]{:S(2)}) collective-permute-start(bf16[32,1536]{1,0:T(8,128)(2,1)S(1)} %constant_dynamic-update-slice_fusion.refs_0_), channel_id=1, source_target_pairs={{0,2},{1,3},{2,0},{3,1},{4,6},{5,7},{6,4},{7,5},{8,10},{9,11},{10,... | collective-permute-start | bytes 294920 | tf_op jit(solution)/shard_map/ppermute | solution.py:225
  8.4 8.6 %collective-permute-start.6 = (bf16[32,1536]{1,0:T(8,128)(2,1)S(1)}, bf16[32,1536]{1,0:T(8,128)(2,1)S(1)}, u32[]{:S(2)}, u32[]{:S(2)}) collective-permute-start(bf16[32,1536]{1,0:T(8,128)(2,1)S(1)} %collective-permute-done.4.refs_4_), channel_id=1, source_target_pairs={{0,1},{1,0},{2,3},{3,2},{4,5},{5,4},{6,7},{7,6},{8,9},{9,8},{10,11... | collective-permute-start | bytes 294920 | tf_op jit(solution)/shard_map/ppermute | solution.py:225
  8.7 9.3 %collective-permute-start.5 = (bf16[32,1536]{1,0:T(8,128)(2,1)S(1)}, bf16[32,1536]{1,0:T(8,128)(2,1)S(1)}, u32[]{:S(2)}, u32[]{:S(2)}) collective-permute-start(bf16[32,1536]{1,0:T(8,128)(2,1)S(1)} %collective-permute-done.4.refs_4_), channel_id=1, source_target_pairs={{0,16},{1,17},{2,18},{3,19},{4,20},{5,21},{6,22},{7,23},{8,24},{9,... | collective-permute-start | bytes 294920 | tf_op jit(solution)/shard_map/ppermute | solution.py:225
  8.7 10.8 %collective-permute-start.7 = (bf16[32,1536]{1,0:T(8,128)(2,1)S(1)}, bf16[32,1536]{1,0:T(8,128)(2,1)S(1)}, u32[]{:S(2)}, u32[]{:S(2)}) collective-permute-start(bf16[32,1536]{1,0:T(8,128)(2,1)S(1)} %collective-permute-done.4.refs_4_), channel_id=1, source_target_pairs={{0,17},{1,16},{2,19},{3,18},{4,21},{5,20},{6,23},{7,22},{8,25},{9,... | collective-permute-start | bytes 294920 | tf_op jit(solution)/shard_map/ppermute | solution.py:225
  14.7 4.8 %collective-permute-start.3 = (bf16[32,1536]{1,0:T(8,128)(2,1)S(1)}, bf16[32,1536]{1,0:T(8,128)(2,1)S(1)}, u32[]{:S(2)}, u32[]{:S(2)}) collective-permute-start(bf16[32,1536]{1,0:T(8,128)(2,1)S(1)} %collective-permute-done.1.refs_1_), channel_id=1, source_target_pairs={{0,2},{1,3},{2,0},{3,1},{4,6},{5,7},{6,4},{7,5},{8,10},{9,11},{10,... | collective-permute-start | bytes 294920 | tf_op jit(solution)/shard_map/ppermute | solution.py:225
  14.7 6.7 %collective-permute-start.8 = (bf16[32,1536]{1,0:T(8,128)(2,1)S(1)}, bf16[32,1536]{1,0:T(8,128)(2,1)S(1)}, u32[]{:S(2)}, u32[]{:S(2)}) collective-permute-start(bf16[32,1536]{1,0:T(8,128)(2,1)S(1)} %collective-permute-done.4.refs_4_), channel_id=1, source_target_pairs={{0,8},{1,9},{2,10},{3,11},{4,12},{5,13},{6,14},{7,15},{8,0},{9,1},... | collective-permute-start | bytes 294920 | tf_op jit(solution)/shard_map/ppermute | solution.py:225
  17.1 4.4 %collective-permute-start.10 = (bf16[32,1536]{1,0:T(8,128)(2,1)S(1)}, bf16[32,1536]{1,0:T(8,128)(2,1)S(1)}, u32[]{:S(2)}, u32[]{:S(2)}) collective-permute-start(bf16[32,1536]{1,0:T(8,128)(2,1)S(1)} %collective-permute-done.6.refs_6_), channel_id=1, source_target_pairs={{0,8},{1,9},{2,10},{3,11},{4,12},{5,13},{6,14},{7,15},{8,0},{9,1},... | collective-permute-start | bytes 294920 | tf_op jit(solution)/shard_map/ppermute | solution.py:225
  17.9 3.5 %collective-permute-start.9 = (bf16[32,1536]{1,0:T(8,128)(2,1)S(1)}, bf16[32,1536]{1,0:T(8,128)(2,1)S(1)}, u32[]{:S(2)}, u32[]{:S(2)}) collective-permute-start(bf16[32,1536]{1,0:T(8,128)(2,1)S(1)} %collective-permute-done.5.refs_5_), channel_id=1, source_target_pairs={{0,8},{1,9},{2,10},{3,11},{4,12},{5,13},{6,14},{7,15},{8,0},{9,1},... | collective-permute-start | bytes 294920 | tf_op jit(solution)/shard_map/ppermute | solution.py:225
  19.5 2.8 %collective-permute-start.11 = (bf16[32,1536]{1,0:T(8,128)(2,1)S(1)}, bf16[32,1536]{1,0:T(8,128)(2,1)S(1)}, u32[]{:S(2)}, u32[]{:S(2)}) collective-permute-start(bf16[32,1536]{1,0:T(8,128)(2,1)S(1)} %collective-permute-done.7.refs_7_), channel_id=1, source_target_pairs={{0,8},{1,9},{2,10},{3,11},{4,12},{5,13},{6,14},{7,15},{8,0},{9,1},... | collective-permute-start | bytes 294920 | tf_op jit(solution)/shard_map/ppermute | solution.py:225

commit v4 on v3

--- a/solution.py
+++ b/solution.py
@@ -154,6 +154,7 @@
         out_shape=tuple(jax.ShapeDtypeStruct(shape, jnp.float32) for shape in shapes),
         in_specs=[in_vmem],
         out_specs=(in_vmem,) * 3,
+        cost_estimate=pl.CostEstimate(flops=10**10, bytes_accessed=2**20, transcendentals=0),
         compiler_params=pltpu.CompilerParams(vmem_limit_bytes=4 * 1024 * 1024),
     )(usable)
 
@@ -236,11 +237,11 @@
     mine = lax.dynamic_update_slice(mine, got, (span * half, 0))
 
     if n_row == 4:
-        across = send(mine, lambda r, c, w: (r, c ^ 2, w))
+        across = send(mine, lambda r, c, w: (r, c ^ 3, w))
         beside = send(mine, lambda r, c, w: (r, c ^ 1, w))
         shifted = [across, beside, send(across, lambda r, c, w: (r, c ^ 1, w))]
         rows = [mine] + shifted
-        row_places = [lambda r, c, w, k=k: c ^ k for k in (0, 2, 1, 3)]
+        row_places = [lambda r, c, w, k=k: c ^ k for k in (0, 3, 1, 2)]
         near = [
             turned,
             send(turned, lambda r, c, w: (r ^ 2, c, w)),

time: 26.8 us -> 25.7 us (0.959)
  the two profiles are of different devices: /device:TPU:29 before, /device:TPU:0 now
where the time goes in v4:
time: 25.7 us; the launch traced here: 25.5 us
  starting transfers between devices  11.2 us (44%)
  waiting for transfers between devices  8.34 us (32%)
  Pallas kernels  4.39 us (17%)
  local copies, waits for them, and re-layouts  1.62 us (6%)
    ppermute x12, starting transfers between devices, send(): return lax.ppermute(data, AXES, pairs)  11.2 us
    ppermute x12, waiting for transfers between devices, send(): return lax.ppermute(data, AXES, pairs)  8.34 us
    pallas_call x1, Pallas kernels, correlate(): pl.pallas_call(make_kernel(row_places, col_places, half, block, span), ou...  4.25 us
    unnamed x4, local copies, waits for them, and re-layouts  1.61 us
  transfers between devices with their start and end apart: 12, of which 6 were waited for; matrix products, arithmetic and copies ran while one was open for 0% of the time, Pallas kernels for 1%

profile of v4, /device:TPU:0, one launch (start us, length us, event | category | flops | bytes accessed | tf_op | source)
XLA Modules:
  0.0 25.5 jit_solution(7748524645355872439)
XLA Ops:
  0.0 2.4 %collective-permute-start.4 = (bf16[32,1536]{1,0:T(8,128)(2,1)}, bf16[32,1536]{1,0:T(8,128)(2,1)S(1)}, u32[]{:S(2)}, u32[]{:S(2)}) collective-permute-start(bf16[32,1536]{1,0:T(8,128)(2,1)} %bitcast.2), channel_id=1, source_target_pairs={{0,24},{1,25},{2,16},{3,17},{4,8},{5,9},{6,0},{7,1},{8,26},{9,27},... | collective-permute-start | bytes 294920 | tf_op jit(solution)/shard_map/ppermute | solution.py:226
  2.4 0.0 copy-start
  2.4 0.9 %copy-done = bf16[4,8,1536]{2,1,0:T(8,128)(2,1)S(1)} copy-done((bf16[4,8,1536]{2,1,0:T(8,128)(2,1)S(1)}, bf16[4,8,1536]{2,1,0:T(8,128)(2,1)}, u32[]{:S(2)}) %copy-start) | copy-done | bytes 98328
  3.4 1.6 %collective-permute-start = (bf16[16,1536]{1,0:T(8,128)(2,1)S(1)}, bf16[16,1536]{1,0:T(8,128)(2,1)S(1)}, u32[]{:S(2)}, u32[]{:S(2)}) collective-permute-start(bf16[16,1536]{1,0:T(8,128)(2,1)S(1)} %get-tuple-element.20), channel_id=1, source_target_pairs={{0,1},{1,0},{2,3},{3,2},{4,5},{5,4},{6,7},{7,6},{8,9},{9,8},{10,11... | collective-permute-start | bytes 147464 | tf_op jit(solution)/shard_map/ppermute | solution.py:226
  4.9 0.0 copy-start.1
  4.9 0.7 %copy-done.1 = s32[8,32]{1,0:T(8,128)S(1)} copy-done((s32[8,32]{1,0:T(8,128)S(1)}, s32[8,32]{1,0:T(8,128)}, u32[]{:S(2)}) %copy-start.1) | copy-done | bytes 1048
  5.6 0.1 shard_map.38
  5.7 2.2 %collective-permute-done = bf16[16,1536]{1,0:T(8,128)(2,1)S(1)} collective-permute-done((bf16[16,1536]{1,0:T(8,128)(2,1)S(1)}, bf16[16,1536]{1,0:T(8,128)(2,1)S(1)}, u32[]{:S(2)}, u32[]{:S(2)}) %collective-permute-start) | collective-permute-done | bytes 49184 | tf_op jit(solution)/shard_map/ppermute | solution.py:226
  7.9 2.3 %collective-permute-start.1 = (bf16[32,1536]{1,0:T(8,128)(2,1)S(1)}, bf16[32,1536]{1,0:T(8,128)(2,1)S(1)}, u32[]{:S(2)}, u32[]{:S(2)}) collective-permute-start(bf16[32,1536]{1,0:T(8,128)(2,1)S(1)} %constant_dynamic-update-slice_fusion.refs_0_), channel_id=1, source_target_pairs={{0,6},{1,7},{2,4},{3,5},{4,2},{5,3},{6,0},{7,1},{8,14},{9,15},{10,... | collective-permute-start | bytes 294920 | tf_op jit(solution)/shard_map/ppermute | solution.py:226
  10.2 0.0 collective-permute-start.2
  10.2 0.0 collective-permute-done.4.refs_4_
  10.2 1.7 %collective-permute-start.6 = (bf16[32,1536]{1,0:T(8,128)(2,1)S(1)}, bf16[32,1536]{1,0:T(8,128)(2,1)S(1)}, u32[]{:S(2)}, u32[]{:S(2)}) collective-permute-start(bf16[32,1536]{1,0:T(8,128)(2,1)S(1)} %collective-permute-done.4.refs_4_), channel_id=1, source_target_pairs={{0,1},{1,0},{2,3},{3,2},{4,5},{5,4},{6,7},{7,6},{8,9},{9,8},{10,11... | collective-permute-start | bytes 294920 | tf_op jit(solution)/shard_map/ppermute | solution.py:226
  11.9 1.7 %collective-permute-start.5 = (bf16[32,1536]{1,0:T(8,128)(2,1)S(1)}, bf16[32,1536]{1,0:T(8,128)(2,1)S(1)}, u32[]{:S(2)}, u32[]{:S(2)}) collective-permute-start(bf16[32,1536]{1,0:T(8,128)(2,1)S(1)} %collective-permute-done.4.refs_4_), channel_id=1, source_target_pairs={{0,16},{1,17},{2,18},{3,19},{4,20},{5,21},{6,22},{7,23},{8,24},{9,... | collective-permute-start | bytes 294920 | tf_op jit(solution)/shard_map/ppermute | solution.py:226
  13.6 0.1 collective-permute-start.7
  13.7 1.7 %collective-permute-done.1.refs_1_ = bf16[32,1536]{1,0:T(8,128)(2,1)S(1)} collective-permute-done((bf16[32,1536]{1,0:T(8,128)(2,1)S(1)}, bf16[32,1536]{1,0:T(8,128)(2,1)S(1)}, u32[]{:S(2)}, u32[]{:S(2)}) %collective-permute-start.1) | collective-permute-done | bytes 98336 | tf_op jit(solution)/shard_map/ppermute | solution.py:226
  15.4 0.9 %collective-permute-start.3 = (bf16[32,1536]{1,0:T(8,128)(2,1)S(1)}, bf16[32,1536]{1,0:T(8,128)(2,1)S(1)}, u32[]{:S(2)}, u32[]{:S(2)}) collective-permute-start(bf16[32,1536]{1,0:T(8,128)(2,1)S(1)} %collective-permute-done.1.refs_1_), channel_id=1, source_target_pairs={{0,2},{1,3},{2,0},{3,1},{4,6},{5,7},{6,4},{7,5},{8,10},{9,11},{10,... | collective-permute-start | bytes 294920 | tf_op jit(solution)/shard_map/ppermute | solution.py:226
  16.3 0.0 collective-permute-done.2.refs_2_
  16.3 0.0 collective-permute-start.8
  16.3 0.0 collective-permute-done.6.refs_6_
  16.3 0.5 %collective-permute-start.10 = (bf16[32,1536]{1,0:T(8,128)(2,1)S(1)}, bf16[32,1536]{1,0:T(8,128)(2,1)S(1)}, u32[]{:S(2)}, u32[]{:S(2)}) collective-permute-start(bf16[32,1536]{1,0:T(8,128)(2,1)S(1)} %collective-permute-done.6.refs_6_), channel_id=1, source_target_pairs={{0,8},{1,9},{2,10},{3,11},{4,12},{5,13},{6,14},{7,15},{8,0},{9,1},... | collective-permute-start | bytes 294920 | tf_op jit(solution)/shard_map/ppermute | solution.py:226
  16.8 0.8 %collective-permute-done.5.refs_5_ = bf16[32,1536]{1,0:T(8,128)(2,1)S(1)} collective-permute-done((bf16[32,1536]{1,0:T(8,128)(2,1)S(1)}, bf16[32,1536]{1,0:T(8,128)(2,1)S(1)}, u32[]{:S(2)}, u32[]{:S(2)}) %collective-permute-start.5) | collective-permute-done | bytes 98336 | tf_op jit(solution)/shard_map/ppermute | solution.py:226
  17.6 0.0 collective-permute-start.9
  17.6 1.5 %collective-permute-done.7.refs_7_ = bf16[32,1536]{1,0:T(8,128)(2,1)S(1)} collective-permute-done((bf16[32,1536]{1,0:T(8,128)(2,1)S(1)}, bf16[32,1536]{1,0:T(8,128)(2,1)S(1)}, u32[]{:S(2)}, u32[]{:S(2)}) %collective-permute-start.7) | collective-permute-done | bytes 98336 | tf_op jit(solution)/shard_map/ppermute | solution.py:226
  19.1 0.9 %collective-permute-done.3.refs_3_ = bf16[32,1536]{1,0:T(8,128)(2,1)S(1)} collective-permute-done((bf16[32,1536]{1,0:T(8,128)(2,1)S(1)}, bf16[32,1536]{1,0:T(8,128)(2,1)S(1)}, u32[]{:S(2)}, u32[]{:S(2)}) %collective-permute-start.3) | collective-permute-done | bytes 98336 | tf_op jit(solution)/shard_map/ppermute | solution.py:226
  20.0 0.0 collective-permute-start.11
  20.0 0.0 collective-permute-done.8.refs_8_
  20.0 0.0 collective-permute-done.10.refs_10_
  20.0 0.0 collective-permute-done.9.refs_9_
  20.0 1.3 %collective-permute-done.11.refs_11_ = bf16[32,1536]{1,0:T(8,128)(2,1)S(1)} collective-permute-done((bf16[32,1536]{1,0:T(8,128)(2,1)S(1)}, bf16[32,1536]{1,0:T(8,128)(2,1)S(1)}, u32[]{:S(2)}, u32[]{:S(2)}) %collective-permute-start.11) | collective-permute-done | bytes 98336 | tf_op jit(solution)/shard_map/ppermute | solution.py:226
  21.3 4.2 %shard_map.39 = f32[4,9,8,768]{3,2,1,0:T(8,128)} custom-call(bf16[32,1536]{1,0:T(8,128)(2,1)S(1)} %constant_dynamic-update-slice_fusion.refs_0_, bf16[32,1536]{1,0:T(8,128)(2,1)S(1)} %collective-permute-done.1.refs_1_, bf16[32,1536]{1,0:T(8,128)(2,1)S(1)} %collective-permute-done.2.refs_2_, bf16[32,1536]{1,0:T(8,128)(2,1)S(1)} %collective-permute-done.3.refs_3_, ...), custom_call_target="tpu_custom_call" | custom-call | tf_op jit(solution)/shard_map/pallas_call | solution.py:167
  (2 shorter events, 0.0 us)
Async XLA Ops:
  0.0 10.2 %collective-permute-start.4 = (bf16[32,1536]{1,0:T(8,128)(2,1)}, bf16[32,1536]{1,0:T(8,128)(2,1)S(1)}, u32[]{:S(2)}, u32[]{:S(2)}) collective-permute-start(bf16[32,1536]{1,0:T(8,128)(2,1)} %bitcast.2), channel_id=1, source_target_pairs={{0,24},{1,25},{2,16},{3,17},{4,8},{5,9},{6,0},{7,1},{8,26},{9,27},... | collective-permute-start | bytes 294920 | tf_op jit(solution)/shard_map/ppermute | solution.py:226
  2.4 0.9 %copy-start = (bf16[4,8,1536]{2,1,0:T(8,128)(2,1)S(1)}, bf16[4,8,1536]{2,1,0:T(8,128)(2,1)}, u32[]{:S(2)}) copy-start(bf16[4,8,1536]{2,1,0:T(8,128)(2,1)} %spectra_ref.1) | copy-start | bytes 294916
  3.4 4.5 %collective-permute-start = (bf16[16,1536]{1,0:T(8,128)(2,1)S(1)}, bf16[16,1536]{1,0:T(8,128)(2,1)S(1)}, u32[]{:S(2)}, u32[]{:S(2)}) collective-permute-start(bf16[16,1536]{1,0:T(8,128)(2,1)S(1)} %get-tuple-element.20), channel_id=1, source_target_pairs={{0,1},{1,0},{2,3},{3,2},{4,5},{5,4},{6,7},{7,6},{8,9},{9,8},{10,11... | collective-permute-start | bytes 147464 | tf_op jit(solution)/shard_map/ppermute | solution.py:226
  4.9 0.7 %copy-start.1 = (s32[8,32]{1,0:T(8,128)S(1)}, s32[8,32]{1,0:T(8,128)}, u32[]{:S(2)}) copy-start(s32[8,32]{1,0:T(8,128)} %usable_ref.1) | copy-start | bytes 3076
  7.9 7.5 %collective-permute-start.1 = (bf16[32,1536]{1,0:T(8,128)(2,1)S(1)}, bf16[32,1536]{1,0:T(8,128)(2,1)S(1)}, u32[]{:S(2)}, u32[]{:S(2)}) collective-permute-start(bf16[32,1536]{1,0:T(8,128)(2,1)S(1)} %constant_dynamic-update-slice_fusion.refs_0_), channel_id=1, source_target_pairs={{0,6},{1,7},{2,4},{3,5},{4,2},{5,3},{6,0},{7,1},{8,14},{9,15},{10,... | collective-permute-start | bytes 294920 | tf_op jit(solution)/shard_map/ppermute | solution.py:226
  10.2 6.1 %collective-permute-start.2 = (bf16[32,1536]{1,0:T(8,128)(2,1)S(1)}, bf16[32,1536]{1,0:T(8,128)(2,1)S(1)}, u32[]{:S(2)}, u32[]{:S(2)}) collective-permute-start(bf16[32,1536]{1,0:T(8,128)(2,1)S(1)} %constant_dynamic-update-slice_fusion.refs_0_), channel_id=1, source_target_pairs={{0,2},{1,3},{2,0},{3,1},{4,6},{5,7},{6,4},{7,5},{8,10},{9,11},{10,... | collective-permute-start | bytes 294920 | tf_op jit(solution)/shard_map/ppermute | solution.py:226
  10.2 6.1 %collective-permute-start.6 = (bf16[32,1536]{1,0:T(8,128)(2,1)S(1)}, bf16[32,1536]{1,0:T(8,128)(2,1)S(1)}, u32[]{:S(2)}, u32[]{:S(2)}) collective-permute-start(bf16[32,1536]{1,0:T(8,128)(2,1)S(1)} %collective-permute-done.4.refs_4_), channel_id=1, source_target_pairs={{0,1},{1,0},{2,3},{3,2},{4,5},{5,4},{6,7},{7,6},{8,9},{9,8},{10,11... | collective-permute-start | bytes 294920 | tf_op jit(solution)/shard_map/ppermute | solution.py:226
  11.9 5.7 %collective-permute-start.5 = (bf16[32,1536]{1,0:T(8,128)(2,1)S(1)}, bf16[32,1536]{1,0:T(8,128)(2,1)S(1)}, u32[]{:S(2)}, u32[]{:S(2)}) collective-permute-start(bf16[32,1536]{1,0:T(8,128)(2,1)S(1)} %collective-permute-done.4.refs_4_), channel_id=1, source_target_pairs={{0,16},{1,17},{2,18},{3,19},{4,20},{5,21},{6,22},{7,23},{8,24},{9,... | collective-permute-start | bytes 294920 | tf_op jit(solution)/shard_map/ppermute | solution.py:226
  13.6 5.5 %collective-permute-start.7 = (bf16[32,1536]{1,0:T(8,128)(2,1)S(1)}, bf16[32,1536]{1,0:T(8,128)(2,1)S(1)}, u32[]{:S(2)}, u32[]{:S(2)}) collective-permute-start(bf16[32,1536]{1,0:T(8,128)(2,1)S(1)} %collective-permute-done.4.refs_4_), channel_id=1, source_target_pairs={{0,17},{1,16},{2,19},{3,18},{4,21},{5,20},{6,23},{7,22},{8,25},{9,... | collective-permute-start | bytes 294920 | tf_op jit(solution)/shard_map/ppermute | solution.py:226
  15.4 4.6 %collective-permute-start.3 = (bf16[32,1536]{1,0:T(8,128)(2,1)S(1)}, bf16[32,1536]{1,0:T(8,128)(2,1)S(1)}, u32[]{:S(2)}, u32[]{:S(2)}) collective-permute-start(bf16[32,1536]{1,0:T(8,128)(2,1)S(1)} %collective-permute-done.1.refs_1_), channel_id=1, source_target_pairs={{0,2},{1,3},{2,0},{3,1},{4,6},{5,7},{6,4},{7,5},{8,10},{9,11},{10,... | collective-permute-start | bytes 294920 | tf_op jit(solution)/shard_map/ppermute | solution.py:226
  16.3 3.7 %collective-permute-start.8 = (bf16[32,1536]{1,0:T(8,128)(2,1)S(1)}, bf16[32,1536]{1,0:T(8,128)(2,1)S(1)}, u32[]{:S(2)}, u32[]{:S(2)}) collective-permute-start(bf16[32,1536]{1,0:T(8,128)(2,1)S(1)} %collective-permute-done.4.refs_4_), channel_id=1, source_target_pairs={{0,8},{1,9},{2,10},{3,11},{4,12},{5,13},{6,14},{7,15},{8,0},{9,1},... | collective-permute-start | bytes 294920 | tf_op jit(solution)/shard_map/ppermute | solution.py:226
  16.3 3.7 %collective-permute-start.10 = (bf16[32,1536]{1,0:T(8,128)(2,1)S(1)}, bf16[32,1536]{1,0:T(8,128)(2,1)S(1)}, u32[]{:S(2)}, u32[]{:S(2)}) collective-permute-start(bf16[32,1536]{1,0:T(8,128)(2,1)S(1)} %collective-permute-done.6.refs_6_), channel_id=1, source_target_pairs={{0,8},{1,9},{2,10},{3,11},{4,12},{5,13},{6,14},{7,15},{8,0},{9,1},... | collective-permute-start | bytes 294920 | tf_op jit(solution)/shard_map/ppermute | solution.py:226
  17.6 2.4 %collective-permute-start.9 = (bf16[32,1536]{1,0:T(8,128)(2,1)S(1)}, bf16[32,1536]{1,0:T(8,128)(2,1)S(1)}, u32[]{:S(2)}, u32[]{:S(2)}) collective-permute-start(bf16[32,1536]{1,0:T(8,128)(2,1)S(1)} %collective-permute-done.5.refs_5_), channel_id=1, source_target_pairs={{0,8},{1,9},{2,10},{3,11},{4,12},{5,13},{6,14},{7,15},{8,0},{9,1},... | collective-permute-start | bytes 294920 | tf_op jit(solution)/shard_map/ppermute | solution.py:226
  20.0 1.3 %collective-permute-start.11 = (bf16[32,1536]{1,0:T(8,128)(2,1)S(1)}, bf16[32,1536]{1,0:T(8,128)(2,1)S(1)}, u32[]{:S(2)}, u32[]{:S(2)}) collective-permute-start(bf16[32,1536]{1,0:T(8,128)(2,1)S(1)} %collective-permute-done.7.refs_7_), channel_id=1, source_target_pairs={{0,8},{1,9},{2,10},{3,11},{4,12},{5,13},{6,14},{7,15},{8,0},{9,1},... | collective-permute-start | bytes 294920 | tf_op jit(solution)/shard_map/ppermute | solution.py:226

commit v5 on v4

v5 whole, which is shorter than its diff:
```python
import math

import jax
import jax.numpy as jnp
import numpy as np
from jax import lax
from jax.experimental import pallas as pl
from jax.experimental.pallas import tpu as pltpu
from jax.sharding import PartitionSpec as P

F = 1024
LAG = 768
DEC = 2
LANES = 128
CHUNKS = F // LANES
TILE = 256
FIRST_FLOPS = 10**9
AXES = ("row", "col", "win")


def build_table():
    shift = DEC * (np.arange(LAG, dtype=np.int64) - LAG // 2)
    phase = (np.arange(F, dtype=np.int64)[:, None] * shift[None, :]) % (2 * F)
    angle = phase.astype(np.float64) * (math.pi / F)
    scale = 1.0 / math.sqrt(F)
    both = np.stack([np.cos(angle) * scale, -np.sin(angle) * scale])
    both = both.reshape(2, CHUNKS, LANES, LAG).transpose(1, 0, 2, 3)
    return both.reshape(2 * F, LAG).astype(np.float32).astype(jnp.bfloat16)


def half_products(second, row_slots, col_slots, row_places, col_places, rmask, cmask, scratch, half, block, span, emit):
    left, right, col_sum, col_diff, row_sum = scratch
    at = tuple(lax.axis_index(name) for name in AXES)
    own = 1 - at[2] if second else at[2]
    per_shard = row_slots[0].shape[1] // LANES
    first_row = span * half if second else 0

    mask = rmask[own]
    for ref, place in zip(row_slots, row_places):
        shard = place(*at)
        for i in range(per_shard):
            data = ref[first_row : first_row + span * half, i * LANES : (i + 1) * LANES]
            left[shard * per_shard + i] = data.astype(jnp.float32) * mask
    mask = cmask[own]
    for ref, place in zip(col_slots, col_places):
        shard = place(*at)
        for i in range(per_shard):
            right[shard * per_shard + i] = ref[:, i * LANES : (i + 1) * LANES].astype(jnp.float32) * mask

    def one_chunk(chunk, carry):
        for b in range(3):
            c, e = right[2 * b * CHUNKS + chunk], right[(2 * b + 1) * CHUNKS + chunk]
            col_sum[b] = c + e
            col_diff[b] = c - e
        for a in range(3):
            row_sum[a] = left[2 * a * CHUNKS + chunk] + left[(2 * a + 1) * CHUNKS + chunk]
        for a in range(3):
            one, two, three = {}, {}, {}
            for w in range(span):
                rows = slice(w * block, (w + 1) * block)
                c = [right[2 * b * CHUNKS + chunk, rows] for b in range(3)]
                plus = [col_sum[b, rows] for b in range(3)]
                minus = [col_diff[b, rows] for b in range(3)]
                for s in range(half):
                    r = w * half + s
                    p = jnp.broadcast_to(left[2 * a * CHUNKS + chunk, r : r + 1], (block, LANES))
                    q = jnp.broadcast_to(left[(2 * a + 1) * CHUNKS + chunk, r : r + 1], (block, LANES))
                    pq = jnp.broadcast_to(row_sum[a, r : r + 1], (block, LANES))
                    for b in range(3):
                        x, y, z = pq * c[b], p * plus[b], q * minus[b]
                        one[s, b] = x if w == 0 else one[s, b] + x
                        two[s, b] = y if w == 0 else two[s, b] + y
                        three[s, b] = z if w == 0 else three[s, b] + z
            for pair in range(half // 2):
                for b in range(3):
                    keys = [(2 * pair, b), (2 * pair + 1, b)]
                    first = ((pair * 3 + a) * 3 + b) * 2 * block
                    emit(chunk, first, [one[k] - three[k] for k in keys], [one[k] - two[k] for k in keys])
        return carry

    lax.fori_loop(0, CHUNKS, one_chunk, 0)


def half_scratch(half, block, span):
    pieces = 6 * CHUNKS
    return [
        pltpu.VMEM((pieces, span * half, LANES), jnp.float32),
        pltpu.VMEM((pieces, span * block, LANES), jnp.float32),
        pltpu.VMEM((3, span * block, LANES), jnp.float32),
        pltpu.VMEM((3, span * block, LANES), jnp.float32),
        pltpu.VMEM((3, span * half, LANES), jnp.float32),
    ]


def first_half(rows, cols, rmask, cmask, row_places, col_places, half, block, span):
    n_rows, n_cols = len(rows), len(cols)
    groups = half * 9 * block

    def kernel(*refs):
        row_slots, col_slots = refs[:n_rows], refs[n_rows : n_rows + n_cols]
        rmask, cmask, real_ref, imag_ref, *scratch = refs[n_rows + n_cols :]

        def emit(chunk, first, reals, imags):
            for n in range(2):
                real_ref[chunk, first + n * block : first + (n + 1) * block] = reals[n]
                imag_ref[chunk, first + n * block : first + (n + 1) * block] = imags[n]

        half_products(
            False, row_slots, col_slots, row_places, col_places, rmask, cmask, scratch, half, block, span, emit
        )

    in_vmem = pl.BlockSpec(memory_space=pltpu.VMEM)
    return pl.pallas_call(
        kernel,
        out_shape=(jax.ShapeDtypeStruct((CHUNKS, groups, LANES), jnp.float32),) * 2,
        in_specs=[in_vmem] * (n_rows + n_cols + 2),
        out_specs=(in_vmem,) * 2,
        scratch_shapes=half_scratch(half, block, span),
        cost_estimate=pl.CostEstimate(flops=FIRST_FLOPS, bytes_accessed=2**20, transcendentals=0),
        compiler_params=pltpu.CompilerParams(vmem_limit_bytes=32 * 1024 * 1024),
    )(*rows, *cols, rmask, cmask)


def correlate(rows, cols, parts, flags, table, row_places, col_places, half, block, span):
    n_rows, n_cols = len(rows), len(cols)
    groups = half * 9 * block

    def kernel(*refs):
        row_slots, col_slots = refs[:n_rows], refs[n_rows : n_rows + n_cols]
        real_ref, imag_ref, rmask, cmask, inv_ref, table_ref, out_hbm, *scratch = refs[n_rows + n_cols :]
        *scratch, cross, staged, out_sem = scratch

        def emit(chunk, first, reals, imags):
            rows = slice(first, first + 2 * block)
            re = real_ref[chunk, rows] + jnp.concatenate(reals, 0)
            im = imag_ref[chunk, rows] + jnp.concatenate(imags, 0)
            cross[chunk, rows, :LANES] = re.astype(jnp.bfloat16)
            cross[chunk, rows, LANES:] = im.astype(jnp.bfloat16)

        half_products(
            True, row_slots, col_slots, row_places, col_places, rmask, cmask, scratch, half, block, span, emit
        )
        copies = []
        for n in range(LAG // TILE):
            acc = None
            for chunk in range(CHUNKS):
                new = jnp.dot(
                    cross[chunk],
                    table_ref[2 * LANES * chunk : 2 * LANES * (chunk + 1), n * TILE : (n + 1) * TILE],
                    preferred_element_type=jnp.float32,
                )
                acc = new if acc is None else acc + new
            for s in range(half):
                inv = inv_ref[s][:, :1]
                for c in range(9):
                    group = ((s // 2) * 9 + c) * 2 + s % 2
                    staged[n, s, c] = acc[group * block : (group + 1) * block] * inv
            copies.append(pltpu.make_async_copy(staged.at[n], out_hbm.at[:, :, :, pl.ds(n * TILE, TILE)], out_sem.at[n]))
            copies[-1].start()
        for copy in copies:
            copy.wait()

    return pl.pallas_call(
        kernel,
        out_shape=jax.ShapeDtypeStruct((half, 9, block, LAG), jnp.float32),
        in_specs=[pl.BlockSpec(memory_space=pltpu.VMEM)] * (n_rows + n_cols + 6),
        out_specs=pl.BlockSpec(memory_space=pltpu.HBM),
        scratch_shapes=half_scratch(half, block, span)
        + [
            pltpu.VMEM((CHUNKS, groups, 2 * LANES), jnp.bfloat16),
            pltpu.VMEM((LAG // TILE, half, 9, block, TILE), jnp.float32),
            pltpu.SemaphoreType.DMA((LAG // TILE,)),
        ],
        compiler_params=pltpu.CompilerParams(vmem_limit_bytes=40 * 1024 * 1024),
    )(*rows, *cols, *parts, *flags, table)


def masks(usable, half, block, span):
    def kernel(usable_ref, rmask, cmask, inv_ref):
        row, col, win = (lax.axis_index(a) for a in AXES)
        usable = usable_ref[...].astype(jnp.float32)
        stations = usable.shape[1]

        def column(first, count, h):
            rows = jnp.concatenate(
                [jnp.broadcast_to(usable[w : w + 1], (count, stations)) for w in range(h * span, (h + 1) * span)], 0
            )
            shape = (span * count, stations)
            picked = lax.broadcasted_iota(jnp.int32, shape, 1) == first + lax.broadcasted_iota(jnp.int32, shape, 0) % count
            return jnp.sum(jnp.where(picked, rows, 0.0), 1, keepdims=True)

        counts = [jnp.zeros((block, LANES), jnp.float32) for _ in range(half)]
        for h in range(2):
            rm = jnp.broadcast_to(column(row * block + win * half, half, h), (span * half, LANES))
            cm = jnp.broadcast_to(column(col * block, block, h), (span * block, LANES))
            rmask[h] = rm
            cmask[h] = cm
            for w in range(span):
                for s in range(half):
                    counts[s] = counts[s] + rm[w * half + s : w * half + s + 1] * cm[w * block : (w + 1) * block]
        for s in range(half):
            inv_ref[s] = 1.0 / jnp.maximum(counts[s], 1.0)

    in_vmem = pl.BlockSpec(memory_space=pltpu.VMEM)
    shapes = ((2, span * half, LANES), (2, span * block, LANES), (half, block, LANES))
    return pl.pallas_call(
        kernel,
        out_shape=tuple(jax.ShapeDtypeStruct(shape, jnp.float32) for shape in shapes),
        in_specs=[in_vmem],
        out_specs=(in_vmem,) * 3,
        cost_estimate=pl.CostEstimate(flops=10**10, bytes_accessed=2**20, transcendentals=0),
        compiler_params=pltpu.CompilerParams(vmem_limit_bytes=4 * 1024 * 1024),
    )(usable)


def split_stations(spectra, half):
    span, block, shard = spectra.shape

    def kernel(spectra_ref, theirs_ref, mine_ref):
        low = [spectra_ref[w, :half] for w in range(span)]
        high = [spectra_ref[w, half:] for w in range(span)]
        first = lax.axis_index("win") == 0
        low, high = jnp.concatenate(low, 0), jnp.concatenate(high, 0)
        theirs_ref[...] = jnp.where(first, high, low)
        mine_ref[: span * half] = jnp.where(first, low, high)
        mine_ref[span * half :] = jnp.zeros((span * half, shard), jnp.bfloat16)

    in_vmem = pl.BlockSpec(memory_space=pltpu.VMEM)
    return pl.pallas_call(
        kernel,
        out_shape=(
            jax.ShapeDtypeStruct((span * half, shard), jnp.bfloat16),
            jax.ShapeDtypeStruct((2 * span * half, shard), jnp.bfloat16),
        ),
        in_specs=[in_vmem],
        out_specs=(in_vmem, in_vmem),
        compiler_params=pltpu.CompilerParams(vmem_limit_bytes=4 * 1024 * 1024),
    )(spectra)


def body(spectra, usable):
    span, block, shard = spectra.shape
    n_row, n_col, n_win = (lax.axis_size(a) for a in AXES)
    assert n_row == n_col and n_win == 2
    half = block // n_win

    def send(data, move):
        pairs = []
        for r in range(n_row):
            for c in range(n_col):
                for w in range(n_win):
                    r2, c2, w2 = move(r, c, w)
                    pairs.append(((r * n_col + c) * n_win + w, (r2 * n_col + c2) * n_win + w2))
        return lax.ppermute(data, AXES, pairs)

    def other_win(r, c, w):
        return r, c, 1 - w

    flat = spectra.reshape(span * block, shard)
    turned = send(flat, lambda r, c, w: (n_row - 1 - c, r, w))
    theirs, mine = split_stations(spectra, half)
    got = send(theirs, other_win)
    flags = masks(usable, half, block, span)
    mine, *flags = lax.optimization_barrier((mine, *flags))
    mine = lax.dynamic_update_slice(mine, got, (span * half, 0))

    if n_row == 4:
        across = send(mine, lambda r, c, w: (r, c ^ 3, w))
        beside = send(mine, lambda r, c, w: (r, c ^ 1, w))
        shifted = [across, beside, send(across, lambda r, c, w: (r, c ^ 1, w))]
        rows = [mine] + shifted
        row_places = [lambda r, c, w, k=k: c ^ k for k in (0, 3, 1, 2)]
        near = [
            turned,
            send(turned, lambda r, c, w: (r ^ 2, c, w)),
            send(turned, other_win),
            send(turned, lambda r, c, w: (r ^ 2, c, 1 - w)),
        ]
        last = lax.optimization_barrier((near[3], *shifted))[0]
        swapped = [send(x, lambda r, c, w: (r ^ 1, c, w)) for x in near[:3] + [last]]
        cols = [[*near[:2], *swapped[:2]], [*near[2:], *swapped[2:]]]
        col_places = [lambda r, c, w, e=e: n_row - 1 - (r ^ e) for e in (0, 2, 1, 3)]
    else:
        gathered = lax.all_gather(mine, "col", axis=0)
        rows = [gathered[i] for i in range(n_col)]
        row_places = [lambda r, c, w, i=i: i for i in range(n_col)]
        near = lax.all_gather(turned, "row", axis=0)
        far = send(near, other_win)
        cols = [[x[i] for i in range(n_row)] for x in (near, far)]
        col_places = [lambda r, c, w, i=i: n_row - 1 - i for i in range(n_row)]

    parts = first_half(rows, cols[0], *flags[:2], row_places, col_places, half, block, span)
    out = correlate(
        rows, cols[1], parts, flags, jnp.asarray(build_table()), row_places, col_places, half, block, span
    )
    return out.transpose(0, 2, 1, 3)


def solution(mesh):
    placed = (P("win", "row", "col"), P())
    return jax.shard_map(
        body,
        mesh=mesh,
        in_specs=placed,
        out_specs=P(("row", "win"), "col", None, None),
        check_vma=False,
    )
```

time: 25.7 us -> 24.8 us (0.965)
  waiting for transfers between devices: 8.34 us -> 7.2 us
    ppermute x12, waiting for transfers between devices: 8.34 us -> 7.2 us  [send(): return lax.ppermute(data, AXES, pairs)]
    pallas_call x1 -> x2, Pallas kernels: 4.25 us -> 4.26 us  [the longest x1 3.12 us: correlate(): pl.pallas_call(kernel, out_shape=jax.ShapeDtypeStruct((half, 9, block, LA...]
    unnamed x4 -> x6, local copies, waits for them, and re-layouts: 1.61 us -> 1.62 us
  transfers between devices with their start and end apart: 12 -> 12, of which waited for: 6 -> 6; matrix products, arithmetic and copies ran while one was open for 0% -> 0% of each run, Pallas kernels for 1% -> 5%
where the time goes in v5:
time: 24.8 us; the launch traced here: 24.4 us
  starting transfers between devices  11.2 us (45%)
  waiting for transfers between devices  7.2 us (29%)
  Pallas kernels  4.4 us (18%)
  local copies, waits for them, and re-layouts  1.62 us (7%)
    ppermute x12, starting transfers between devices, send(): return lax.ppermute(data, AXES, pairs)  11.2 us
    ppermute x12, waiting for transfers between devices, send(): return lax.ppermute(data, AXES, pairs)  7.2 us
    pallas_call x1, Pallas kernels, correlate(): pl.pallas_call(kernel, out_shape=jax.ShapeDtypeStruct((half, 9, block, LA...  3.12 us
    unnamed x6, local copies, waits for them, and re-layouts  1.62 us
    pallas_call x1, Pallas kernels, first_half(): pl.pallas_call(kernel, out_shape=(jax.ShapeDtypeStruct((CHUNKS, groups, L...  1.14 us
  transfers between devices with their start and end apart: 12, of which 6 were waited for; matrix products, arithmetic and copies ran while one was open for 0% of the time, Pallas kernels for 5%

profile of v5, /device:TPU:0, one launch (start us, length us, event | category | flops | bytes accessed | tf_op | source)
XLA Modules:
  0.0 24.4 jit_solution(15448659022545230462)
XLA Ops:
  0.0 2.4 %collective-permute-start.4 = (bf16[32,1536]{1,0:T(8,128)(2,1)}, bf16[32,1536]{1,0:T(8,128)(2,1)S(1)}, u32[]{:S(2)}, u32[]{:S(2)}) collective-permute-start(bf16[32,1536]{1,0:T(8,128)(2,1)} %bitcast.2), channel_id=1, source_target_pairs={{0,24},{1,25},{2,16},{3,17},{4,8},{5,9},{6,0},{7,1},{8,26},{9,27},... | collective-permute-start | bytes 294920 | tf_op jit(solution)/shard_map/ppermute | solution.py:254
  2.4 0.0 copy-start.1
  2.4 0.9 %copy-done.1 = bf16[4,8,1536]{2,1,0:T(8,128)(2,1)S(1)} copy-done((bf16[4,8,1536]{2,1,0:T(8,128)(2,1)S(1)}, bf16[4,8,1536]{2,1,0:T(8,128)(2,1)}, u32[]{:S(2)}) %copy-start.1) | copy-done | bytes 98328
  3.4 1.6 %collective-permute-start = (bf16[16,1536]{1,0:T(8,128)(2,1)S(1)}, bf16[16,1536]{1,0:T(8,128)(2,1)S(1)}, u32[]{:S(2)}, u32[]{:S(2)}) collective-permute-start(bf16[16,1536]{1,0:T(8,128)(2,1)S(1)} %get-tuple-element.22), channel_id=1, source_target_pairs={{0,1},{1,0},{2,3},{3,2},{4,5},{5,4},{6,7},{7,6},{8,9},{9,8},{10,11... | collective-permute-start | bytes 147464 | tf_op jit(solution)/shard_map/ppermute | solution.py:254
  4.9 0.0 copy-start.2
  4.9 0.7 %copy-done.2 = s32[8,32]{1,0:T(8,128)S(1)} copy-done((s32[8,32]{1,0:T(8,128)S(1)}, s32[8,32]{1,0:T(8,128)}, u32[]{:S(2)}) %copy-start.2) | copy-done | bytes 1048
  5.6 0.1 shard_map.38
  5.7 2.2 %collective-permute-done = bf16[16,1536]{1,0:T(8,128)(2,1)S(1)} collective-permute-done((bf16[16,1536]{1,0:T(8,128)(2,1)S(1)}, bf16[16,1536]{1,0:T(8,128)(2,1)S(1)}, u32[]{:S(2)}, u32[]{:S(2)}) %collective-permute-start) | collective-permute-done | bytes 49184 | tf_op jit(solution)/shard_map/ppermute | solution.py:254
  7.9 0.0 copy-start
  7.9 2.3 %collective-permute-start.1 = (bf16[32,1536]{1,0:T(8,128)(2,1)S(1)}, bf16[32,1536]{1,0:T(8,128)(2,1)S(1)}, u32[]{:S(2)}, u32[]{:S(2)}) collective-permute-start(bf16[32,1536]{1,0:T(8,128)(2,1)S(1)} %constant_dynamic-update-slice_fusion.refs_0_), channel_id=1, source_target_pairs={{0,6},{1,7},{2,4},{3,5},{4,2},{5,3},{6,0},{7,1},{8,14},{9,15},{10,... | collective-permute-start | bytes 294920 | tf_op jit(solution)/shard_map/ppermute | solution.py:254
  10.2 0.0 collective-permute-start.2
  10.2 0.0 collective-permute-done.4.refs_4_
  10.2 1.9 %collective-permute-start.9 = (bf16[32,1536]{1,0:T(8,128)(2,1)S(1)}, bf16[32,1536]{1,0:T(8,128)(2,1)S(1)}, u32[]{:S(2)}, u32[]{:S(2)}) collective-permute-start(bf16[32,1536]{1,0:T(8,128)(2,1)S(1)} %collective-permute-done.4.refs_4_), channel_id=1, source_target_pairs={{0,16},{1,17},{2,18},{3,19},{4,20},{5,21},{6,22},{7,23},{8,24},{9,... | collective-permute-start | bytes 294920 | tf_op jit(solution)/shard_map/ppermute | solution.py:254
  12.1 1.5 %collective-permute-start.5 = (bf16[32,1536]{1,0:T(8,128)(2,1)S(1)}, bf16[32,1536]{1,0:T(8,128)(2,1)S(1)}, u32[]{:S(2)}, u32[]{:S(2)}) collective-permute-start(bf16[32,1536]{1,0:T(8,128)(2,1)S(1)} %collective-permute-done.4.refs_4_), channel_id=1, source_target_pairs={{0,1},{1,0},{2,3},{3,2},{4,5},{5,4},{6,7},{7,6},{8,9},{9,8},{10,11... | collective-permute-start | bytes 294920 | tf_op jit(solution)/shard_map/ppermute | solution.py:254
  13.6 0.1 collective-permute-start.6
  13.7 1.7 %collective-permute-done.1.refs_1_ = bf16[32,1536]{1,0:T(8,128)(2,1)S(1)} collective-permute-done((bf16[32,1536]{1,0:T(8,128)(2,1)S(1)}, bf16[32,1536]{1,0:T(8,128)(2,1)S(1)}, u32[]{:S(2)}, u32[]{:S(2)}) %collective-permute-start.1) | collective-permute-done | bytes 98336 | tf_op jit(solution)/shard_map/ppermute | solution.py:254
  15.4 0.9 %collective-permute-start.3 = (bf16[32,1536]{1,0:T(8,128)(2,1)S(1)}, bf16[32,1536]{1,0:T(8,128)(2,1)S(1)}, u32[]{:S(2)}, u32[]{:S(2)}) collective-permute-start(bf16[32,1536]{1,0:T(8,128)(2,1)S(1)} %collective-permute-done.1.refs_1_), channel_id=1, source_target_pairs={{0,2},{1,3},{2,0},{3,1},{4,6},{5,7},{6,4},{7,5},{8,10},{9,11},{10,... | collective-permute-start | bytes 294920 | tf_op jit(solution)/shard_map/ppermute | solution.py:254
  16.3 0.0 collective-permute-done.2.refs_2_
  16.3 0.0 collective-permute-start.10
  16.3 0.0 collective-permute-done.9.refs_5_
  16.3 0.5 %collective-permute-start.11 = (bf16[32,1536]{1,0:T(8,128)(2,1)S(1)}, bf16[32,1536]{1,0:T(8,128)(2,1)S(1)}, u32[]{:S(2)}, u32[]{:S(2)}) collective-permute-start(bf16[32,1536]{1,0:T(8,128)(2,1)S(1)} %collective-permute-done.9.refs_5_), channel_id=1, source_target_pairs={{0,8},{1,9},{2,10},{3,11},{4,12},{5,13},{6,14},{7,15},{8,0},{9,1},... | collective-permute-start | bytes 294920 | tf_op jit(solution)/shard_map/ppermute | solution.py:254
  16.8 0.2 collective-permute-done.5.refs_4_
  17.0 0.0 collective-permute-start.7
  17.0 2.1 %collective-permute-done.6.refs_5_ = bf16[32,1536]{1,0:T(8,128)(2,1)S(1)} collective-permute-done((bf16[32,1536]{1,0:T(8,128)(2,1)S(1)}, bf16[32,1536]{1,0:T(8,128)(2,1)S(1)}, u32[]{:S(2)}, u32[]{:S(2)}) %collective-permute-start.6) | collective-permute-done | bytes 98336 | tf_op jit(solution)/shard_map/ppermute | solution.py:254
  19.1 0.9 %collective-permute-done.3.refs_3_ = bf16[32,1536]{1,0:T(8,128)(2,1)S(1)} collective-permute-done((bf16[32,1536]{1,0:T(8,128)(2,1)S(1)}, bf16[32,1536]{1,0:T(8,128)(2,1)S(1)}, u32[]{:S(2)}, u32[]{:S(2)}) %collective-permute-start.3) | collective-permute-done | bytes 98336 | tf_op jit(solution)/shard_map/ppermute | solution.py:254
  20.0 0.0 collective-permute-start.8
  20.0 0.0 collective-permute-done.10.refs_6_
  20.0 0.0 collective-permute-done.11.refs_7_
  20.0 1.1 %shard_map.39 = (f32[8,288,128]{2,1,0:T(8,128)S(1)}, f32[8,288,128]{2,1,0:T(8,128)S(1)}) custom-call(bf16[32,1536]{1,0:T(8,128)(2,1)S(1)} %constant_dynamic-update-slice_fusion.refs_0_, bf16[32,1536]{1,0:T(8,128)(2,1)S(1)} %collective-permute-done.1.refs_1_, bf16[32,1536]{1,0:T(8,128)(2,1)S(1)} %collective-permute-done.2.refs_2_, ...), custom_call_target="tpu_custom_call" | custom-call | flops 1000000000 | bytes 1048576 | tf_op jit(solution)/shard_map/pallas_call | solution.py:113
  21.2 0.0 collective-permute-done.7.refs_6_
  21.2 0.1 collective-permute-done.8.refs_7_
  21.3 0.0 copy-done
  21.3 3.1 %shard_map.40 = f32[4,9,8,768]{3,2,1,0:T(8,128)} custom-call(bf16[32,1536]{1,0:T(8,128)(2,1)S(1)} %constant_dynamic-update-slice_fusion.refs_0_, bf16[32,1536]{1,0:T(8,128)(2,1)S(1)} %collective-permute-done.1.refs_1_, bf16[32,1536]{1,0:T(8,128)(2,1)S(1)} %collective-permute-done.2.refs_2_, bf16[32,1536]{1,0:T(8,128)(2,1)S(1)} %collective-permute-done.3.refs_3_, ...), custom_call_target="tpu_custom_call" | custom-call | tf_op jit(solution)/shard_map/pallas_call | solution.py:163
  (2 shorter events, 0.0 us)
Async XLA Ops:
  0.0 10.2 %collective-permute-start.4 = (bf16[32,1536]{1,0:T(8,128)(2,1)}, bf16[32,1536]{1,0:T(8,128)(2,1)S(1)}, u32[]{:S(2)}, u32[]{:S(2)}) collective-permute-start(bf16[32,1536]{1,0:T(8,128)(2,1)} %bitcast.2), channel_id=1, source_target_pairs={{0,24},{1,25},{2,16},{3,17},{4,8},{5,9},{6,0},{7,1},{8,26},{9,27},... | collective-permute-start | bytes 294920 | tf_op jit(solution)/shard_map/ppermute | solution.py:254
  2.4 0.9 %copy-start.1 = (bf16[4,8,1536]{2,1,0:T(8,128)(2,1)S(1)}, bf16[4,8,1536]{2,1,0:T(8,128)(2,1)}, u32[]{:S(2)}) copy-start(bf16[4,8,1536]{2,1,0:T(8,128)(2,1)} %spectra_ref.1) | copy-start | bytes 294916
  3.4 4.5 %collective-permute-start = (bf16[16,1536]{1,0:T(8,128)(2,1)S(1)}, bf16[16,1536]{1,0:T(8,128)(2,1)S(1)}, u32[]{:S(2)}, u32[]{:S(2)}) collective-permute-start(bf16[16,1536]{1,0:T(8,128)(2,1)S(1)} %get-tuple-element.22), channel_id=1, source_target_pairs={{0,1},{1,0},{2,3},{3,2},{4,5},{5,4},{6,7},{7,6},{8,9},{9,8},{10,11... | collective-permute-start | bytes 147464 | tf_op jit(solution)/shard_map/ppermute | solution.py:254
  4.9 0.7 %copy-start.2 = (s32[8,32]{1,0:T(8,128)S(1)}, s32[8,32]{1,0:T(8,128)}, u32[]{:S(2)}) copy-start(s32[8,32]{1,0:T(8,128)} %usable_ref.1) | copy-start | bytes 3076
  7.9 13.4 %copy-start = (bf16[2048,768]{1,0:T(8,128)(2,1)S(1)}, bf16[2048,768]{1,0:T(8,128)(2,1)}, u32[]{:S(2)}) copy-start(bf16[2048,768]{1,0:T(8,128)(2,1)} %constant.6.clone.refs_13_) | copy-start | bytes 9437188
  7.9 7.5 %collective-permute-start.1 = (bf16[32,1536]{1,0:T(8,128)(2,1)S(1)}, bf16[32,1536]{1,0:T(8,128)(2,1)S(1)}, u32[]{:S(2)}, u32[]{:S(2)}) collective-permute-start(bf16[32,1536]{1,0:T(8,128)(2,1)S(1)} %constant_dynamic-update-slice_fusion.refs_0_), channel_id=1, source_target_pairs={{0,6},{1,7},{2,4},{3,5},{4,2},{5,3},{6,0},{7,1},{8,14},{9,15},{10,... | collective-permute-start | bytes 294920 | tf_op jit(solution)/shard_map/ppermute | solution.py:254
  10.2 6.1 %collective-permute-start.2 = (bf16[32,1536]{1,0:T(8,128)(2,1)S(1)}, bf16[32,1536]{1,0:T(8,128)(2,1)S(1)}, u32[]{:S(2)}, u32[]{:S(2)}) collective-permute-start(bf16[32,1536]{1,0:T(8,128)(2,1)S(1)} %constant_dynamic-update-slice_fusion.refs_0_), channel_id=1, source_target_pairs={{0,2},{1,3},{2,0},{3,1},{4,6},{5,7},{6,4},{7,5},{8,10},{9,11},{10,... | collective-permute-start | bytes 294920 | tf_op jit(solution)/shard_map/ppermute | solution.py:254
  10.2 6.1 %collective-permute-start.9 = (bf16[32,1536]{1,0:T(8,128)(2,1)S(1)}, bf16[32,1536]{1,0:T(8,128)(2,1)S(1)}, u32[]{:S(2)}, u32[]{:S(2)}) collective-permute-start(bf16[32,1536]{1,0:T(8,128)(2,1)S(1)} %collective-permute-done.4.refs_4_), channel_id=1, source_target_pairs={{0,16},{1,17},{2,18},{3,19},{4,20},{5,21},{6,22},{7,23},{8,24},{9,... | collective-permute-start | bytes 294920 | tf_op jit(solution)/shard_map/ppermute | solution.py:254
  12.1 4.9 %collective-permute-start.5 = (bf16[32,1536]{1,0:T(8,128)(2,1)S(1)}, bf16[32,1536]{1,0:T(8,128)(2,1)S(1)}, u32[]{:S(2)}, u32[]{:S(2)}) collective-permute-start(bf16[32,1536]{1,0:T(8,128)(2,1)S(1)} %collective-permute-done.4.refs_4_), channel_id=1, source_target_pairs={{0,1},{1,0},{2,3},{3,2},{4,5},{5,4},{6,7},{7,6},{8,9},{9,8},{10,11... | collective-permute-start | bytes 294920 | tf_op jit(solution)/shard_map/ppermute | solution.py:254
  13.6 5.5 %collective-permute-start.6 = (bf16[32,1536]{1,0:T(8,128)(2,1)S(1)}, bf16[32,1536]{1,0:T(8,128)(2,1)S(1)}, u32[]{:S(2)}, u32[]{:S(2)}) collective-permute-start(bf16[32,1536]{1,0:T(8,128)(2,1)S(1)} %collective-permute-done.4.refs_4_), channel_id=1, source_target_pairs={{0,17},{1,16},{2,19},{3,18},{4,21},{5,20},{6,23},{7,22},{8,25},{9,... | collective-permute-start | bytes 294920 | tf_op jit(solution)/shard_map/ppermute | solution.py:254
  15.4 4.6 %collective-permute-start.3 = (bf16[32,1536]{1,0:T(8,128)(2,1)S(1)}, bf16[32,1536]{1,0:T(8,128)(2,1)S(1)}, u32[]{:S(2)}, u32[]{:S(2)}) collective-permute-start(bf16[32,1536]{1,0:T(8,128)(2,1)S(1)} %collective-permute-done.1.refs_1_), channel_id=1, source_target_pairs={{0,2},{1,3},{2,0},{3,1},{4,6},{5,7},{6,4},{7,5},{8,10},{9,11},{10,... | collective-permute-start | bytes 294920 | tf_op jit(solution)/shard_map/ppermute | solution.py:254
  16.3 3.7 %collective-permute-start.10 = (bf16[32,1536]{1,0:T(8,128)(2,1)S(1)}, bf16[32,1536]{1,0:T(8,128)(2,1)S(1)}, u32[]{:S(2)}, u32[]{:S(2)}) collective-permute-start(bf16[32,1536]{1,0:T(8,128)(2,1)S(1)} %collective-permute-done.4.refs_4_), channel_id=1, source_target_pairs={{0,8},{1,9},{2,10},{3,11},{4,12},{5,13},{6,14},{7,15},{8,0},{9,1},... | collective-permute-start | bytes 294920 | tf_op jit(solution)/shard_map/ppermute | solution.py:254
  16.3 3.7 %collective-permute-start.11 = (bf16[32,1536]{1,0:T(8,128)(2,1)S(1)}, bf16[32,1536]{1,0:T(8,128)(2,1)S(1)}, u32[]{:S(2)}, u32[]{:S(2)}) collective-permute-start(bf16[32,1536]{1,0:T(8,128)(2,1)S(1)} %collective-permute-done.9.refs_5_), channel_id=1, source_target_pairs={{0,8},{1,9},{2,10},{3,11},{4,12},{5,13},{6,14},{7,15},{8,0},{9,1},... | collective-permute-start | bytes 294920 | tf_op jit(solution)/shard_map/ppermute | solution.py:254
  17.0 4.1 %collective-permute-start.7 = (bf16[32,1536]{1,0:T(8,128)(2,1)S(1)}, bf16[32,1536]{1,0:T(8,128)(2,1)S(1)}, u32[]{:S(2)}, u32[]{:S(2)}) collective-permute-start(bf16[32,1536]{1,0:T(8,128)(2,1)S(1)} %collective-permute-done.5.refs_4_), channel_id=1, source_target_pairs={{0,8},{1,9},{2,10},{3,11},{4,12},{5,13},{6,14},{7,15},{8,0},{9,1},... | collective-permute-start | bytes 294920 | tf_op jit(solution)/shard_map/ppermute | solution.py:254
  20.0 1.3 %collective-permute-start.8 = (bf16[32,1536]{1,0:T(8,128)(2,1)S(1)}, bf16[32,1536]{1,0:T(8,128)(2,1)S(1)}, u32[]{:S(2)}, u32[]{:S(2)}) collective-permute-start(bf16[32,1536]{1,0:T(8,128)(2,1)S(1)} %collective-permute-done.6.refs_5_), channel_id=1, source_target_pairs={{0,8},{1,9},{2,10},{3,11},{4,12},{5,13},{6,14},{7,15},{8,0},{9,1},... | collective-permute-start | bytes 294920 | tf_op jit(solution)/shard_map/ppermute | solution.py:254

commit v6 on v5

--- a/solution.py
+++ b/solution.py
@@ -266,7 +266,8 @@
 
     if n_row == 4:
         across = send(mine, lambda r, c, w: (r, c ^ 3, w))
-        beside = send(mine, lambda r, c, w: (r, c ^ 1, w))
+        ready = lax.optimization_barrier((mine, turned))[0]
+        beside = send(ready, lambda r, c, w: (r, c ^ 1, w))
         shifted = [across, beside, send(across, lambda r, c, w: (r, c ^ 1, w))]
         rows = [mine] + shifted
         row_places = [lambda r, c, w, k=k: c ^ k for k in (0, 3, 1, 2)]

time: 24.8 us -> 24.6 us (level)
  waiting for transfers between devices: 7.2 us -> 6.81 us
  starting transfers between devices: 11.2 us -> 11.5 us
    ppermute x12, waiting for transfers between devices: 7.2 us -> 6.81 us  [send(): return lax.ppermute(data, AXES, pairs)]
    ppermute x12, starting transfers between devices: 11.2 us -> 11.5 us  [send(): return lax.ppermute(data, AXES, pairs)]
  transfers between devices with their start and end apart: 12 -> 12, of which waited for: 6 -> 7; matrix products, arithmetic and copies ran while one was open for 0% -> 0% of each run, Pallas kernels for 5% -> 5%
where the time goes in v6:
time: 24.6 us; the launch traced here: 24.4 us
  starting transfers between devices  11.5 us (47%)
  waiting for transfers between devices  6.81 us (28%)
  Pallas kernels  4.4 us (18%)
  local copies, waits for them, and re-layouts  1.62 us (7%)
    ppermute x12, starting transfers between devices, send(): return lax.ppermute(data, AXES, pairs)  11.5 us
    ppermute x12, waiting for transfers between devices, send(): return lax.ppermute(data, AXES, pairs)  6.81 us
    pallas_call x1, Pallas kernels, correlate(): pl.pallas_call(kernel, out_shape=jax.ShapeDtypeStruct((half, 9, block, LA...  3.12 us
    unnamed x6, local copies, waits for them, and re-layouts  1.62 us
    pallas_call x1, Pallas kernels, first_half(): pl.pallas_call(kernel, out_shape=(jax.ShapeDtypeStruct((CHUNKS, groups, L...  1.14 us
  transfers between devices with their start and end apart: 12, of which 7 were waited for; matrix products, arithmetic and copies ran while one was open for 0% of the time, Pallas kernels for 5%

profile of v6, /device:TPU:0, one launch (start us, length us, event | category | flops | bytes accessed | tf_op | source)
XLA Modules:
  0.0 24.4 jit_solution(16753466797769468902)
XLA Ops:
  0.0 2.4 %collective-permute-start.2 = (bf16[32,1536]{1,0:T(8,128)(2,1)}, bf16[32,1536]{1,0:T(8,128)(2,1)S(1)}, u32[]{:S(2)}, u32[]{:S(2)}) collective-permute-start(bf16[32,1536]{1,0:T(8,128)(2,1)} %bitcast.2), channel_id=1, source_target_pairs={{0,24},{1,25},{2,16},{3,17},{4,8},{5,9},{6,0},{7,1},{8,26},{9,27},... | collective-permute-start | bytes 294920 | tf_op jit(solution)/shard_map/ppermute | solution.py:254
  2.4 0.0 copy-start.1
  2.4 0.9 %copy-done.1 = bf16[4,8,1536]{2,1,0:T(8,128)(2,1)S(1)} copy-done((bf16[4,8,1536]{2,1,0:T(8,128)(2,1)S(1)}, bf16[4,8,1536]{2,1,0:T(8,128)(2,1)}, u32[]{:S(2)}) %copy-start.1) | copy-done | bytes 98328
  3.4 1.6 %collective-permute-start = (bf16[16,1536]{1,0:T(8,128)(2,1)S(1)}, bf16[16,1536]{1,0:T(8,128)(2,1)S(1)}, u32[]{:S(2)}, u32[]{:S(2)}) collective-permute-start(bf16[16,1536]{1,0:T(8,128)(2,1)S(1)} %get-tuple-element.23), channel_id=1, source_target_pairs={{0,1},{1,0},{2,3},{3,2},{4,5},{5,4},{6,7},{7,6},{8,9},{9,8},{10,11... | collective-permute-start | bytes 147464 | tf_op jit(solution)/shard_map/ppermute | solution.py:254
  4.9 0.0 copy-start.2
  4.9 0.7 %copy-done.2 = s32[8,32]{1,0:T(8,128)S(1)} copy-done((s32[8,32]{1,0:T(8,128)S(1)}, s32[8,32]{1,0:T(8,128)}, u32[]{:S(2)}) %copy-start.2) | copy-done | bytes 1048
  5.6 0.1 shard_map.38
  5.7 2.2 %collective-permute-done = bf16[16,1536]{1,0:T(8,128)(2,1)S(1)} collective-permute-done((bf16[16,1536]{1,0:T(8,128)(2,1)S(1)}, bf16[16,1536]{1,0:T(8,128)(2,1)S(1)}, u32[]{:S(2)}, u32[]{:S(2)}) %collective-permute-start) | collective-permute-done | bytes 49184 | tf_op jit(solution)/shard_map/ppermute | solution.py:254
  7.9 0.0 copy-start
  7.9 2.3 %collective-permute-start.1 = (bf16[32,1536]{1,0:T(8,128)(2,1)S(1)}, bf16[32,1536]{1,0:T(8,128)(2,1)S(1)}, u32[]{:S(2)}, u32[]{:S(2)}) collective-permute-start(bf16[32,1536]{1,0:T(8,128)(2,1)S(1)} %constant_dynamic-update-slice_fusion.refs_0_), channel_id=1, source_target_pairs={{0,6},{1,7},{2,4},{3,5},{4,2},{5,3},{6,0},{7,1},{8,14},{9,15},{10,... | collective-permute-start | bytes 294920 | tf_op jit(solution)/shard_map/ppermute | solution.py:254
  10.2 0.0 collective-permute-done.2.refs_4_
  10.2 1.9 %collective-permute-start.9 = (bf16[32,1536]{1,0:T(8,128)(2,1)S(1)}, bf16[32,1536]{1,0:T(8,128)(2,1)S(1)}, u32[]{:S(2)}, u32[]{:S(2)}) collective-permute-start(bf16[32,1536]{1,0:T(8,128)(2,1)S(1)} %collective-permute-done.2.refs_4_), channel_id=1, source_target_pairs={{0,16},{1,17},{2,18},{3,19},{4,20},{5,21},{6,22},{7,23},{8,24},{9,... | collective-permute-start | bytes 294920 | tf_op jit(solution)/shard_map/ppermute | solution.py:254
  12.1 1.3 %collective-permute-start.6 = (bf16[32,1536]{1,0:T(8,128)(2,1)S(1)}, bf16[32,1536]{1,0:T(8,128)(2,1)S(1)}, u32[]{:S(2)}, u32[]{:S(2)}) collective-permute-start(bf16[32,1536]{1,0:T(8,128)(2,1)S(1)} %collective-permute-done.2.refs_4_), channel_id=1, source_target_pairs={{0,17},{1,16},{2,19},{3,18},{4,21},{5,20},{6,23},{7,22},{8,25},{9,... | collective-permute-start | bytes 294920 | tf_op jit(solution)/shard_map/ppermute | solution.py:254
  13.4 0.3 %collective-permute-start.5 = (bf16[32,1536]{1,0:T(8,128)(2,1)S(1)}, bf16[32,1536]{1,0:T(8,128)(2,1)S(1)}, u32[]{:S(2)}, u32[]{:S(2)}) collective-permute-start(bf16[32,1536]{1,0:T(8,128)(2,1)S(1)} %collective-permute-done.2.refs_4_), channel_id=1, source_target_pairs={{0,1},{1,0},{2,3},{3,2},{4,5},{5,4},{6,7},{7,6},{8,9},{9,8},{10,11... | collective-permute-start | bytes 294920 | tf_op jit(solution)/shard_map/ppermute | solution.py:254
  13.7 0.0 collective-permute-start.3
  13.7 1.1 %collective-permute-done.1.refs_1_ = bf16[32,1536]{1,0:T(8,128)(2,1)S(1)} collective-permute-done((bf16[32,1536]{1,0:T(8,128)(2,1)S(1)}, bf16[32,1536]{1,0:T(8,128)(2,1)S(1)}, u32[]{:S(2)}, u32[]{:S(2)}) %collective-permute-start.1) | collective-permute-done | bytes 98336 | tf_op jit(solution)/shard_map/ppermute | solution.py:254
  14.8 1.5 %collective-permute-start.4 = (bf16[32,1536]{1,0:T(8,128)(2,1)S(1)}, bf16[32,1536]{1,0:T(8,128)(2,1)S(1)}, u32[]{:S(2)}, u32[]{:S(2)}) collective-permute-start(bf16[32,1536]{1,0:T(8,128)(2,1)S(1)} %collective-permute-done.1.refs_1_), channel_id=1, source_target_pairs={{0,2},{1,3},{2,0},{3,1},{4,6},{5,7},{6,4},{7,5},{8,10},{9,11},{10,... | collective-permute-start | bytes 294920 | tf_op jit(solution)/shard_map/ppermute | solution.py:254
  16.3 0.0 collective-permute-done.9.refs_5_
  16.3 0.0 collective-permute-start.10
  16.3 1.4 %collective-permute-done.6.refs_5_ = bf16[32,1536]{1,0:T(8,128)(2,1)S(1)} collective-permute-done((bf16[32,1536]{1,0:T(8,128)(2,1)S(1)}, bf16[32,1536]{1,0:T(8,128)(2,1)S(1)}, u32[]{:S(2)}, u32[]{:S(2)}) %collective-permute-start.6) | collective-permute-done | bytes 98336 | tf_op jit(solution)/shard_map/ppermute | solution.py:254
  17.7 0.0 collective-permute-start.11
  17.7 0.3 %collective-permute-done.5.refs_4_ = bf16[32,1536]{1,0:T(8,128)(2,1)S(1)} collective-permute-done((bf16[32,1536]{1,0:T(8,128)(2,1)S(1)}, bf16[32,1536]{1,0:T(8,128)(2,1)S(1)}, u32[]{:S(2)}, u32[]{:S(2)}) %collective-permute-start.5) | collective-permute-done | bytes 98336 | tf_op jit(solution)/shard_map/ppermute | solution.py:254
  18.0 0.3 %collective-permute-start.7 = (bf16[32,1536]{1,0:T(8,128)(2,1)S(1)}, bf16[32,1536]{1,0:T(8,128)(2,1)S(1)}, u32[]{:S(2)}, u32[]{:S(2)}) collective-permute-start(bf16[32,1536]{1,0:T(8,128)(2,1)S(1)} %collective-permute-done.5.refs_4_), channel_id=1, source_target_pairs={{0,8},{1,9},{2,10},{3,11},{4,12},{5,13},{6,14},{7,15},{8,0},{9,1},... | collective-permute-start | bytes 294920 | tf_op jit(solution)/shard_map/ppermute | solution.py:254
  18.2 0.7 %collective-permute-done.3.refs_2_ = bf16[32,1536]{1,0:T(8,128)(2,1)S(1)} collective-permute-done((bf16[32,1536]{1,0:T(8,128)(2,1)S(1)}, bf16[32,1536]{1,0:T(8,128)(2,1)S(1)}, u32[]{:S(2)}, u32[]{:S(2)}) %collective-permute-start.3) | collective-permute-done | bytes 98336 | tf_op jit(solution)/shard_map/ppermute | solution.py:254
  18.9 1.1 %collective-permute-done.4.refs_3_ = bf16[32,1536]{1,0:T(8,128)(2,1)S(1)} collective-permute-done((bf16[32,1536]{1,0:T(8,128)(2,1)S(1)}, bf16[32,1536]{1,0:T(8,128)(2,1)S(1)}, u32[]{:S(2)}, u32[]{:S(2)}) %collective-permute-start.4) | collective-permute-done | bytes 98336 | tf_op jit(solution)/shard_map/ppermute | solution.py:254
  19.9 0.0 collective-permute-start.8
  19.9 0.0 collective-permute-done.10.refs_6_
  20.0 0.0 collective-permute-done.11.refs_7_
  20.0 1.1 %shard_map.39 = (f32[8,288,128]{2,1,0:T(8,128)S(1)}, f32[8,288,128]{2,1,0:T(8,128)S(1)}) custom-call(bf16[32,1536]{1,0:T(8,128)(2,1)S(1)} %constant_dynamic-update-slice_fusion.refs_0_, bf16[32,1536]{1,0:T(8,128)(2,1)S(1)} %collective-permute-done.1.refs_1_, bf16[32,1536]{1,0:T(8,128)(2,1)S(1)} %collective-permute-done.3.refs_2_, ...), custom_call_target="tpu_custom_call" | custom-call | flops 1000000000 | bytes 1048576 | tf_op jit(solution)/shard_map/pallas_call | solution.py:113
  21.1 0.0 collective-permute-done.7.refs_6_
  21.1 0.1 collective-permute-done.8.refs_7_
  21.2 0.0 copy-done
  21.3 3.1 %shard_map.40 = f32[4,9,8,768]{3,2,1,0:T(8,128)} custom-call(bf16[32,1536]{1,0:T(8,128)(2,1)S(1)} %constant_dynamic-update-slice_fusion.refs_0_, bf16[32,1536]{1,0:T(8,128)(2,1)S(1)} %collective-permute-done.1.refs_1_, bf16[32,1536]{1,0:T(8,128)(2,1)S(1)} %collective-permute-done.3.refs_2_, bf16[32,1536]{1,0:T(8,128)(2,1)S(1)} %collective-permute-done.4.refs_3_, ...), custom_call_target="tpu_custom_call" | custom-call | tf_op jit(solution)/shard_map/pallas_call | solution.py:163
  (2 shorter events, 0.0 us)
Async XLA Ops:
  0.0 10.2 %collective-permute-start.2 = (bf16[32,1536]{1,0:T(8,128)(2,1)}, bf16[32,1536]{1,0:T(8,128)(2,1)S(1)}, u32[]{:S(2)}, u32[]{:S(2)}) collective-permute-start(bf16[32,1536]{1,0:T(8,128)(2,1)} %bitcast.2), channel_id=1, source_target_pairs={{0,24},{1,25},{2,16},{3,17},{4,8},{5,9},{6,0},{7,1},{8,26},{9,27},... | collective-permute-start | bytes 294920 | tf_op jit(solution)/shard_map/ppermute | solution.py:254
  2.4 0.9 %copy-start.1 = (bf16[4,8,1536]{2,1,0:T(8,128)(2,1)S(1)}, bf16[4,8,1536]{2,1,0:T(8,128)(2,1)}, u32[]{:S(2)}) copy-start(bf16[4,8,1536]{2,1,0:T(8,128)(2,1)} %spectra_ref.1) | copy-start | bytes 294916
  3.4 4.5 %collective-permute-start = (bf16[16,1536]{1,0:T(8,128)(2,1)S(1)}, bf16[16,1536]{1,0:T(8,128)(2,1)S(1)}, u32[]{:S(2)}, u32[]{:S(2)}) collective-permute-start(bf16[16,1536]{1,0:T(8,128)(2,1)S(1)} %get-tuple-element.23), channel_id=1, source_target_pairs={{0,1},{1,0},{2,3},{3,2},{4,5},{5,4},{6,7},{7,6},{8,9},{9,8},{10,11... | collective-permute-start | bytes 147464 | tf_op jit(solution)/shard_map/ppermute | solution.py:254
  4.9 0.7 %copy-start.2 = (s32[8,32]{1,0:T(8,128)S(1)}, s32[8,32]{1,0:T(8,128)}, u32[]{:S(2)}) copy-start(s32[8,32]{1,0:T(8,128)} %usable_ref.1) | copy-start | bytes 3076
  7.9 13.3 %copy-start = (bf16[2048,768]{1,0:T(8,128)(2,1)S(1)}, bf16[2048,768]{1,0:T(8,128)(2,1)}, u32[]{:S(2)}) copy-start(bf16[2048,768]{1,0:T(8,128)(2,1)} %constant.6.clone.refs_13_) | copy-start | bytes 9437188
  7.9 6.9 %collective-permute-start.1 = (bf16[32,1536]{1,0:T(8,128)(2,1)S(1)}, bf16[32,1536]{1,0:T(8,128)(2,1)S(1)}, u32[]{:S(2)}, u32[]{:S(2)}) collective-permute-start(bf16[32,1536]{1,0:T(8,128)(2,1)S(1)} %constant_dynamic-update-slice_fusion.refs_0_), channel_id=1, source_target_pairs={{0,6},{1,7},{2,4},{3,5},{4,2},{5,3},{6,0},{7,1},{8,14},{9,15},{10,... | collective-permute-start | bytes 294920 | tf_op jit(solution)/shard_map/ppermute | solution.py:254
  10.2 6.1 %collective-permute-start.9 = (bf16[32,1536]{1,0:T(8,128)(2,1)S(1)}, bf16[32,1536]{1,0:T(8,128)(2,1)S(1)}, u32[]{:S(2)}, u32[]{:S(2)}) collective-permute-start(bf16[32,1536]{1,0:T(8,128)(2,1)S(1)} %collective-permute-done.2.refs_4_), channel_id=1, source_target_pairs={{0,16},{1,17},{2,18},{3,19},{4,20},{5,21},{6,22},{7,23},{8,24},{9,... | collective-permute-start | bytes 294920 | tf_op jit(solution)/shard_map/ppermute | solution.py:254
  12.1 5.6 %collective-permute-start.6 = (bf16[32,1536]{1,0:T(8,128)(2,1)S(1)}, bf16[32,1536]{1,0:T(8,128)(2,1)S(1)}, u32[]{:S(2)}, u32[]{:S(2)}) collective-permute-start(bf16[32,1536]{1,0:T(8,128)(2,1)S(1)} %collective-permute-done.2.refs_4_), channel_id=1, source_target_pairs={{0,17},{1,16},{2,19},{3,18},{4,21},{5,20},{6,23},{7,22},{8,25},{9,... | collective-permute-start | bytes 294920 | tf_op jit(solution)/shard_map/ppermute | solution.py:254
  13.4 4.6 %collective-permute-start.5 = (bf16[32,1536]{1,0:T(8,128)(2,1)S(1)}, bf16[32,1536]{1,0:T(8,128)(2,1)S(1)}, u32[]{:S(2)}, u32[]{:S(2)}) collective-permute-start(bf16[32,1536]{1,0:T(8,128)(2,1)S(1)} %collective-permute-done.2.refs_4_), channel_id=1, source_target_pairs={{0,1},{1,0},{2,3},{3,2},{4,5},{5,4},{6,7},{7,6},{8,9},{9,8},{10,11... | collective-permute-start | bytes 294920 | tf_op jit(solution)/shard_map/ppermute | solution.py:254
  13.7 5.2 %collective-permute-start.3 = (bf16[32,1536]{1,0:T(8,128)(2,1)S(1)}, bf16[32,1536]{1,0:T(8,128)(2,1)S(1)}, u32[]{:S(2)}, u32[]{:S(2)}) collective-permute-start(bf16[32,1536]{1,0:T(8,128)(2,1)S(1)} %constant_dynamic-update-slice_fusion.refs_0_), channel_id=1, source_target_pairs={{0,2},{1,3},{2,0},{3,1},{4,6},{5,7},{6,4},{7,5},{8,10},{9,11},{10,... | collective-permute-start | bytes 294920 | tf_op jit(solution)/shard_map/ppermute | solution.py:254
  14.8 5.2 %collective-permute-start.4 = (bf16[32,1536]{1,0:T(8,128)(2,1)S(1)}, bf16[32,1536]{1,0:T(8,128)(2,1)S(1)}, u32[]{:S(2)}, u32[]{:S(2)}) collective-permute-start(bf16[32,1536]{1,0:T(8,128)(2,1)S(1)} %collective-permute-done.1.refs_1_), channel_id=1, source_target_pairs={{0,2},{1,3},{2,0},{3,1},{4,6},{5,7},{6,4},{7,5},{8,10},{9,11},{10,... | collective-permute-start | bytes 294920 | tf_op jit(solution)/shard_map/ppermute | solution.py:254
  16.3 3.7 %collective-permute-start.10 = (bf16[32,1536]{1,0:T(8,128)(2,1)S(1)}, bf16[32,1536]{1,0:T(8,128)(2,1)S(1)}, u32[]{:S(2)}, u32[]{:S(2)}) collective-permute-start(bf16[32,1536]{1,0:T(8,128)(2,1)S(1)} %collective-permute-done.2.refs_4_), channel_id=1, source_target_pairs={{0,8},{1,9},{2,10},{3,11},{4,12},{5,13},{6,14},{7,15},{8,0},{9,1},... | collective-permute-start | bytes 294920 | tf_op jit(solution)/shard_map/ppermute | solution.py:254
  17.7 2.2 %collective-permute-start.11 = (bf16[32,1536]{1,0:T(8,128)(2,1)S(1)}, bf16[32,1536]{1,0:T(8,128)(2,1)S(1)}, u32[]{:S(2)}, u32[]{:S(2)}) collective-permute-start(bf16[32,1536]{1,0:T(8,128)(2,1)S(1)} %collective-permute-done.9.refs_5_), channel_id=1, source_target_pairs={{0,8},{1,9},{2,10},{3,11},{4,12},{5,13},{6,14},{7,15},{8,0},{9,1},... | collective-permute-start | bytes 294920 | tf_op jit(solution)/shard_map/ppermute | solution.py:254
  18.0 3.1 %collective-permute-start.7 = (bf16[32,1536]{1,0:T(8,128)(2,1)S(1)}, bf16[32,1536]{1,0:T(8,128)(2,1)S(1)}, u32[]{:S(2)}, u32[]{:S(2)}) collective-permute-start(bf16[32,1536]{1,0:T(8,128)(2,1)S(1)} %collective-permute-done.5.refs_4_), channel_id=1, source_target_pairs={{0,8},{1,9},{2,10},{3,11},{4,12},{5,13},{6,14},{7,15},{8,0},{9,1},... | collective-permute-start | bytes 294920 | tf_op jit(solution)/shard_map/ppermute | solution.py:254
  19.9 1.3 %collective-permute-start.8 = (bf16[32,1536]{1,0:T(8,128)(2,1)S(1)}, bf16[32,1536]{1,0:T(8,128)(2,1)S(1)}, u32[]{:S(2)}, u32[]{:S(2)}) collective-permute-start(bf16[32,1536]{1,0:T(8,128)(2,1)S(1)} %collective-permute-done.6.refs_5_), channel_id=1, source_target_pairs={{0,8},{1,9},{2,10},{3,11},{4,12},{5,13},{6,14},{7,15},{8,0},{9,1},... | collective-permute-start | bytes 294920 | tf_op jit(solution)/shard_map/ppermute | solution.py:254

commit v7 on v6

--- a/solution.py
+++ b/solution.py
@@ -217,12 +217,12 @@
     span, block, shard = spectra.shape
 
     def kernel(spectra_ref, theirs_ref, mine_ref):
-        low = [spectra_ref[w, :half] for w in range(span)]
-        high = [spectra_ref[w, half:] for w in range(span)]
+        data = spectra_ref[...].astype(jnp.float32)
+        low = jnp.concatenate([data[w * block : w * block + half] for w in range(span)], 0)
+        high = jnp.concatenate([data[w * block + half : (w + 1) * block] for w in range(span)], 0)
         first = lax.axis_index("win") == 0
-        low, high = jnp.concatenate(low, 0), jnp.concatenate(high, 0)
-        theirs_ref[...] = jnp.where(first, high, low)
-        mine_ref[: span * half] = jnp.where(first, low, high)
+        theirs_ref[...] = jnp.where(first, high, low).astype(jnp.bfloat16)
+        mine_ref[: span * half] = jnp.where(first, low, high).astype(jnp.bfloat16)
         mine_ref[span * half :] = jnp.zeros((span * half, shard), jnp.bfloat16)
 
     in_vmem = pl.BlockSpec(memory_space=pltpu.VMEM)
@@ -235,7 +235,7 @@
         in_specs=[in_vmem],
         out_specs=(in_vmem, in_vmem),
         compiler_params=pltpu.CompilerParams(vmem_limit_bytes=4 * 1024 * 1024),
-    )(spectra)
+    )(spectra.reshape(span * block, shard))
 
 
 def body(spectra, usable):

time: 24.6 us -> 24.6 us (level)
  no operation moved by 1% of the time
where the time goes in v7:
time: 24.6 us; the launch traced here: 24.4 us
  starting transfers between devices  11.5 us (47%)
  waiting for transfers between devices  6.81 us (28%)
  Pallas kernels  4.39 us (18%)
  local copies, waits for them, and re-layouts  1.62 us (7%)
    ppermute x12, starting transfers between devices, send(): return lax.ppermute(data, AXES, pairs)  11.5 us
    ppermute x12, waiting for transfers between devices, send(): return lax.ppermute(data, AXES, pairs)  6.81 us
    pallas_call x1, Pallas kernels, correlate(): pl.pallas_call(kernel, out_shape=jax.ShapeDtypeStruct((half, 9, block, LA...  3.12 us
    unnamed x6, local copies, waits for them, and re-layouts  1.62 us
    pallas_call x1, Pallas kernels, first_half(): pl.pallas_call(kernel, out_shape=(jax.ShapeDtypeStruct((CHUNKS, groups, L...  1.14 us
  transfers between devices with their start and end apart: 12, of which 7 were waited for; matrix products, arithmetic and copies ran while one was open for 0% of the time, Pallas kernels for 5%

profile of v7, /device:TPU:0, one launch (start us, length us, event | category | flops | bytes accessed | tf_op | source)
XLA Modules:
  0.0 24.4 jit_solution(1549722447742616667)
XLA Ops:
  0.0 2.4 %collective-permute-start.2 = (bf16[32,1536]{1,0:T(8,128)(2,1)}, bf16[32,1536]{1,0:T(8,128)(2,1)S(1)}, u32[]{:S(2)}, u32[]{:S(2)}) collective-permute-start(bf16[32,1536]{1,0:T(8,128)(2,1)} %bitcast.2), channel_id=1, source_target_pairs={{0,24},{1,25},{2,16},{3,17},{4,8},{5,9},{6,0},{7,1},{8,26},{9,27},... | collective-permute-start | bytes 294920 | tf_op jit(solution)/shard_map/ppermute | solution.py:254
  2.4 0.0 copy-start.1
  2.4 0.9 %copy-done.1 = bf16[4,8,1536]{2,1,0:T(8,128)(2,1)S(1)} copy-done((bf16[4,8,1536]{2,1,0:T(8,128)(2,1)S(1)}, bf16[4,8,1536]{2,1,0:T(8,128)(2,1)}, u32[]{:S(2)}) %copy-start.1) | copy-done | bytes 98328
  3.4 1.6 %collective-permute-start = (bf16[16,1536]{1,0:T(8,128)(2,1)S(1)}, bf16[16,1536]{1,0:T(8,128)(2,1)S(1)}, u32[]{:S(2)}, u32[]{:S(2)}) collective-permute-start(bf16[16,1536]{1,0:T(8,128)(2,1)S(1)} %get-tuple-element.23), channel_id=1, source_target_pairs={{0,1},{1,0},{2,3},{3,2},{4,5},{5,4},{6,7},{7,6},{8,9},{9,8},{10,11... | collective-permute-start | bytes 147464 | tf_op jit(solution)/shard_map/ppermute | solution.py:254
  4.9 0.0 copy-start.2
  4.9 0.7 %copy-done.2 = s32[8,32]{1,0:T(8,128)S(1)} copy-done((s32[8,32]{1,0:T(8,128)S(1)}, s32[8,32]{1,0:T(8,128)}, u32[]{:S(2)}) %copy-start.2) | copy-done | bytes 1048
  5.6 0.1 shard_map.38
  5.7 2.2 %collective-permute-done = bf16[16,1536]{1,0:T(8,128)(2,1)S(1)} collective-permute-done((bf16[16,1536]{1,0:T(8,128)(2,1)S(1)}, bf16[16,1536]{1,0:T(8,128)(2,1)S(1)}, u32[]{:S(2)}, u32[]{:S(2)}) %collective-permute-start) | collective-permute-done | bytes 49184 | tf_op jit(solution)/shard_map/ppermute | solution.py:254
  7.9 0.0 copy-start
  7.9 2.3 %collective-permute-start.1 = (bf16[32,1536]{1,0:T(8,128)(2,1)S(1)}, bf16[32,1536]{1,0:T(8,128)(2,1)S(1)}, u32[]{:S(2)}, u32[]{:S(2)}) collective-permute-start(bf16[32,1536]{1,0:T(8,128)(2,1)S(1)} %constant_dynamic-update-slice_fusion.refs_0_), channel_id=1, source_target_pairs={{0,6},{1,7},{2,4},{3,5},{4,2},{5,3},{6,0},{7,1},{8,14},{9,15},{10,... | collective-permute-start | bytes 294920 | tf_op jit(solution)/shard_map/ppermute | solution.py:254
  10.2 0.0 collective-permute-done.2.refs_4_
  10.2 1.9 %collective-permute-start.9 = (bf16[32,1536]{1,0:T(8,128)(2,1)S(1)}, bf16[32,1536]{1,0:T(8,128)(2,1)S(1)}, u32[]{:S(2)}, u32[]{:S(2)}) collective-permute-start(bf16[32,1536]{1,0:T(8,128)(2,1)S(1)} %collective-permute-done.2.refs_4_), channel_id=1, source_target_pairs={{0,16},{1,17},{2,18},{3,19},{4,20},{5,21},{6,22},{7,23},{8,24},{9,... | collective-permute-start | bytes 294920 | tf_op jit(solution)/shard_map/ppermute | solution.py:254
  12.1 1.3 %collective-permute-start.6 = (bf16[32,1536]{1,0:T(8,128)(2,1)S(1)}, bf16[32,1536]{1,0:T(8,128)(2,1)S(1)}, u32[]{:S(2)}, u32[]{:S(2)}) collective-permute-start(bf16[32,1536]{1,0:T(8,128)(2,1)S(1)} %collective-permute-done.2.refs_4_), channel_id=1, source_target_pairs={{0,17},{1,16},{2,19},{3,18},{4,21},{5,20},{6,23},{7,22},{8,25},{9,... | collective-permute-start | bytes 294920 | tf_op jit(solution)/shard_map/ppermute | solution.py:254
  13.4 0.3 %collective-permute-start.5 = (bf16[32,1536]{1,0:T(8,128)(2,1)S(1)}, bf16[32,1536]{1,0:T(8,128)(2,1)S(1)}, u32[]{:S(2)}, u32[]{:S(2)}) collective-permute-start(bf16[32,1536]{1,0:T(8,128)(2,1)S(1)} %collective-permute-done.2.refs_4_), channel_id=1, source_target_pairs={{0,1},{1,0},{2,3},{3,2},{4,5},{5,4},{6,7},{7,6},{8,9},{9,8},{10,11... | collective-permute-start | bytes 294920 | tf_op jit(solution)/shard_map/ppermute | solution.py:254
  13.7 0.0 collective-permute-start.3
  13.7 1.1 %collective-permute-done.1.refs_1_ = bf16[32,1536]{1,0:T(8,128)(2,1)S(1)} collective-permute-done((bf16[32,1536]{1,0:T(8,128)(2,1)S(1)}, bf16[32,1536]{1,0:T(8,128)(2,1)S(1)}, u32[]{:S(2)}, u32[]{:S(2)}) %collective-permute-start.1) | collective-permute-done | bytes 98336 | tf_op jit(solution)/shard_map/ppermute | solution.py:254
  14.8 1.5 %collective-permute-start.4 = (bf16[32,1536]{1,0:T(8,128)(2,1)S(1)}, bf16[32,1536]{1,0:T(8,128)(2,1)S(1)}, u32[]{:S(2)}, u32[]{:S(2)}) collective-permute-start(bf16[32,1536]{1,0:T(8,128)(2,1)S(1)} %collective-permute-done.1.refs_1_), channel_id=1, source_target_pairs={{0,2},{1,3},{2,0},{3,1},{4,6},{5,7},{6,4},{7,5},{8,10},{9,11},{10,... | collective-permute-start | bytes 294920 | tf_op jit(solution)/shard_map/ppermute | solution.py:254
  16.3 0.0 collective-permute-done.9.refs_5_
  16.3 0.0 collective-permute-start.10
  16.3 1.4 %collective-permute-done.6.refs_5_ = bf16[32,1536]{1,0:T(8,128)(2,1)S(1)} collective-permute-done((bf16[32,1536]{1,0:T(8,128)(2,1)S(1)}, bf16[32,1536]{1,0:T(8,128)(2,1)S(1)}, u32[]{:S(2)}, u32[]{:S(2)}) %collective-permute-start.6) | collective-permute-done | bytes 98336 | tf_op jit(solution)/shard_map/ppermute | solution.py:254
  17.7 0.0 collective-permute-start.11
  17.7 0.3 %collective-permute-done.5.refs_4_ = bf16[32,1536]{1,0:T(8,128)(2,1)S(1)} collective-permute-done((bf16[32,1536]{1,0:T(8,128)(2,1)S(1)}, bf16[32,1536]{1,0:T(8,128)(2,1)S(1)}, u32[]{:S(2)}, u32[]{:S(2)}) %collective-permute-start.5) | collective-permute-done | bytes 98336 | tf_op jit(solution)/shard_map/ppermute | solution.py:254
  18.0 0.3 %collective-permute-start.7 = (bf16[32,1536]{1,0:T(8,128)(2,1)S(1)}, bf16[32,1536]{1,0:T(8,128)(2,1)S(1)}, u32[]{:S(2)}, u32[]{:S(2)}) collective-permute-start(bf16[32,1536]{1,0:T(8,128)(2,1)S(1)} %collective-permute-done.5.refs_4_), channel_id=1, source_target_pairs={{0,8},{1,9},{2,10},{3,11},{4,12},{5,13},{6,14},{7,15},{8,0},{9,1},... | collective-permute-start | bytes 294920 | tf_op jit(solution)/shard_map/ppermute | solution.py:254
  18.2 0.7 %collective-permute-done.3.refs_2_ = bf16[32,1536]{1,0:T(8,128)(2,1)S(1)} collective-permute-done((bf16[32,1536]{1,0:T(8,128)(2,1)S(1)}, bf16[32,1536]{1,0:T(8,128)(2,1)S(1)}, u32[]{:S(2)}, u32[]{:S(2)}) %collective-permute-start.3) | collective-permute-done | bytes 98336 | tf_op jit(solution)/shard_map/ppermute | solution.py:254
  18.9 1.1 %collective-permute-done.4.refs_3_ = bf16[32,1536]{1,0:T(8,128)(2,1)S(1)} collective-permute-done((bf16[32,1536]{1,0:T(8,128)(2,1)S(1)}, bf16[32,1536]{1,0:T(8,128)(2,1)S(1)}, u32[]{:S(2)}, u32[]{:S(2)}) %collective-permute-start.4) | collective-permute-done | bytes 98336 | tf_op jit(solution)/shard_map/ppermute | solution.py:254
  19.9 0.0 collective-permute-start.8
  19.9 0.0 collective-permute-done.10.refs_6_
  19.9 0.0 collective-permute-done.11.refs_7_
  19.9 1.1 %shard_map.39 = (f32[8,288,128]{2,1,0:T(8,128)S(1)}, f32[8,288,128]{2,1,0:T(8,128)S(1)}) custom-call(bf16[32,1536]{1,0:T(8,128)(2,1)S(1)} %constant_dynamic-update-slice_fusion.refs_0_, bf16[32,1536]{1,0:T(8,128)(2,1)S(1)} %collective-permute-done.1.refs_1_, bf16[32,1536]{1,0:T(8,128)(2,1)S(1)} %collective-permute-done.3.refs_2_, ...), custom_call_target="tpu_custom_call" | custom-call | flops 1000000000 | bytes 1048576 | tf_op jit(solution)/shard_map/pallas_call | solution.py:113
  21.1 0.0 collective-permute-done.7.refs_6_
  21.1 0.1 collective-permute-done.8.refs_7_
  21.2 0.0 copy-done
  21.2 3.1 %shard_map.40 = f32[4,9,8,768]{3,2,1,0:T(8,128)} custom-call(bf16[32,1536]{1,0:T(8,128)(2,1)S(1)} %constant_dynamic-update-slice_fusion.refs_0_, bf16[32,1536]{1,0:T(8,128)(2,1)S(1)} %collective-permute-done.1.refs_1_, bf16[32,1536]{1,0:T(8,128)(2,1)S(1)} %collective-permute-done.3.refs_2_, bf16[32,1536]{1,0:T(8,128)(2,1)S(1)} %collective-permute-done.4.refs_3_, ...), custom_call_target="tpu_custom_call" | custom-call | tf_op jit(solution)/shard_map/pallas_call | solution.py:163
  (2 shorter events, 0.0 us)
Async XLA Ops:
  0.0 10.2 %collective-permute-start.2 = (bf16[32,1536]{1,0:T(8,128)(2,1)}, bf16[32,1536]{1,0:T(8,128)(2,1)S(1)}, u32[]{:S(2)}, u32[]{:S(2)}) collective-permute-start(bf16[32,1536]{1,0:T(8,128)(2,1)} %bitcast.2), channel_id=1, source_target_pairs={{0,24},{1,25},{2,16},{3,17},{4,8},{5,9},{6,0},{7,1},{8,26},{9,27},... | collective-permute-start | bytes 294920 | tf_op jit(solution)/shard_map/ppermute | solution.py:254
  2.4 0.9 %copy-start.1 = (bf16[4,8,1536]{2,1,0:T(8,128)(2,1)S(1)}, bf16[4,8,1536]{2,1,0:T(8,128)(2,1)}, u32[]{:S(2)}) copy-start(bf16[4,8,1536]{2,1,0:T(8,128)(2,1)} %param.3) | copy-start | bytes 294916
  3.4 4.5 %collective-permute-start = (bf16[16,1536]{1,0:T(8,128)(2,1)S(1)}, bf16[16,1536]{1,0:T(8,128)(2,1)S(1)}, u32[]{:S(2)}, u32[]{:S(2)}) collective-permute-start(bf16[16,1536]{1,0:T(8,128)(2,1)S(1)} %get-tuple-element.23), channel_id=1, source_target_pairs={{0,1},{1,0},{2,3},{3,2},{4,5},{5,4},{6,7},{7,6},{8,9},{9,8},{10,11... | collective-permute-start | bytes 147464 | tf_op jit(solution)/shard_map/ppermute | solution.py:254
  4.9 0.7 %copy-start.2 = (s32[8,32]{1,0:T(8,128)S(1)}, s32[8,32]{1,0:T(8,128)}, u32[]{:S(2)}) copy-start(s32[8,32]{1,0:T(8,128)} %usable_ref.1) | copy-start | bytes 3076
  7.9 13.3 %copy-start = (bf16[2048,768]{1,0:T(8,128)(2,1)S(1)}, bf16[2048,768]{1,0:T(8,128)(2,1)}, u32[]{:S(2)}) copy-start(bf16[2048,768]{1,0:T(8,128)(2,1)} %constant.6.clone.refs_13_) | copy-start | bytes 9437188
  7.9 6.9 %collective-permute-start.1 = (bf16[32,1536]{1,0:T(8,128)(2,1)S(1)}, bf16[32,1536]{1,0:T(8,128)(2,1)S(1)}, u32[]{:S(2)}, u32[]{:S(2)}) collective-permute-start(bf16[32,1536]{1,0:T(8,128)(2,1)S(1)} %constant_dynamic-update-slice_fusion.refs_0_), channel_id=1, source_target_pairs={{0,6},{1,7},{2,4},{3,5},{4,2},{5,3},{6,0},{7,1},{8,14},{9,15},{10,... | collective-permute-start | bytes 294920 | tf_op jit(solution)/shard_map/ppermute | solution.py:254
  10.2 6.1 %collective-permute-start.9 = (bf16[32,1536]{1,0:T(8,128)(2,1)S(1)}, bf16[32,1536]{1,0:T(8,128)(2,1)S(1)}, u32[]{:S(2)}, u32[]{:S(2)}) collective-permute-start(bf16[32,1536]{1,0:T(8,128)(2,1)S(1)} %collective-permute-done.2.refs_4_), channel_id=1, source_target_pairs={{0,16},{1,17},{2,18},{3,19},{4,20},{5,21},{6,22},{7,23},{8,24},{9,... | collective-permute-start | bytes 294920 | tf_op jit(solution)/shard_map/ppermute | solution.py:254
  12.1 5.6 %collective-permute-start.6 = (bf16[32,1536]{1,0:T(8,128)(2,1)S(1)}, bf16[32,1536]{1,0:T(8,128)(2,1)S(1)}, u32[]{:S(2)}, u32[]{:S(2)}) collective-permute-start(bf16[32,1536]{1,0:T(8,128)(2,1)S(1)} %collective-permute-done.2.refs_4_), channel_id=1, source_target_pairs={{0,17},{1,16},{2,19},{3,18},{4,21},{5,20},{6,23},{7,22},{8,25},{9,... | collective-permute-start | bytes 294920 | tf_op jit(solution)/shard_map/ppermute | solution.py:254
  13.4 4.6 %collective-permute-start.5 = (bf16[32,1536]{1,0:T(8,128)(2,1)S(1)}, bf16[32,1536]{1,0:T(8,128)(2,1)S(1)}, u32[]{:S(2)}, u32[]{:S(2)}) collective-permute-start(bf16[32,1536]{1,0:T(8,128)(2,1)S(1)} %collective-permute-done.2.refs_4_), channel_id=1, source_target_pairs={{0,1},{1,0},{2,3},{3,2},{4,5},{5,4},{6,7},{7,6},{8,9},{9,8},{10,11... | collective-permute-start | bytes 294920 | tf_op jit(solution)/shard_map/ppermute | solution.py:254
  13.7 5.2 %collective-permute-start.3 = (bf16[32,1536]{1,0:T(8,128)(2,1)S(1)}, bf16[32,1536]{1,0:T(8,128)(2,1)S(1)}, u32[]{:S(2)}, u32[]{:S(2)}) collective-permute-start(bf16[32,1536]{1,0:T(8,128)(2,1)S(1)} %constant_dynamic-update-slice_fusion.refs_0_), channel_id=1, source_target_pairs={{0,2},{1,3},{2,0},{3,1},{4,6},{5,7},{6,4},{7,5},{8,10},{9,11},{10,... | collective-permute-start | bytes 294920 | tf_op jit(solution)/shard_map/ppermute | solution.py:254
  14.8 5.2 %collective-permute-start.4 = (bf16[32,1536]{1,0:T(8,128)(2,1)S(1)}, bf16[32,1536]{1,0:T(8,128)(2,1)S(1)}, u32[]{:S(2)}, u32[]{:S(2)}) collective-permute-start(bf16[32,1536]{1,0:T(8,128)(2,1)S(1)} %collective-permute-done.1.refs_1_), channel_id=1, source_target_pairs={{0,2},{1,3},{2,0},{3,1},{4,6},{5,7},{6,4},{7,5},{8,10},{9,11},{10,... | collective-permute-start | bytes 294920 | tf_op jit(solution)/shard_map/ppermute | solution.py:254
  16.3 3.7 %collective-permute-start.10 = (bf16[32,1536]{1,0:T(8,128)(2,1)S(1)}, bf16[32,1536]{1,0:T(8,128)(2,1)S(1)}, u32[]{:S(2)}, u32[]{:S(2)}) collective-permute-start(bf16[32,1536]{1,0:T(8,128)(2,1)S(1)} %collective-permute-done.2.refs_4_), channel_id=1, source_target_pairs={{0,8},{1,9},{2,10},{3,11},{4,12},{5,13},{6,14},{7,15},{8,0},{9,1},... | collective-permute-start | bytes 294920 | tf_op jit(solution)/shard_map/ppermute | solution.py:254
  17.7 2.2 %collective-permute-start.11 = (bf16[32,1536]{1,0:T(8,128)(2,1)S(1)}, bf16[32,1536]{1,0:T(8,128)(2,1)S(1)}, u32[]{:S(2)}, u32[]{:S(2)}) collective-permute-start(bf16[32,1536]{1,0:T(8,128)(2,1)S(1)} %collective-permute-done.9.refs_5_), channel_id=1, source_target_pairs={{0,8},{1,9},{2,10},{3,11},{4,12},{5,13},{6,14},{7,15},{8,0},{9,1},... | collective-permute-start | bytes 294920 | tf_op jit(solution)/shard_map/ppermute | solution.py:254
  18.0 3.1 %collective-permute-start.7 = (bf16[32,1536]{1,0:T(8,128)(2,1)S(1)}, bf16[32,1536]{1,0:T(8,128)(2,1)S(1)}, u32[]{:S(2)}, u32[]{:S(2)}) collective-permute-start(bf16[32,1536]{1,0:T(8,128)(2,1)S(1)} %collective-permute-done.5.refs_4_), channel_id=1, source_target_pairs={{0,8},{1,9},{2,10},{3,11},{4,12},{5,13},{6,14},{7,15},{8,0},{9,1},... | collective-permute-start | bytes 294920 | tf_op jit(solution)/shard_map/ppermute | solution.py:254
  19.9 1.3 %collective-permute-start.8 = (bf16[32,1536]{1,0:T(8,128)(2,1)S(1)}, bf16[32,1536]{1,0:T(8,128)(2,1)S(1)}, u32[]{:S(2)}, u32[]{:S(2)}) collective-permute-start(bf16[32,1536]{1,0:T(8,128)(2,1)S(1)} %collective-permute-done.6.refs_5_), channel_id=1, source_target_pairs={{0,8},{1,9},{2,10},{3,11},{4,12},{5,13},{6,14},{7,15},{8,0},{9,1},... | collective-permute-start | bytes 294920 | tf_op jit(solution)/shard_map/ppermute | solution.py:254

commit v8 on v7

--- a/solution.py
+++ b/solution.py
@@ -78,7 +78,7 @@
                     emit(chunk, first, [one[k] - three[k] for k in keys], [one[k] - two[k] for k in keys])
         return carry
 
-    lax.fori_loop(0, CHUNKS, one_chunk, 0)
+    lax.fori_loop(0, CHUNKS, one_chunk, 0, unroll=2)
 
 
 def half_scratch(half, block, span):
@@ -257,7 +257,7 @@
         return r, c, 1 - w
 
     flat = spectra.reshape(span * block, shard)
-    turned = send(flat, lambda r, c, w: (n_row - 1 - c, r, w))
+    turned = send(flat, lambda r, c, w: ((c + 1) % n_row, r, w))
     theirs, mine = split_stations(spectra, half)
     got = send(theirs, other_win)
     flags = masks(usable, half, block, span)
@@ -280,7 +280,7 @@
         last = lax.optimization_barrier((near[3], *shifted))[0]
         swapped = [send(x, lambda r, c, w: (r ^ 1, c, w)) for x in near[:3] + [last]]
         cols = [[*near[:2], *swapped[:2]], [*near[2:], *swapped[2:]]]
-        col_places = [lambda r, c, w, e=e: n_row - 1 - (r ^ e) for e in (0, 2, 1, 3)]
+        col_places = [lambda r, c, w, e=e: lax.rem((r ^ e) + n_row - 1, n_row) for e in (0, 2, 1, 3)]
     else:
         gathered = lax.all_gather(mine, "col", axis=0)
         rows = [gathered[i] for i in range(n_col)]
@@ -288,7 +288,7 @@
         near = lax.all_gather(turned, "row", axis=0)
         far = send(near, other_win)
         cols = [[x[i] for i in range(n_row)] for x in (near, far)]
-        col_places = [lambda r, c, w, i=i: n_row - 1 - i for i in range(n_row)]
+        col_places = [lambda r, c, w, i=i: (i + n_row - 1) % n_row for i in range(n_row)]
 
     parts = first_half(rows, cols[0], *flags[:2], row_places, col_places, half, block, span)
     out = correlate(

time: 24.6 us -> 24.3 us (0.988)
  waiting for transfers between devices: 6.81 us -> 4.98 us
  starting transfers between devices: 11.5 us -> 13.2 us
    ppermute x12, waiting for transfers between devices: 6.81 us -> 4.98 us  [send(): return lax.ppermute(data, AXES, pairs)]
    ppermute x12, starting transfers between devices: 11.5 us -> 13.2 us  [send(): return lax.ppermute(data, AXES, pairs)]
  transfers between devices with their start and end apart: 12 -> 12, of which waited for: 7 -> 5; matrix products, arithmetic and copies ran while one was open for 0% -> 0% of each run, Pallas kernels for 5% -> 5%
where the time goes in v8:
time: 24.3 us; the launch traced here: 24.1 us
  starting transfers between devices  13.2 us (54%)
  waiting for transfers between devices  4.98 us (20%)
  Pallas kernels  4.3 us (18%)
  local copies, waits for them, and re-layouts  1.59 us (7%)
    ppermute x12, starting transfers between devices, send(): return lax.ppermute(data, AXES, pairs)  13.2 us
    ppermute x12, waiting for transfers between devices, send(): return lax.ppermute(data, AXES, pairs)  4.98 us
    pallas_call x1, Pallas kernels, correlate(): pl.pallas_call(kernel, out_shape=jax.ShapeDtypeStruct((half, 9, block, LA...  3.08 us
    unnamed x6, local copies, waits for them, and re-layouts  1.58 us
    pallas_call x1, Pallas kernels, first_half(): pl.pallas_call(kernel, out_shape=(jax.ShapeDtypeStruct((CHUNKS, groups, L...  1.09 us
  transfers between devices with their start and end apart: 12, of which 5 were waited for; matrix products, arithmetic and copies ran while one was open for 0% of the time, Pallas kernels for 5%

profile of v8, /device:TPU:0, one launch (start us, length us, event | category | flops | bytes accessed | tf_op | source)
XLA Modules:
  0.0 24.1 jit_solution(232852307079568734)
XLA Ops:
  0.0 0.5 %collective-permute-start.2 = (bf16[32,1536]{1,0:T(8,128)(2,1)}, bf16[32,1536]{1,0:T(8,128)(2,1)S(1)}, u32[]{:S(2)}, u32[]{:S(2)}) collective-permute-start(bf16[32,1536]{1,0:T(8,128)(2,1)} %bitcast.2), channel_id=1, source_target_pairs={{0,8},{1,9},{2,16},{3,17},{4,24},{5,25},{6,0},{7,1},{8,10},{9,11},... | collective-permute-start | bytes 294920 | tf_op jit(solution)/shard_map/ppermute | solution.py:254
  0.5 0.0 copy-start.1
  0.5 0.9 %copy-done.1 = bf16[4,8,1536]{2,1,0:T(8,128)(2,1)S(1)} copy-done((bf16[4,8,1536]{2,1,0:T(8,128)(2,1)S(1)}, bf16[4,8,1536]{2,1,0:T(8,128)(2,1)}, u32[]{:S(2)}) %copy-start.1) | copy-done | bytes 98328
  1.4 2.6 %collective-permute-start = (bf16[16,1536]{1,0:T(8,128)(2,1)S(1)}, bf16[16,1536]{1,0:T(8,128)(2,1)S(1)}, u32[]{:S(2)}, u32[]{:S(2)}) collective-permute-start(bf16[16,1536]{1,0:T(8,128)(2,1)S(1)} %get-tuple-element.23), channel_id=1, source_target_pairs={{0,1},{1,0},{2,3},{3,2},{4,5},{5,4},{6,7},{7,6},{8,9},{9,8},{10,11... | collective-permute-start | bytes 147464 | tf_op jit(solution)/shard_map/ppermute | solution.py:254
  3.9 0.0 copy-start.2
  3.9 0.7 %copy-done.2 = s32[8,32]{1,0:T(8,128)S(1)} copy-done((s32[8,32]{1,0:T(8,128)S(1)}, s32[8,32]{1,0:T(8,128)}, u32[]{:S(2)}) %copy-start.2) | copy-done | bytes 1048
  4.6 0.1 shard_map.38
  4.7 1.3 %collective-permute-done = bf16[16,1536]{1,0:T(8,128)(2,1)S(1)} collective-permute-done((bf16[16,1536]{1,0:T(8,128)(2,1)S(1)}, bf16[16,1536]{1,0:T(8,128)(2,1)S(1)}, u32[]{:S(2)}, u32[]{:S(2)}) %collective-permute-start) | collective-permute-done | bytes 49184 | tf_op jit(solution)/shard_map/ppermute | solution.py:254
  6.0 0.0 copy-start
  6.0 4.2 %collective-permute-start.1 = (bf16[32,1536]{1,0:T(8,128)(2,1)S(1)}, bf16[32,1536]{1,0:T(8,128)(2,1)S(1)}, u32[]{:S(2)}, u32[]{:S(2)}) collective-permute-start(bf16[32,1536]{1,0:T(8,128)(2,1)S(1)} %constant_dynamic-update-slice_fusion.refs_0_), channel_id=1, source_target_pairs={{0,6},{1,7},{2,4},{3,5},{4,2},{5,3},{6,0},{7,1},{8,14},{9,15},{10,... | collective-permute-start | bytes 294920 | tf_op jit(solution)/shard_map/ppermute | solution.py:254
  10.2 0.0 collective-permute-done.2.refs_4_
  10.2 1.9 %collective-permute-start.9 = (bf16[32,1536]{1,0:T(8,128)(2,1)S(1)}, bf16[32,1536]{1,0:T(8,128)(2,1)S(1)}, u32[]{:S(2)}, u32[]{:S(2)}) collective-permute-start(bf16[32,1536]{1,0:T(8,128)(2,1)S(1)} %collective-permute-done.2.refs_4_), channel_id=1, source_target_pairs={{0,16},{1,17},{2,18},{3,19},{4,20},{5,21},{6,22},{7,23},{8,24},{9,... | collective-permute-start | bytes 294920 | tf_op jit(solution)/shard_map/ppermute | solution.py:254
  12.1 1.3 %collective-permute-start.6 = (bf16[32,1536]{1,0:T(8,128)(2,1)S(1)}, bf16[32,1536]{1,0:T(8,128)(2,1)S(1)}, u32[]{:S(2)}, u32[]{:S(2)}) collective-permute-start(bf16[32,1536]{1,0:T(8,128)(2,1)S(1)} %collective-permute-done.2.refs_4_), channel_id=1, source_target_pairs={{0,17},{1,16},{2,19},{3,18},{4,21},{5,20},{6,23},{7,22},{8,25},{9,... | collective-permute-start | bytes 294920 | tf_op jit(solution)/shard_map/ppermute | solution.py:254
  13.4 0.3 %collective-permute-start.5 = (bf16[32,1536]{1,0:T(8,128)(2,1)S(1)}, bf16[32,1536]{1,0:T(8,128)(2,1)S(1)}, u32[]{:S(2)}, u32[]{:S(2)}) collective-permute-start(bf16[32,1536]{1,0:T(8,128)(2,1)S(1)} %collective-permute-done.2.refs_4_), channel_id=1, source_target_pairs={{0,1},{1,0},{2,3},{3,2},{4,5},{5,4},{6,7},{7,6},{8,9},{9,8},{10,11... | collective-permute-start | bytes 294920 | tf_op jit(solution)/shard_map/ppermute | solution.py:254
  13.7 0.3 %collective-permute-start.3 = (bf16[32,1536]{1,0:T(8,128)(2,1)S(1)}, bf16[32,1536]{1,0:T(8,128)(2,1)S(1)}, u32[]{:S(2)}, u32[]{:S(2)}) collective-permute-start(bf16[32,1536]{1,0:T(8,128)(2,1)S(1)} %constant_dynamic-update-slice_fusion.refs_0_), channel_id=1, source_target_pairs={{0,2},{1,3},{2,0},{3,1},{4,6},{5,7},{6,4},{7,5},{8,10},{9,11},{10,... | collective-permute-start | bytes 294920 | tf_op jit(solution)/shard_map/ppermute | solution.py:254
  14.0 0.0 collective-permute-done.1.refs_1_
  14.0 1.8 %collective-permute-start.4 = (bf16[32,1536]{1,0:T(8,128)(2,1)S(1)}, bf16[32,1536]{1,0:T(8,128)(2,1)S(1)}, u32[]{:S(2)}, u32[]{:S(2)}) collective-permute-start(bf16[32,1536]{1,0:T(8,128)(2,1)S(1)} %collective-permute-done.1.refs_1_), channel_id=1, source_target_pairs={{0,2},{1,3},{2,0},{3,1},{4,6},{5,7},{6,4},{7,5},{8,10},{9,11},{10,... | collective-permute-start | bytes 294920 | tf_op jit(solution)/shard_map/ppermute | solution.py:254
  15.7 0.0 collective-permute-done.9.refs_5_
  15.7 0.0 collective-permute-start.10
  15.7 2.4 %collective-permute-done.6.refs_5_ = bf16[32,1536]{1,0:T(8,128)(2,1)S(1)} collective-permute-done((bf16[32,1536]{1,0:T(8,128)(2,1)S(1)}, bf16[32,1536]{1,0:T(8,128)(2,1)S(1)}, u32[]{:S(2)}, u32[]{:S(2)}) %collective-permute-start.6) | collective-permute-done | bytes 98336 | tf_op jit(solution)/shard_map/ppermute | solution.py:254
  18.1 0.0 collective-permute-start.11
  18.1 0.0 collective-permute-done.5.refs_4_
  18.1 0.5 %collective-permute-start.7 = (bf16[32,1536]{1,0:T(8,128)(2,1)S(1)}, bf16[32,1536]{1,0:T(8,128)(2,1)S(1)}, u32[]{:S(2)}, u32[]{:S(2)}) collective-permute-start(bf16[32,1536]{1,0:T(8,128)(2,1)S(1)} %collective-permute-done.5.refs_4_), channel_id=1, source_target_pairs={{0,8},{1,9},{2,10},{3,11},{4,12},{5,13},{6,14},{7,15},{8,0},{9,1},... | collective-permute-start | bytes 294920 | tf_op jit(solution)/shard_map/ppermute | solution.py:254
  18.6 0.1 collective-permute-done.3.refs_2_
  18.7 1.1 %collective-permute-done.4.refs_3_ = bf16[32,1536]{1,0:T(8,128)(2,1)S(1)} collective-permute-done((bf16[32,1536]{1,0:T(8,128)(2,1)S(1)}, bf16[32,1536]{1,0:T(8,128)(2,1)S(1)}, u32[]{:S(2)}, u32[]{:S(2)}) %collective-permute-start.4) | collective-permute-done | bytes 98336 | tf_op jit(solution)/shard_map/ppermute | solution.py:254
  19.8 0.0 collective-permute-start.8
  19.8 0.0 collective-permute-done.10.refs_6_
  19.8 0.0 collective-permute-done.11.refs_7_
  19.8 1.1 %shard_map.39 = (f32[8,288,128]{2,1,0:T(8,128)S(1)}, f32[8,288,128]{2,1,0:T(8,128)S(1)}) custom-call(bf16[32,1536]{1,0:T(8,128)(2,1)S(1)} %constant_dynamic-update-slice_fusion.refs_0_, bf16[32,1536]{1,0:T(8,128)(2,1)S(1)} %collective-permute-done.1.refs_1_, bf16[32,1536]{1,0:T(8,128)(2,1)S(1)} %collective-permute-done.3.refs_2_, ...), custom_call_target="tpu_custom_call" | custom-call | flops 1000000000 | bytes 1048576 | tf_op jit(solution)/shard_map/pallas_call | solution.py:113
  20.9 0.0 collective-permute-done.7.refs_6_
  20.9 0.2 collective-permute-done.8.refs_7_
  21.1 0.0 copy-done
  21.1 3.1 %shard_map.40 = f32[4,9,8,768]{3,2,1,0:T(8,128)} custom-call(bf16[32,1536]{1,0:T(8,128)(2,1)S(1)} %constant_dynamic-update-slice_fusion.refs_0_, bf16[32,1536]{1,0:T(8,128)(2,1)S(1)} %collective-permute-done.1.refs_1_, bf16[32,1536]{1,0:T(8,128)(2,1)S(1)} %collective-permute-done.3.refs_2_, bf16[32,1536]{1,0:T(8,128)(2,1)S(1)} %collective-permute-done.4.refs_3_, ...), custom_call_target="tpu_custom_call" | custom-call | tf_op jit(solution)/shard_map/pallas_call | solution.py:163
  (2 shorter events, 0.0 us)
Async XLA Ops:
  0.0 10.2 %collective-permute-start.2 = (bf16[32,1536]{1,0:T(8,128)(2,1)}, bf16[32,1536]{1,0:T(8,128)(2,1)S(1)}, u32[]{:S(2)}, u32[]{:S(2)}) collective-permute-start(bf16[32,1536]{1,0:T(8,128)(2,1)} %bitcast.2), channel_id=1, source_target_pairs={{0,8},{1,9},{2,16},{3,17},{4,24},{5,25},{6,0},{7,1},{8,10},{9,11},... | collective-permute-start | bytes 294920 | tf_op jit(solution)/shard_map/ppermute | solution.py:254
  0.5 0.9 %copy-start.1 = (bf16[4,8,1536]{2,1,0:T(8,128)(2,1)S(1)}, bf16[4,8,1536]{2,1,0:T(8,128)(2,1)}, u32[]{:S(2)}) copy-start(bf16[4,8,1536]{2,1,0:T(8,128)(2,1)} %param.3) | copy-start | bytes 294916
  1.4 4.6 %collective-permute-start = (bf16[16,1536]{1,0:T(8,128)(2,1)S(1)}, bf16[16,1536]{1,0:T(8,128)(2,1)S(1)}, u32[]{:S(2)}, u32[]{:S(2)}) collective-permute-start(bf16[16,1536]{1,0:T(8,128)(2,1)S(1)} %get-tuple-element.23), channel_id=1, source_target_pairs={{0,1},{1,0},{2,3},{3,2},{4,5},{5,4},{6,7},{7,6},{8,9},{9,8},{10,11... | collective-permute-start | bytes 147464 | tf_op jit(solution)/shard_map/ppermute | solution.py:254
  3.9 0.7 %copy-start.2 = (s32[8,32]{1,0:T(8,128)S(1)}, s32[8,32]{1,0:T(8,128)}, u32[]{:S(2)}) copy-start(s32[8,32]{1,0:T(8,128)} %usable_ref.1) | copy-start | bytes 3076
  6.0 15.0 %copy-start = (bf16[2048,768]{1,0:T(8,128)(2,1)S(1)}, bf16[2048,768]{1,0:T(8,128)(2,1)}, u32[]{:S(2)}) copy-start(bf16[2048,768]{1,0:T(8,128)(2,1)} %constant.6.clone.refs_13_) | copy-start | bytes 9437188
  6.0 7.9 %collective-permute-start.1 = (bf16[32,1536]{1,0:T(8,128)(2,1)S(1)}, bf16[32,1536]{1,0:T(8,128)(2,1)S(1)}, u32[]{:S(2)}, u32[]{:S(2)}) collective-permute-start(bf16[32,1536]{1,0:T(8,128)(2,1)S(1)} %constant_dynamic-update-slice_fusion.refs_0_), channel_id=1, source_target_pairs={{0,6},{1,7},{2,4},{3,5},{4,2},{5,3},{6,0},{7,1},{8,14},{9,15},{10,... | collective-permute-start | bytes 294920 | tf_op jit(solution)/shard_map/ppermute | solution.py:254
  10.2 5.5 %collective-permute-start.9 = (bf16[32,1536]{1,0:T(8,128)(2,1)S(1)}, bf16[32,1536]{1,0:T(8,128)(2,1)S(1)}, u32[]{:S(2)}, u32[]{:S(2)}) collective-permute-start(bf16[32,1536]{1,0:T(8,128)(2,1)S(1)} %collective-permute-done.2.refs_4_), channel_id=1, source_target_pairs={{0,16},{1,17},{2,18},{3,19},{4,20},{5,21},{6,22},{7,23},{8,24},{9,... | collective-permute-start | bytes 294920 | tf_op jit(solution)/shard_map/ppermute | solution.py:254
  12.1 6.0 %collective-permute-start.6 = (bf16[32,1536]{1,0:T(8,128)(2,1)S(1)}, bf16[32,1536]{1,0:T(8,128)(2,1)S(1)}, u32[]{:S(2)}, u32[]{:S(2)}) collective-permute-start(bf16[32,1536]{1,0:T(8,128)(2,1)S(1)} %collective-permute-done.2.refs_4_), channel_id=1, source_target_pairs={{0,17},{1,16},{2,19},{3,18},{4,21},{5,20},{6,23},{7,22},{8,25},{9,... | collective-permute-start | bytes 294920 | tf_op jit(solution)/shard_map/ppermute | solution.py:254
  13.4 4.7 %collective-permute-start.5 = (bf16[32,1536]{1,0:T(8,128)(2,1)S(1)}, bf16[32,1536]{1,0:T(8,128)(2,1)S(1)}, u32[]{:S(2)}, u32[]{:S(2)}) collective-permute-start(bf16[32,1536]{1,0:T(8,128)(2,1)S(1)} %collective-permute-done.2.refs_4_), channel_id=1, source_target_pairs={{0,1},{1,0},{2,3},{3,2},{4,5},{5,4},{6,7},{7,6},{8,9},{9,8},{10,11... | collective-permute-start | bytes 294920 | tf_op jit(solution)/shard_map/ppermute | solution.py:254
  13.7 5.0 %collective-permute-start.3 = (bf16[32,1536]{1,0:T(8,128)(2,1)S(1)}, bf16[32,1536]{1,0:T(8,128)(2,1)S(1)}, u32[]{:S(2)}, u32[]{:S(2)}) collective-permute-start(bf16[32,1536]{1,0:T(8,128)(2,1)S(1)} %constant_dynamic-update-slice_fusion.refs_0_), channel_id=1, source_target_pairs={{0,2},{1,3},{2,0},{3,1},{4,6},{5,7},{6,4},{7,5},{8,10},{9,11},{10,... | collective-permute-start | bytes 294920 | tf_op jit(solution)/shard_map/ppermute | solution.py:254
  14.0 5.8 %collective-permute-start.4 = (bf16[32,1536]{1,0:T(8,128)(2,1)S(1)}, bf16[32,1536]{1,0:T(8,128)(2,1)S(1)}, u32[]{:S(2)}, u32[]{:S(2)}) collective-permute-start(bf16[32,1536]{1,0:T(8,128)(2,1)S(1)} %collective-permute-done.1.refs_1_), channel_id=1, source_target_pairs={{0,2},{1,3},{2,0},{3,1},{4,6},{5,7},{6,4},{7,5},{8,10},{9,11},{10,... | collective-permute-start | bytes 294920 | tf_op jit(solution)/shard_map/ppermute | solution.py:254
  15.7 4.0 %collective-permute-start.10 = (bf16[32,1536]{1,0:T(8,128)(2,1)S(1)}, bf16[32,1536]{1,0:T(8,128)(2,1)S(1)}, u32[]{:S(2)}, u32[]{:S(2)}) collective-permute-start(bf16[32,1536]{1,0:T(8,128)(2,1)S(1)} %collective-permute-done.2.refs_4_), channel_id=1, source_target_pairs={{0,8},{1,9},{2,10},{3,11},{4,12},{5,13},{6,14},{7,15},{8,0},{9,1},... | collective-permute-start | bytes 294920 | tf_op jit(solution)/shard_map/ppermute | solution.py:254
  18.1 1.7 %collective-permute-start.11 = (bf16[32,1536]{1,0:T(8,128)(2,1)S(1)}, bf16[32,1536]{1,0:T(8,128)(2,1)S(1)}, u32[]{:S(2)}, u32[]{:S(2)}) collective-permute-start(bf16[32,1536]{1,0:T(8,128)(2,1)S(1)} %collective-permute-done.9.refs_5_), channel_id=1, source_target_pairs={{0,8},{1,9},{2,10},{3,11},{4,12},{5,13},{6,14},{7,15},{8,0},{9,1},... | collective-permute-start | bytes 294920 | tf_op jit(solution)/shard_map/ppermute | solution.py:254
  18.1 2.8 %collective-permute-start.7 = (bf16[32,1536]{1,0:T(8,128)(2,1)S(1)}, bf16[32,1536]{1,0:T(8,128)(2,1)S(1)}, u32[]{:S(2)}, u32[]{:S(2)}) collective-permute-start(bf16[32,1536]{1,0:T(8,128)(2,1)S(1)} %collective-permute-done.5.refs_4_), channel_id=1, source_target_pairs={{0,8},{1,9},{2,10},{3,11},{4,12},{5,13},{6,14},{7,15},{8,0},{9,1},... | collective-permute-start | bytes 294920 | tf_op jit(solution)/shard_map/ppermute | solution.py:254
  19.8 1.3 %collective-permute-start.8 = (bf16[32,1536]{1,0:T(8,128)(2,1)S(1)}, bf16[32,1536]{1,0:T(8,128)(2,1)S(1)}, u32[]{:S(2)}, u32[]{:S(2)}) collective-permute-start(bf16[32,1536]{1,0:T(8,128)(2,1)S(1)} %collective-permute-done.6.refs_5_), channel_id=1, source_target_pairs={{0,8},{1,9},{2,10},{3,11},{4,12},{5,13},{6,14},{7,15},{8,0},{9,1},... | collective-permute-start | bytes 294920 | tf_op jit(solution)/shard_map/ppermute | solution.py:254
